TPU v7x, 32 devices: a whole 2x2x4 slice. The times are simulated.
32 devices in a mesh: docs: 16 (over z, x, core), half: 2 (over y).
Axes of the slice: x: 2, y: 2, z: 4, core: 2. Of those that a mesh axis runs over, the one named last changes fastest.
Arguments:
- hidden_in: bfloat16 [32, 1024, 768], P('docs', 'half'), may hold values from -6 to 6
- boxes: int32 [4, 32, 1024], P(None, 'docs'), may hold values from 0 to 999
- lengths: int32 [32], P('docs'), may hold values from 640 to 1024, as said below
- cotangent: bfloat16 [32, 1024, 768], P('docs', 'half'), may hold values from -6 to 6
- layout_weight: bfloat16 [128, 768], replicated, may hold values from -0.5 to 0.5
- qkv_weight: bfloat16 [768, 2304], replicated, may hold values from -0.21875 to 0.21875
- qv_bias: bfloat16 [2, 768], replicated, may hold values from -3 to 3
- bias_tables: bfloat16 [3, 32, 12], replicated, may hold values from -4 to 4
- out_weight: bfloat16 [768, 768], replicated, may hold values from -0.625 to 0.625
- out_bias: bfloat16 [768], replicated, may hold values from -3 to 3
- norm1_gain: bfloat16 [768], replicated, may hold values from 0.5 to 1.5
- norm1_bias: bfloat16 [768], replicated, may hold values from -3 to 3
- ff_in: bfloat16 [768, 3072], replicated, may hold values from -0.21875 to 0.21875
- ff_in_bias: bfloat16 [3072], replicated, may hold values from -3 to 3
- ff_out: bfloat16 [3072, 768], replicated, may hold values from -0.109375 to 0.109375
- ff_out_bias: bfloat16 [768], replicated, may hold values from -3 to 3
- norm2_gain: bfloat16 [768], replicated, may hold values from 0.5 to 1.5
- norm2_bias: bfloat16 [768], replicated, may hold values from -3 to 3
Outputs:
- layer_out: bfloat16 [32, 1024, 768], P('docs', 'half')
- input_grad: bfloat16 [32, 1024, 768], P('docs', 'half')
- layout_weight_grad: float32 [128, 768], replicated
- qkv_weight_grad: float32 [768, 2304], replicated
- qv_bias_grad: float32 [2, 768], replicated
- bias_tables_grad: float32 [3, 32, 12], replicated
- out_weight_grad: float32 [768, 768], replicated
- out_bias_grad: float32 [768], replicated
- norm1_gain_grad: float32 [768], replicated
- norm1_bias_grad: float32 [768], replicated
- ff_in_grad: float32 [768, 3072], replicated
- ff_in_bias_grad: float32 [3072], replicated
- ff_out_grad: float32 [3072, 768], replicated
- ff_out_bias_grad: float32 [768], replicated
- norm2_gain_grad: float32 [768], replicated
- norm2_bias_grad: float32 [768], replicated
Inputs may be any that keep to these rules, and one draw needn't show every extreme that they name: `lengths`: one sequence, which one drawn from the seed, has length 1024.
All inputs are finite; a program needn't handle non-finite values.
Results may differ from a plain program's by a relative error of at most 0.015.
Values may be sent and summed in bfloat16 or wider, within the bound.
No kernel may reach another device: no remote copies, remote signals or barrier semaphores. Data moves between devices by JAX's collectives and lax.ppermute only.
A program may use at most 384 MiB of HBM per device.

v0:
```python
import math

import jax
import jax.numpy as jnp
from jax import lax
from jax.sharding import PartitionSpec as P

BOXQ = 1000


NEAR_EDGES = (1, 2, 3, 4, 5, 6, 7, 8, 12, 16, 24, 32, 64, 128, 256)
FAR_EDGES = (1, 2, 4, 8, 16, 32, 64, 96, 128, 192, 256, 384, 512, 768, 1024)


def fourier(coords):
    scaled = coords.astype(jnp.float32) / BOXQ
    freqs = (jnp.arange(16, dtype=jnp.float32) + 1.0) * math.pi
    angle = scaled[:, :, None] * freqs[None, None, :]
    waves = jnp.concatenate([jnp.sin(angle), jnp.cos(angle)], axis=2)
    return jnp.transpose(waves, (1, 0, 2)).reshape(coords.shape[1], 128)


def level(rel, edges):
    magnitude = jnp.abs(rel)
    result = jnp.zeros(rel.shape, jnp.int32)
    for edge in edges:
        result = result + (magnitude >= edge).astype(jnp.int32)
    return result + 16 * (rel > 0).astype(jnp.int32)


def layer_norm(resid, gain, shift):
    centre = resid - jnp.mean(resid, axis=-1, keepdims=True)
    spread = jnp.mean(centre * centre, axis=-1, keepdims=True)
    return centre * lax.rsqrt(spread + 1e-06) * gain + shift


def gelu_exact(value):
    return jax.nn.gelu(value, approximate=False)


def inner(left, right):
    return lax.dot_general(
        left, right, (((0,), (0,)), ((), ())), preferred_element_type=jnp.float32
    )


def back_dot(left, right):
    return lax.dot_general(
        left, right, (((1,), (1,)), ((), ())), preferred_element_type=jnp.float32
    )


def bucket_hots(box_seq, first, half_len, full_len, buckets):
    key_pos = jnp.arange(full_len, dtype=jnp.int32)
    query_pos = first + jnp.arange(half_len, dtype=jnp.int32)
    across = box_seq[0] + box_seq[2]
    down = box_seq[1] + box_seq[3]
    own_across = lax.dynamic_slice_in_dim(across, first, half_len, 0)
    own_down = lax.dynamic_slice_in_dim(down, first, half_len, 0)
    near_hot = jax.nn.one_hot(
        level(key_pos[None, :] - query_pos[:, None], NEAR_EDGES), buckets, dtype=jnp.bfloat16
    )
    across_hot = jax.nn.one_hot(
        level(across[None, :] - own_across[:, None], FAR_EDGES), buckets, dtype=jnp.bfloat16
    )
    down_hot = jax.nn.one_hot(
        level(down[None, :] - own_down[:, None], FAR_EDGES), buckets, dtype=jnp.bfloat16
    )
    return (near_hot, across_hot, down_hot)


def raw_scores(query_seq, key_seq, hots, tables, length_seq, heads):
    q_heads = query_seq.reshape(query_seq.shape[0], heads, -1)
    k_heads = key_seq.reshape(key_seq.shape[0], heads, -1)
    scores = (
        jnp.einsum("qhd,khd->hqk", q_heads, k_heads, preferred_element_type=jnp.float32) * 0.125
    )
    for kind in range(3):
        scores = scores + jnp.einsum(
            "qkb,bh->hqk", hots[kind], tables[kind], preferred_element_type=jnp.float32
        )
    valid = jnp.arange(key_seq.shape[0], dtype=jnp.int32) < length_seq
    return jnp.where(valid[None, None, :], scores, -1e30)


def shards(
    hidden_in,
    boxes,
    lengths,
    cotangent,
    layout_weight,
    qkv_weight,
    qv_bias,
    bias_tables,
    out_weight,
    out_bias,
    norm1_gain,
    norm1_bias,
    ff_in,
    ff_in_bias,
    ff_out,
    ff_out_bias,
    norm2_gain,
    norm2_bias,
):
    seqs, half_len, width = hidden_in.shape
    full_len = half_len * lax.axis_size("half")
    heads = bias_tables.shape[2]
    buckets = bias_tables.shape[1]
    rows = seqs * half_len
    first = lax.axis_index("half") * half_len
    own_boxes = lax.dynamic_slice_in_dim(boxes, first, half_len, 2)
    feats = fourier(own_boxes.reshape(4, rows)).astype(jnp.bfloat16)
    start = hidden_in.reshape(rows, width).astype(jnp.float32) + jnp.dot(
        feats, layout_weight, preferred_element_type=jnp.float32
    )
    start_low = start.astype(jnp.bfloat16)
    qkv = jnp.dot(start_low, qkv_weight, preferred_element_type=jnp.float32)
    bias_pair = qv_bias.astype(jnp.float32)
    query = (qkv[:, :width] + bias_pair[0]).astype(jnp.bfloat16).reshape(seqs, half_len, width)
    keys = qkv[:, width : 2 * width].astype(jnp.bfloat16).reshape(seqs, half_len, width)
    values = (
        (qkv[:, 2 * width :] + bias_pair[1]).astype(jnp.bfloat16).reshape(seqs, half_len, width)
    )
    keys_all, values_all = (
        lax.all_gather(keys, "half", axis=1, tiled=True),
        lax.all_gather(values, "half", axis=1, tiled=True),
    )
    box_seqs = jnp.transpose(boxes, (1, 0, 2))

    def attend(item):
        query_seq, key_seq, value_seq, box_seq, length_seq = item
        hots = bucket_hots(box_seq, first, half_len, full_len, buckets)
        scores = raw_scores(query_seq, key_seq, hots, bias_tables, length_seq, heads)
        top = jnp.max(scores, axis=-1, keepdims=True)
        expo = jnp.exp(scores - top)
        total = jnp.sum(expo, axis=-1, keepdims=True)
        probs = (expo / total).astype(jnp.bfloat16)
        v_heads = value_seq.reshape(full_len, heads, -1)
        context = jnp.einsum("hqk,khd->qhd", probs, v_heads, preferred_element_type=jnp.float32)
        return (context.reshape(half_len, width), top + jnp.log(total))

    context, log_total = lax.map(attend, (query, keys_all, values_all, box_seqs, lengths))
    context_low = context.reshape(rows, width).astype(jnp.bfloat16)
    attended = jnp.dot(
        context_low, out_weight, preferred_element_type=jnp.float32
    ) + out_bias.astype(jnp.float32)
    mid, norm1_pull = jax.vjp(
        layer_norm, start + attended, norm1_gain.astype(jnp.float32), norm1_bias.astype(jnp.float32)
    )
    mid_low = mid.astype(jnp.bfloat16)
    hidden_pre = jnp.dot(mid_low, ff_in, preferred_element_type=jnp.float32) + ff_in_bias.astype(
        jnp.float32
    )
    activated, gelu_pull = jax.vjp(gelu_exact, hidden_pre)
    activated = activated.astype(jnp.bfloat16)
    branch = jnp.dot(activated, ff_out, preferred_element_type=jnp.float32) + ff_out_bias.astype(
        jnp.float32
    )
    result, norm2_pull = jax.vjp(
        layer_norm, mid + branch, norm2_gain.astype(jnp.float32), norm2_bias.astype(jnp.float32)
    )
    layer_out = result.astype(jnp.bfloat16).reshape(seqs, half_len, width)
    upstream_grad = cotangent.reshape(rows, width).astype(jnp.float32)
    grad_r2, gain2_grad, shift2_grad = norm2_pull(upstream_grad)
    grad_ff = grad_r2.astype(jnp.bfloat16)
    ffout_grad = inner(activated, grad_ff)
    ffoutb_grad = jnp.sum(grad_ff.astype(jnp.float32), axis=0)
    grad_inner = gelu_pull(back_dot(grad_ff, ff_out))[0].astype(jnp.bfloat16)
    ffin_grad = inner(mid_low, grad_inner)
    ffinb_grad = jnp.sum(grad_inner.astype(jnp.float32), axis=0)
    grad_mid = grad_r2 + back_dot(grad_inner, ff_in)
    grad_r1, gain1_grad, shift1_grad = norm1_pull(grad_mid)
    grad_att = grad_r1.astype(jnp.bfloat16)
    outw_grad = inner(context_low, grad_att)
    outb_grad = jnp.sum(grad_att.astype(jnp.float32), axis=0)
    grad_context = (
        back_dot(grad_att, out_weight).astype(jnp.bfloat16).reshape(seqs, half_len, width)
    )

    def attend_back(item):
        query_seq, key_seq, value_seq, grad_seq, box_seq, length_seq, lse_seq = item
        hots = bucket_hots(box_seq, first, half_len, full_len, buckets)
        scores = raw_scores(query_seq, key_seq, hots, bias_tables, length_seq, heads)
        probs = jnp.exp(scores - lse_seq)
        q_heads = query_seq.reshape(half_len, heads, -1)
        k_heads = key_seq.reshape(full_len, heads, -1)
        v_heads = value_seq.reshape(full_len, heads, -1)
        g_heads = grad_seq.reshape(half_len, heads, -1)
        grad_probs = jnp.einsum(
            "qhd,khd->hqk", g_heads, v_heads, preferred_element_type=jnp.float32
        )
        weighted = jnp.sum(probs * grad_probs, axis=-1, keepdims=True)
        grad_scores = (probs * (grad_probs - weighted)).astype(jnp.bfloat16)
        grad_query = (
            jnp.einsum("hqk,khd->qhd", grad_scores, k_heads, preferred_element_type=jnp.float32)
            * 0.125
        )
        grad_key = (
            jnp.einsum("hqk,qhd->khd", grad_scores, q_heads, preferred_element_type=jnp.float32)
            * 0.125
        )
        grad_value = jnp.einsum(
            "hqk,qhd->khd", probs.astype(jnp.bfloat16), g_heads, preferred_element_type=jnp.float32
        )
        table_part = jnp.stack(
            [
                jnp.einsum(
                    "qkb,hqk->bh", hots[kind], grad_scores, preferred_element_type=jnp.float32
                )
                for kind in range(3)
            ]
        )
        return (
            grad_query.reshape(half_len, width),
            grad_key.reshape(full_len, width),
            grad_value.reshape(full_len, width),
            table_part,
        )

    grad_query, grad_key_all, grad_value_all, table_parts = lax.map(
        attend_back, (query, keys_all, values_all, grad_context, box_seqs, lengths, log_total)
    )
    table_grad = jnp.sum(table_parts, axis=0)
    grad_key, grad_value = (
        lax.psum_scatter(
            grad_key_all.astype(jnp.bfloat16), "half", scatter_dimension=1, tiled=True
        ).astype(jnp.float32),
        lax.psum_scatter(
            grad_value_all.astype(jnp.bfloat16), "half", scatter_dimension=1, tiled=True
        ).astype(jnp.float32),
    )
    query_low = grad_query.reshape(rows, width).astype(jnp.bfloat16)
    key_low = grad_key.reshape(rows, width).astype(jnp.bfloat16)
    value_low = grad_value.reshape(rows, width).astype(jnp.bfloat16)
    grad_qkv = jnp.concatenate([query_low, key_low, value_low], axis=1)
    qkv_grad = inner(start_low, grad_qkv)
    qvb_grad = jnp.stack(
        [
            jnp.sum(query_low.astype(jnp.float32), axis=0),
            jnp.sum(value_low.astype(jnp.float32), axis=0),
        ]
    )
    grad_start = (grad_r1 + back_dot(grad_qkv, qkv_weight)).astype(jnp.bfloat16)
    input_grad = grad_start.reshape(seqs, half_len, width)
    lay_grad = inner(feats, grad_start)
    totals = lax.psum(
        (
            lay_grad,
            qkv_grad,
            qvb_grad,
            table_grad,
            outw_grad,
            outb_grad,
            gain1_grad,
            shift1_grad,
            ffin_grad,
            ffinb_grad,
            ffout_grad,
            ffoutb_grad,
            gain2_grad,
            shift2_grad,
        ),
        ("docs", "half"),
    )
    (
        lay_total,
        qkv_total,
        qvb_total,
        table_total,
        outw_total,
        outb_total,
        gain1_total,
        shift1_total,
        ffin_total,
        ffinb_total,
        ffout_total,
        ffoutb_total,
        gain2_total,
        shift2_total,
    ) = totals
    return (
        layer_out,
        input_grad,
        lay_total,
        qkv_total,
        qvb_total,
        table_total,
        outw_total,
        outb_total,
        gain1_total,
        shift1_total,
        ffin_total,
        ffinb_total,
        ffout_total,
        ffoutb_total,
        gain2_total,
        shift2_total,
    )


def solution(mesh):
    placed = (
        P("docs", "half", None),
        P(None, "docs", None),
        P("docs"),
        P("docs", "half", None),
        P(),
        P(),
        P(),
        P(),
        P(),
        P(),
        P(),
        P(),
        P(),
        P(),
        P(),
        P(),
        P(),
        P(),
    )
    return jax.shard_map(
        shards,
        mesh=mesh,
        in_specs=placed,
        out_specs=(
            P("docs", "half", None),
            P("docs", "half", None),
            P(),
            P(),
            P(),
            P(),
            P(),
            P(),
            P(),
            P(),
            P(),
            P(),
            P(),
            P(),
            P(),
            P(),
        ),
        check_vma=False,
    )
```

profile of v0, /device:TPU:0, one launch (start us, length us, event | category | flops | bytes accessed | tf_op | source)
XLA Modules:
  0.0 1849.5 jit_solution(1952540397926910032)
XLA Ops:
  44.8 27.7 %all-gather.5.cloned.1.call-done = bf16[2,1024,768]{1,2,0:T(8,128)(2,1)} async-done(((bf16[2,512,768]{1,2,0:T(8,128)(2,1)}), bf16[2,1024,768]{1,2,0:T(8,128)(2,1)}) %all-gather.5.cloned.1.call-update) | async-done | bytes 3145744 | tf_op jit(solution)/shard_map/all_gather | solution.py:126
  72.5 47.1 %all-gather.3.cloned.1.call-done = bf16[2,1024,768]{1,2,0:T(8,128)(2,1)} async-done(((bf16[2,512,768]{1,2,0:T(8,128)(2,1)}), bf16[2,1024,768]{1,2,0:T(8,128)(2,1)}) %all-gather.3.cloned.1.call-update) | async-done | bytes 3145744 | tf_op jit(solution)/shard_map/all_gather | solution.py:127
  120.8 361.9 %while.32 = (s32[]{:T(128)}, bf16[2,512,768]{2,1,0:T(8,128)(2,1)}, f32[2,12,512,1]{2,1,3,0:T(8,128)}, bf16[2,1024,768]{1,2,0:T(8,128)(2,1)}, s32[2]{0:T(128)}, /...) while((s32[]{:T(128)}, bf16[2,512,768]{2,1,0:T(8,128)(2,1)}, ...), condition=%wide.region_3.4_spmd, body=%wide.region_0.3_spmd.sunk | while | flops 3015177728 | bytes 280648032 | solution.py:143
  207.2 74.9 %fusion.258 = (f32[12,512]{1,0:T(8,128)S(1)}, f32[12,512,1024]{2,1,0:T(8,128)}) fusion(f32[512,1024,12]{1,2,0:T(8,128)} %fusion.255, f32[512,1024,12]{1,2,0:T(8,128)} %fusion.256, f32[512,1024,12]{1,2,0:T(8,128)} %fusion.257, bf16[512,12,64]{0,2,1:T(8,128)(2,1)S(1)} %bitcast.279, bf16[1024,12,64]{0,2,1:T(8,128)(2,1)S(1)} %bitcast.278, ...), kind=kOutput, calls=%fused_computation.278.clone.1 | convolution fusion | flops 843048960 | bytes 103048192 | tf_op jit(solution)/shard_map/while/body/eval_jaxpr/qhd,khd->hqk/dot_general | solution.py:76
  372.4 74.9 %fusion.258 = (f32[12,512]{1,0:T(8,128)S(1)}, f32[12,512,1024]{2,1,0:T(8,128)}) fusion(f32[512,1024,12]{1,2,0:T(8,128)} %fusion.255, f32[512,1024,12]{1,2,0:T(8,128)} %fusion.256, f32[512,1024,12]{1,2,0:T(8,128)} %fusion.257, bf16[512,12,64]{0,2,1:T(8,128)(2,1)S(1)} %bitcast.279, bf16[1024,12,64]{0,2,1:T(8,128)(2,1)S(1)} %bitcast.278, ...), kind=kOutput, calls=%fused_computation.278.clone.1 | convolution fusion | flops 843048960 | bytes 103048192 | tf_op jit(solution)/shard_map/while/body/eval_jaxpr/qhd,khd->hqk/dot_general | solution.py:76
  488.5 35.1 %multiply_convert_fusion.1 = (bf16[1024,3072]{1,0:T(8,128)(2,1)S(1)}, f32[1024,3072]{1,0:T(8,128)}, f32[1024,3072]{1,0:T(8,128)}) fusion(f32[3072]{0:T(1024)S(1)} %copy-done.47, bf16[768,3072]{1,0:T(8,128)(2,1)S(1)} %bitcast.313, f32[1024,768]{1,0:T(8,128)S(1)} %get-tuple-element.471, f32[768]{0:T(1024)S(1)} %copy-done.37, f32[768]{0:T(1024)S(1)} %copy-done.35, ...), kind=kOutput, calls=%fused_computation.200 | convolution fusion | flops 5043388416 | bytes 39348224 | tf_op jit(solution)/shard_map/dot_general | solution.py:152
  538.9 18.7 %convert_reduce_fusion = (f32[3072]{0:T(1024)}, bf16[1024,3072]{1,0:T(8,128)(2,1)}) fusion(f32[1024,3072]{1,0:T(8,128)} %get-tuple-element.448, bf16[1024,768]{1,0:T(8,128)(2,1)} %get-tuple-element.440, bf16[3072,768]{1,0:T(8,128)(2,1)} %param.36, f32[1024,3072]{1,0:T(8,128)} %get-tuple-element.472, f32[3072]{0:T(1024)S(1)} %copy-done.47), kind=kOutput, calls=%fused_computation.198 | convolution fusion | flops 4885312512 | bytes 37773312 | tf_op jit(solution)/shard_map/dot_general | solution.py:48
  575.7 699.9 %while.33 = (s32[]{:T(128)}, bf16[2,512,768]{2,1,0:T(8,128)(2,1)}, bf16[2,1024,768]{2,1,0:T(8,128)(2,1)}, bf16[2,1024,768]{2,1,0:T(8,128)(2,1)}, f32[2,3,32,12]{...) while((s32[]{:T(128)}, bf16[2,512,768]{2,1,0:T(8,128)(2,1)}, ...), condition=%wide.region_14.15_spmd, body=%wide.region_12.14_spmd.sunk | while | flops 6698041344 | bytes 661715904 | solution.py:221
  630.3 30.4 %copy.129 = f32[512,1024,12]{1,0,2:T(8,128)} copy(f32[512,1024,12]{0,2,1:T(8,128)} %fusion.280) | data formatting | bytes 50331648 | tf_op jit(solution)/shard_map/while/body/eval_jaxpr/qkb,bh->hqk/dot_general | solution.py:79
  676.2 30.4 %copy.127 = f32[512,1024,12]{1,0,2:T(8,128)} copy(f32[512,1024,12]{0,2,1:T(8,128)} %fusion.278) | data formatting | bytes 50331648 | tf_op jit(solution)/shard_map/while/body/eval_jaxpr/qkb,bh->hqk/dot_general | solution.py:79
  722.1 30.4 %copy.128 = f32[512,1024,12]{1,0,2:T(8,128)} copy(f32[512,1024,12]{0,2,1:T(8,128)} %fusion.279) | data formatting | bytes 50331648 | tf_op jit(solution)/shard_map/while/body/eval_jaxpr/qkb,bh->hqk/dot_general | solution.py:79
  752.5 42.1 %multiply_reduce_fusion.6 = (f32[12,512]{1,0:T(8,128)S(1)}, f32[12,512,1024]{2,1,0:T(8,128)}) fusion(f32[12,512,1024]{2,1,0:T(8,128)} %fusion.277, f32[12,512]{1,0:T(8,128)} %dynamic-slice_bitcast_fusion.2, f32[512,1024,12]{1,0,2:T(8,128)} %copy.127, f32[512,1024,12]{1,0,2:T(8,128)} %copy.128, f32[512,1024,12]{1,0,2:T(8,128)} %copy.129, ...), kind=kOutput, calls=%fused_computation.111.clone.1 | convolution fusion | flops 855631872 | bytes 128238592 | tf_op jit(solution)/shard_map/while/body/eval_jaxpr/qhd,khd->hqk/dot_general | solution.py:76
  794.5 21.4 %multiply_convert_fusion.3 = bf16[12,512,1024]{2,1,0:T(8,128)(2,1)} fusion(f32[12,512,1024]{2,1,0:T(8,128)} %get-tuple-element.660, f32[12,512,1024]{2,1,0:T(8,128)} %fusion.277, f32[12,512]{1,0:T(8,128)S(1)} %get-tuple-element.661), kind=kLoop, calls=%fused_computation.110.clone.1 | loop fusion | flops 18874368 | bytes 62939136 | tf_op jit(solution)/shard_map/while/body/eval_jaxpr/convert_element_type | solution.py:194
  858.7 23.0 %copy.133 = bf16[12,512,1024]{1,0,2:T(8,128)(2,1)} copy(bf16[12,512,1024]{2,1,0:T(8,128)(2,1)} %multiply_convert_fusion.3) | data formatting | bytes 25165824 | tf_op jit(solution)/shard_map/while/body/eval_jaxpr/convert_element_type | solution.py:194
  975.9 30.4 %copy.129 = f32[512,1024,12]{1,0,2:T(8,128)} copy(f32[512,1024,12]{0,2,1:T(8,128)} %fusion.280) | data formatting | bytes 50331648 | tf_op jit(solution)/shard_map/while/body/eval_jaxpr/qkb,bh->hqk/dot_general | solution.py:79
  1021.7 30.4 %copy.127 = f32[512,1024,12]{1,0,2:T(8,128)} copy(f32[512,1024,12]{0,2,1:T(8,128)} %fusion.278) | data formatting | bytes 50331648 | tf_op jit(solution)/shard_map/while/body/eval_jaxpr/qkb,bh->hqk/dot_general | solution.py:79
  1067.6 30.4 %copy.128 = f32[512,1024,12]{1,0,2:T(8,128)} copy(f32[512,1024,12]{0,2,1:T(8,128)} %fusion.279) | data formatting | bytes 50331648 | tf_op jit(solution)/shard_map/while/body/eval_jaxpr/qkb,bh->hqk/dot_general | solution.py:79
  1098.0 42.1 %multiply_reduce_fusion.6 = (f32[12,512]{1,0:T(8,128)S(1)}, f32[12,512,1024]{2,1,0:T(8,128)}) fusion(f32[12,512,1024]{2,1,0:T(8,128)} %fusion.277, f32[12,512]{1,0:T(8,128)} %dynamic-slice_bitcast_fusion.2, f32[512,1024,12]{1,0,2:T(8,128)} %copy.127, f32[512,1024,12]{1,0,2:T(8,128)} %copy.128, f32[512,1024,12]{1,0,2:T(8,128)} %copy.129, ...), kind=kOutput, calls=%fused_computation.111.clone.1 | convolution fusion | flops 855631872 | bytes 128238592 | tf_op jit(solution)/shard_map/while/body/eval_jaxpr/qhd,khd->hqk/dot_general | solution.py:76
  1140.1 21.6 %multiply_convert_fusion.3 = bf16[12,512,1024]{2,1,0:T(8,128)(2,1)} fusion(f32[12,512,1024]{2,1,0:T(8,128)} %get-tuple-element.660, f32[12,512,1024]{2,1,0:T(8,128)} %fusion.277, f32[12,512]{1,0:T(8,128)S(1)} %get-tuple-element.661), kind=kLoop, calls=%fused_computation.110.clone.1 | loop fusion | flops 18874368 | bytes 62939136 | tf_op jit(solution)/shard_map/while/body/eval_jaxpr/convert_element_type | solution.py:194
  1204.4 23.0 %copy.133 = bf16[12,512,1024]{1,0,2:T(8,128)(2,1)} copy(bf16[12,512,1024]{2,1,0:T(8,128)(2,1)} %multiply_convert_fusion.3) | data formatting | bytes 25165824 | tf_op jit(solution)/shard_map/while/body/eval_jaxpr/convert_element_type | solution.py:194
  1300.6 18.6 %reduce-scatter.3.cloned.1.call-done = bf16[2,512,768]{2,1,0:T(8,128)(2,1)} async-done(((bf16[2,1024,768]{2,1,0:T(8,128)(2,1)}), bf16[2,512,768]{2,1,0:T(8,128)(2,1)}) %reduce-scatter.3.cloned.1.call-update) | async-done | bytes 1572880 | tf_op jit(solution)/shard_map/reduce_scatter | solution.py:226
  1319.2 45.6 %reduce-scatter.5.cloned.1.call-done = bf16[2,512,768]{2,1,0:T(8,128)(2,1)} async-done(((bf16[2,1024,768]{2,1,0:T(8,128)(2,1)}), bf16[2,512,768]{2,1,0:T(8,128)(2,1)}) %reduce-scatter.5.cloned.1.call-update) | async-done | bytes 1572880 | tf_op jit(solution)/shard_map/reduce_scatter | solution.py:229
  1388.2 44.0 %all-reduce = (f32[2,768]{1,0:T(2,128)}, f32[3,32,12]{1,2,0:T(8,128)}, f32[768]{0:T(1024)}, f32[768]{0:T(1024)}, f32[768]{0:T(1024)}, /*index=5*/f32[3072]{0:T(1...) all-reduce(f32[2,768]{1,0:T(2,128)S(1)} %pad_maximum_fusion.6, ...), channel_id=1, replica_groups=mesh['docs'=16,'half'=2] {'docs','half'}, use_global_device_ids=true, to_apply=%region_21.22 | all-reduce | flops 10368 | bytes 82944 | tf_op jit(solution)/shard_map/psum | solution.py:247
  1432.3 387.4 %all-reduce.4.cloned.1.call-done = (f32[128,768]{1,0:T(8,128)}, f32[768,2304]{1,0:T(8,128)}, f32[768,768]{1,0:T(8,128)}, f32[768,3072]{1,0:T(8,128)}, f32[3072,768]{1,0:T(8,128)}) async-done(((f32[128,768]{1,0:T(8,128)}, f32[768,2304]{1,0:T(8,128)}, f32[768,768]{1,0:T(8,128)}, f32[768,3072]{1,0:T(8,128)}, f32[3072,768]{1,0:T(8,128)}), (f32[128,768]{1,0:T(8,128)}, f32[768,2304]{1,0:T(8,128)}, ...) | async-done | bytes 28704784 | tf_op jit(solution)/shard_map/psum | solution.py:247
  (341 shorter events, 664.2 us)
Async XLA Ops:
  7.2 65.3 %all-gather.5.cloned.1.call-start = ((), (), s32[]{:S(2)}) async-start(), calls=%async_computation.3 | async-start | bytes 4718592 | tf_op jit(solution)/shard_map/all_gather | solution.py:126
  24.7 94.9 %all-gather.3.cloned.1.call-start = ((), (), s32[]{:S(2)}) async-start(), calls=%async_computation.2 | async-start | bytes 4718592 | tf_op jit(solution)/shard_map/all_gather | solution.py:127
  32.4 88.4 %copy-start.26 = (bf16[3,32,12]{1,2,0:T(8,128)(2,1)S(1)}, bf16[3,32,12]{1,2,0:T(8,128)(2,1)}, u32[]{:S(2)}) copy-start(bf16[3,32,12]{1,2,0:T(8,128)(2,1)} %param.29) | copy-start | bytes 6916
  32.5 1286.7 %reduce-scatter.3.cloned.1.call-start = ((), (), s32[]{:S(2)}) async-start(), calls=%async_computation.4 | async-start | bytes 4718592 | tf_op jit(solution)/shard_map/reduce_scatter | solution.py:226
  120.8 361.9 %copy-start.49 = (f32[768]{0:T(1024)S(1)}, f32[768]{0:T(1024)}, u32[]{:S(2)}) copy-start(f32[768]{0:T(1024)} %convert_element_type.984) | copy-start | bytes 9220
  482.8 40.8 %slice-start.3 = ((s8[4718592]{0:T(1024)(128)(4,1)}), s8[4194304]{0:T(1024)(128)(4,1)S(1)}, s32[]{:S(2)}) async-start(s8[4718592]{0:T(1024)(128)(4,1)} %bitcast.310), calls=%async_computation.10 | async-start | bytes 8388608
  487.7 80.5 %copy-start.10 = (f32[1024,768]{1,0:T(8,128)}, f32[1024,768]{1,0:T(8,128)S(1)}, u32[]{:S(2)}) copy-start(f32[1024,768]{1,0:T(8,128)S(1)} %get-tuple-element.471) | copy-start | bytes 9437188
  487.7 80.5 %copy-start.29 = (f32[1024]{0:T(1024)}, f32[1024]{0:T(1024)S(1)}, u32[]{:S(2)}) copy-start(f32[1024]{0:T(1024)S(1)} %broadcast_multiply_fusion.1) | copy-start | bytes 12292
  488.5 79.7 %copy-start.31 = (f32[1024]{0:T(1024)}, f32[1024]{0:T(1024)S(1)}, u32[]{:S(2)}) copy-start(f32[1024]{0:T(1024)S(1)} %fusion.154) | copy-start | bytes 12292
  488.5 35.1 %copy-start.48 = (f32[768]{0:T(1024)S(1)}, f32[768]{0:T(1024)}, u32[]{:S(2)}) copy-start(f32[768]{0:T(1024)} %convert_element_type.990) | copy-start | bytes 9220
  488.5 35.1 %slice-start.4 = ((s8[4718592]{0:T(1024)(128)(4,1)}), s8[524288]{0:T(1024)(128)(4,1)S(1)}, s32[]{:S(2)}) async-start(s8[4718592]{0:T(1024)(128)(4,1)} %bitcast.310), calls=%async_computation.11 | async-start | bytes 1048576
  722.1 30.4 %copy-start.34 = (pred[1024]{0:T(1024)(128)(4,1)S(1)}, pred[1024]{0:T(1024)(128)(4,1)}, u32[]{:S(2)}) copy-start(pred[1024]{0:T(1024)(128)(4,1)} %iota_compare_fusion.44) | copy-start | bytes 3076 | tf_op jit(solution)/shard_map/while
  794.5 21.4 %copy-start.3 = (bf16[1,512,768]{1,2,0:T(8,128)(2,1)S(1)}, bf16[1,512,768]{1,2,0:T(8,128)(2,1)}, u32[]{:S(2)}) copy-start(bf16[1,512,768]{1,2,0:T(8,128)(2,1)} %copy.126) | copy-start | bytes 2359300 | tf_op jit(solution)/shard_map/while
  881.7 13.1 copy-start.4
  894.8 13.3 copy-start.5
  908.1 13.4 copy-start.55
  1067.6 30.4 %copy-start.34 = (pred[1024]{0:T(1024)(128)(4,1)S(1)}, pred[1024]{0:T(1024)(128)(4,1)}, u32[]{:S(2)}) copy-start(pred[1024]{0:T(1024)(128)(4,1)} %iota_compare_fusion.44) | copy-start | bytes 3076 | tf_op jit(solution)/shard_map/while
  1140.1 21.6 %copy-start.3 = (bf16[1,512,768]{1,2,0:T(8,128)(2,1)S(1)}, bf16[1,512,768]{1,2,0:T(8,128)(2,1)}, u32[]{:S(2)}) copy-start(bf16[1,512,768]{1,2,0:T(8,128)(2,1)} %copy.126) | copy-start | bytes 2359300 | tf_op jit(solution)/shard_map/while
  1227.4 13.1 copy-start.4
  1253.5 13.4 copy-start.55
  1275.6 89.1 %reduce-scatter.5.cloned.1.call-start = ((), (), s32[]{:S(2)}) async-start(), calls=%async_computation.5 | async-start | bytes 4718592 | tf_op jit(solution)/shard_map/reduce_scatter | solution.py:229
  1276.3 543.3 %all-reduce.4.cloned.1.call-start = ((), (), s32[]{:S(2)}) async-start(), calls=%async_computation.6 | async-start | bytes 57409536 | tf_op jit(solution)/shard_map/psum | solution.py:247
  1276.3 16.5 slice-start.7
  1292.8 71.9 %copy-start.45 = (f32[1024]{0:T(1024)S(1)}, f32[1024]{0:T(1024)}, u32[]{:S(2)}) copy-start(f32[1024]{0:T(1024)} %copy-done.44) | copy-start | bytes 12292
  (63 other events, 401.6 us)
Sparse Core Ops, SparseCore 0:
  24.8 47.6 all-gather.4
  74.6 44.9 all-gather.2
  1275.8 43.3 reduce-scatter.2
  1321.3 43.3 reduce-scatter.4
  1379.7 439.8 all-reduce.3
where the time goes:
time: 1860 us; the launch traced here: 1850 us
  matrix products  729 us (39%)
  waiting for transfers between devices  527 us (28%)
  local copies, waits for them, and re-layouts  340 us (18%)
  other arithmetic  153 us (8%)
  blocking collectives  44 us (2%)
  loops' own time  41.2 us (2%)
    psum x1, waiting for transfers between devices, shards(): lax.psum((lay_grad, qkv_grad, qvb_grad, table_grad, outw_grad, outb_grad,...  387 us
    dot_general x4, matrix products, raw_scores(): jnp.einsum('qhd,khd->hqk', q_heads, k_heads, preferred_element_type=jnp.f...  234 us
    dot_general x12, matrix products, raw_scores(): jnp.einsum('qkb,bh->hqk', hots[kind], tables[kind], preferred_element_typ...  192 us
    dot_general x6, local copies, waits for them, and re-layouts, raw_scores(): jnp.einsum('qkb,bh->hqk', hots[kind], tables[kind], preferred_element_typ...  182 us
    dot_general x6, matrix products, attend_back(): jnp.einsum('qkb,hqk->bh', hots[kind], grad_scores, preferred_element_type...  78 us
    all_gather x1, waiting for transfers between devices, shards(): lax.all_gather(values, 'half', axis=1, tiled=True)  47.1 us
    add x12, other arithmetic, level(): return result + 16 * (rel > 0).astype(jnp.int32)  47 us
    convert_element_type x2, local copies, waits for them, and re-layouts, attend_back(): grad_scores = (probs * (grad_probs - weighted)).astype(jnp.bfloat16)  46 us
  transfers between devices with their start and end apart: 5, of which 5 were waited for; matrix products, arithmetic and copies ran while one was open for 3% of the time, Pallas kernels for 0%

commit v1 on v0

v1 whole, which is shorter than its diff:
```python
import functools, math
import numpy as np
import jax, jax.numpy as jnp
from jax import lax
from jax.experimental import pallas as pl
from jax.experimental.pallas import tpu as pltpu

BF=jnp.bfloat16; F32=jnp.float32
NEAR_EDGES = (1, 2, 3, 4, 5, 6, 7, 8, 12, 16, 24, 32, 64, 128, 256)
FAR_EDGES = (1, 2, 4, 8, 16, 32, 64, 96, 128, 192, 256, 384, 512, 768, 1024)
LOG2E=math.log2(math.e)
IB=256
JC=128

def nt(a,b):
    return lax.dot_general(a,b,(((1,),(1,)),((),())),preferred_element_type=F32)
def nn(a,b):
    return lax.dot_general(a,b,(((1,),(0,)),((),())),preferred_element_type=F32)
def level(rel, edges):
    magnitude = jnp.abs(rel)
    result = jnp.zeros(rel.shape, jnp.int32)
    for edge in edges:
        result = result + (magnitude >= edge).astype(jnp.int32)
    return result + 16 * (rel > 0).astype(jnp.int32)

def lookup(table, idx):
    rows=idx.shape[0]
    t=jnp.broadcast_to(table[0:1], (rows,128))
    return jnp.take_along_axis(t, idx, axis=1, mode="promise_in_bounds")

def far_level(d, lo, hi):
    a=jnp.abs(d)
    small=lookup(lo, jnp.minimum(a,127))
    big=lookup(hi, a>>4)
    return jnp.where(a<16, small, big)+jnp.where(d>0,16,0)

def fwd_kernel(len_ref, q_ref, k_ref, v_ref, cq_ref, ck_ref, lev_ref, tab_ref, nidx_ref,
               ctx_ref, p_ref, linv_ref, idx_ref, wide_ref, vt_ref, s_ref):
    g=pl.program_id(0); b=pl.program_id(1)
    full=k_ref.shape[0]
    nj=full//JC
    @pl.when(g==0)
    def _():
        length=len_ref[0]
        for m in range(nj):
            rows=slice(m*JC,(m+1)*JC)
            valid=(lax.broadcasted_iota(jnp.int32,(JC,128),0)+m*JC)<length
            for kind in range(2):
                ck=ck_ref[kind,rows,:]
                for c in range(IB//128):
                    d=ck-cq_ref[kind:kind+1,c*128:(c+1)*128]
                    idx=far_level(d,lev_ref[0:8],lev_ref[8:16])
                    if kind==0: idx=jnp.where(valid,idx,32)
                    idx_ref[kind,b,rows,c*128:(c+1)*128]=idx
    @pl.when(b==0)
    def _():
        vt_ref[0:128,:]=v_ref[...].T
        vt_ref[128:144,:]=jnp.ones((16,full),BF)
        for h in range(2):
            for c in range(2*full//128):
                wide_ref[h,:,c*128:(c+1)*128]=lookup(tab_ref[h,0],nidx_ref[:,c*128:(c+1)*128])
    lane=lax.broadcasted_iota(jnp.int32,(IB,128),1)
    q2=q_ref[...]*jnp.asarray(0.125,BF)
    outs=[]
    for h in range(2):
        qh=jnp.where((lane<64)==(h==0),q2,jnp.zeros_like(q2))
        top=jnp.full((8,IB),-jnp.inf,F32)
        for m in range(nj):
            rows=slice(m*JC,(m+1)*JC)
            s=nt(k_ref[rows,:],qh)
            near=wide_ref[h,:,pl.ds(pl.multiple_of(b*IB+(full-m*JC),128),IB)]
            bias=jnp.concatenate([lookup(tab_ref[h,1],idx_ref[0,b,rows,c*128:(c+1)*128])+lookup(tab_ref[h,2],idx_ref[1,b,rows,c*128:(c+1)*128]) for c in range(IB//128)],axis=1)
            s=s+near+bias
            s_ref[rows,:]=s
            top=jnp.maximum(top,jnp.max(s.reshape(JC//8,8,IB),axis=0))
        mx=jnp.max(top,axis=0,keepdims=True)*LOG2E
        for m in range(nj):
            rows=slice(m*JC,(m+1)*JC)
            p_ref[h,0,rows,:]=jnp.exp2(s_ref[rows,:]*LOG2E-mx).astype(BF)
        lhs=jnp.concatenate([vt_ref[64*h:64*h+64,:],vt_ref[128:144,:]],axis=0)
        r=nn(lhs,p_ref[h,0])
        inv=1.0/r[64:65]
        linv_ref[0,h:h+1,:]=inv
        outs.append(r[:64]*inv)
    ctx_ref[...]=jnp.concatenate(outs,axis=0).T.astype(BF)

def fwd_attention(q,k,v,qcol,kcol,vcol,length,crow,ccol,lev,tab,nidx,heads=12):
    full=q.shape[0]; width=heads*64; pairs=heads//2; nb=full//IB
    return pl.pallas_call(
        fwd_kernel, grid=(pairs,nb),
        in_specs=[pl.BlockSpec(memory_space=pltpu.SMEM),
          pl.BlockSpec((IB,128),lambda g,b:(b,qcol+g)),
          pl.BlockSpec((full,128),lambda g,b:(0,kcol+g)),
          pl.BlockSpec((full,128),lambda g,b:(0,vcol+g)),
          pl.BlockSpec((2,IB),lambda g,b:(0,b)),
          pl.BlockSpec((2,full,128),lambda g,b:(0,0,0)),
          pl.BlockSpec((16,128),lambda g,b:(0,0)),
          pl.BlockSpec((2,3,8,128),lambda g,b:(g,0,0,0)),
          pl.BlockSpec((128,2*full),lambda g,b:(0,0))],
        out_specs=[pl.BlockSpec((IB,128),lambda g,b:(b,g)),
          pl.BlockSpec((2,1,full,IB),lambda g,b:(g,b,0,0)),
          pl.BlockSpec((1,8,IB),lambda g,b:(g,0,b))],
        out_shape=[jax.ShapeDtypeStruct((full,width),BF),
          jax.ShapeDtypeStruct((heads,nb,full,IB),BF),
          jax.ShapeDtypeStruct((pairs,8,full),F32)],
        scratch_shapes=[pltpu.VMEM((2,nb,full,IB),jnp.int32),pltpu.VMEM((2,128,2*full),F32),
          pltpu.VMEM((144,full),BF),pltpu.VMEM((full,IB),F32)],
        compiler_params=pltpu.CompilerParams(vmem_limit_bytes=48*1024*1024),
        cost_estimate=pl.CostEstimate(flops=2*2*heads*full*full*64*4,bytes_accessed=heads*full*full*2,transcendentals=heads*full*full),
        name="attend",
    )(length,q,k,v,crow,ccol,lev,tab,nidx)

def bwd_kernel(q_ref,k_ref,v_ref,go_ref,ctx_ref,p_ref,linv_ref,
               dq_ref,dk_ref,dv_ref,ds_ref,diag_ref,
               kt_ref,acc_ref,wide_ref):
    g=pl.program_id(0); b=pl.program_id(1); nb=pl.num_programs(1)
    full=k_ref.shape[0]
    nj=full//JC
    @pl.when(b==0)
    def _():
        kt_ref[...]=k_ref[...].T
        acc_ref[...]=jnp.zeros_like(acc_ref)
        wide_ref[...]=jnp.zeros_like(wide_ref)
    gt=go_ref[...].astype(F32).T
    ct=ctx_ref[...].astype(F32).T
    rowi=lax.broadcasted_iota(jnp.int32,(128,IB),0)
    inv=jnp.where(rowi<64,jnp.broadcast_to(linv_ref[0,0:1,:],(128,IB)),jnp.broadcast_to(linv_ref[0,1:2,:],(128,IB)))
    gs=gt*inv
    pr=gs*ct
    gsb=gs.astype(BF)
    gos=gs.T.astype(BF)
    lane=lax.broadcasted_iota(jnp.int32,(IB,128),1)
    q2=q_ref[...]
    zero=jnp.zeros_like(q2)
    qs=[];gg=[];dqs=[]
    for h in range(2):
        keep=(lane<64)==(h==0)
        qs.append(jnp.where(keep,q2,zero)); gg.append(jnp.where(keep,gos,zero))
        dd=jnp.sum(pr[64*h:64*h+64],axis=0,keepdims=True)
        gh=jnp.where((rowi<64)==(h==0),gsb,jnp.zeros_like(gsb))
        for m in range(nj):
            rows=slice(m*JC,(m+1)*JC)
            gp=nn(v_ref[rows,:],gh)
            ds=p_ref[h,0,rows,:].astype(F32)*(gp-dd)
            ds_ref[h,0,rows,:]=ds.astype(BF)
            sl=pl.ds(pl.multiple_of(b*IB+(full-m*JC),128),IB)
            wide_ref[h,:,sl]=wide_ref[h,:,sl]+ds
        dqs.append(nn(kt_ref[64*h:64*h+64,:],ds_ref[h,0]))
    qcat=jnp.concatenate(qs,axis=0); gcat=jnp.concatenate(gg,axis=0)
    for m in range(nj):
        rows=slice(m*JC,(m+1)*JC)
        acc_ref[0,rows,:]+=nn(jnp.concatenate([ds_ref[0,0,rows,:],ds_ref[1,0,rows,:]],axis=1),qcat)
        acc_ref[1,rows,:]+=nn(jnp.concatenate([p_ref[0,0,rows,:],p_ref[1,0,rows,:]],axis=1),gcat)
    dq_ref[...]=(jnp.concatenate(dqs,axis=0)*0.125).T.astype(BF)
    @pl.when(b==nb-1)
    def _():
        dk_ref[...]=(acc_ref[0]*0.125).astype(BF)
        dv_ref[...]=acc_ref[1].astype(BF)
        for h in range(2):
            tot=jnp.zeros((8,2*full),F32)
            for r in range(16):
                x=wide_ref[h,r*8:(r+1)*8,:]
                tot=tot+pltpu.roll(x,2*full-r*8,1) if r else tot+x
            one=tot[0:1]
            for r in range(1,8):
                one=one+pltpu.roll(tot[r:r+1],2*full-r,1)
            diag_ref[0,h:h+1,:]=one

def bwd_attention(q,k,v,qcol,kcol,vcol,go,ctx,p,linv,heads=12):
    full=q.shape[0]; width=heads*64; pairs=heads//2; nb=full//IB
    return pl.pallas_call(
        bwd_kernel, grid=(pairs,nb),
        in_specs=[pl.BlockSpec((IB,128),lambda g,b:(b,qcol+g)),
          pl.BlockSpec((full,128),lambda g,b:(0,kcol+g)),
          pl.BlockSpec((full,128),lambda g,b:(0,vcol+g)),
          pl.BlockSpec((IB,128),lambda g,b:(b,g)),
          pl.BlockSpec((IB,128),lambda g,b:(b,g)),
          pl.BlockSpec((2,1,full,IB),lambda g,b:(g,b,0,0)),
          pl.BlockSpec((1,8,IB),lambda g,b:(g,0,b))],
        out_specs=[pl.BlockSpec((IB,128),lambda g,b:(b,g)),
          pl.BlockSpec((full,128),lambda g,b:(0,g)),
          pl.BlockSpec((full,128),lambda g,b:(0,g)),
          pl.BlockSpec((2,1,full,IB),lambda g,b:(g,b,0,0)),
          pl.BlockSpec((1,8,2*full),lambda g,b:(g,0,0))],
        out_shape=[jax.ShapeDtypeStruct((full,width),BF)]*3+[
          jax.ShapeDtypeStruct((heads,nb,full,IB),BF),
          jax.ShapeDtypeStruct((pairs,8,2*full),F32)],
        scratch_shapes=[pltpu.VMEM((128,full),BF),pltpu.VMEM((2,full,128),F32),pltpu.VMEM((2,128,2*full),F32)],
        compiler_params=pltpu.CompilerParams(vmem_limit_bytes=48*1024*1024),
        cost_estimate=pl.CostEstimate(flops=2*4*heads*full*full*64*4,bytes_accessed=2*heads*full*full*2,transcendentals=0),
        name="attend_back",
    )(q,k,v,go,ctx,p,linv)

THRESH=[-8192]+[1-e for e in reversed(FAR_EDGES)]+list(FAR_EDGES)
def hist_kernel(ds_ref, crow_ref, ccol_ref, out_ref, acc_ref, *, heads, dt):
    t=pl.program_id(0)
    nb=ds_ref.shape[1]
    sub=ds_ref.shape[2]//16
    @pl.when(t==0)
    def _(): acc_ref[...]=jnp.zeros_like(acc_ref)
    one=jnp.ones((16,IB),BF); zero=jnp.zeros((16,IB),BF)
    for u in range(sub):
        for kb in range(nb):
            parts=[]
            for kind in range(2):
                row=jnp.broadcast_to(crow_ref[kind:kind+1,kb*IB:(kb+1)*IB],(16,IB)).astype(dt)
                col=jnp.concatenate([ccol_ref[kind,u*16:(u+1)*16,:]]*(IB//128),axis=1)
                for e in range(32):
                    th=THRESH[min(e,30)]
                    parts.append(jnp.where(row<=(col-th).astype(dt),one,zero))
            lhs=jnp.concatenate(parts,axis=0)
            rhs=ds_ref[:,kb,u*16:(u+1)*16,:].reshape(heads*16,IB)
            acc_ref[...]+=nt(lhs,rhs)
    @pl.when(t==pl.num_programs(0)-1)
    def _():
        r=lax.broadcasted_iota(jnp.int32,(1024,heads*16),0); c=lax.broadcasted_iota(jnp.int32,(1024,heads*16),1)
        a=jnp.where((r%16)==(c%16),acc_ref[...],0.0)
        a=jnp.sum(a.reshape(64,16,heads*16),axis=1)
        out_ref[...]=a
def hist(ds,crow,ccol,heads=12,jb=32,dt=jnp.int32):
    nb,full=ds.shape[1:3]
    return pl.pallas_call(functools.partial(hist_kernel,heads=heads,dt=dt),grid=(full//jb,),
        in_specs=[pl.BlockSpec((heads,nb,jb,IB),lambda t:(0,0,t,0)),
          pl.BlockSpec((2,full),lambda t:(0,0)),
          pl.BlockSpec((2,jb,128),lambda t:(0,t,0))],
        out_specs=pl.BlockSpec((64,heads*16),lambda t:(0,0)),
        out_shape=jax.ShapeDtypeStruct((64,heads*16),F32),
        scratch_shapes=[pltpu.VMEM((1024,heads*16),F32)],
        compiler_params=pltpu.CompilerParams(vmem_limit_bytes=48*1024*1024),
        cost_estimate=pl.CostEstimate(flops=2*full*full*64*256,bytes_accessed=heads*full*full*2,transcendentals=0),
        name="bucket_sums")(ds,crow,ccol)

def tables(bias_tables, full):
    t=jnp.transpose(bias_tables.astype(F32),(2,0,1))
    t=jnp.pad(t,((0,0),(0,0),(0,96)))
    t=t.at[:,1,32].set(-1e30)
    return jnp.broadcast_to(t[:,:,None,:],(t.shape[0],3,8,128))
def np_level(d,edges):
    a=np.abs(d); r=np.zeros(d.shape,np.int32)
    for e in edges: r+=(a>=e)
    return r+16*(d>0)
def consts(full):
    lo=np_level(-np.arange(128),FAR_EDGES).astype(np.int32)
    hi=np_level(-np.arange(128)*16,FAR_EDGES).astype(np.int32)
    lev=np.concatenate([np.broadcast_to(lo,(8,128)),np.broadcast_to(hi,(8,128))])
    return jnp.asarray(lev)
def near_idx(full):
    r=lax.broadcasted_iota(jnp.int32,(128,2*full),0); u=lax.broadcasted_iota(jnp.int32,(128,2*full),1)
    return level(r+full-u,NEAR_EDGES)


from jax.sharding import PartitionSpec as P

BOXQ = 1000


def fourier(coords):
    scaled = coords.astype(F32) / BOXQ
    freqs = (jnp.arange(16, dtype=F32) + 1.0) * math.pi
    angle = scaled[:, :, None] * freqs[None, None, :]
    waves = jnp.concatenate([jnp.sin(angle), jnp.cos(angle)], axis=2)
    return jnp.transpose(waves, (1, 0, 2)).reshape(coords.shape[1], 128)


def layer_norm(resid, gain, shift):
    centre = resid - jnp.mean(resid, axis=-1, keepdims=True)
    spread = jnp.mean(centre * centre, axis=-1, keepdims=True)
    return centre * lax.rsqrt(spread + 1e-06) * gain + shift


def gelu_exact(value):
    return jax.nn.gelu(value, approximate=False)


def inner(left, right):
    return lax.dot_general(left, right, (((0,), (0,)), ((), ())), preferred_element_type=F32)


def far_table(sums):
    total = sums[0]
    count = len(FAR_EDGES)
    below = [total - sums[count - i] for i in range(count)]
    above = [sums[count + 1 + i] for i in range(count)]
    zero = jnp.zeros_like(total)
    rows = [total - below[0] - above[0]]
    for side in (below, above):
        edges = side + [zero]
        rows += [edges[i] - edges[i + 1] for i in range(count)]
        if side is below:
            rows.append(zero)
    return jnp.stack(rows)


def swap(part, me):
    own = jnp.where(me == 0, part[0], part[1])
    other = jnp.where(me == 0, part[1], part[0])
    came = lax.ppermute(other, "half", [(0, 1), (1, 0)])
    return jnp.concatenate([jnp.where(me == 0, own, came), jnp.where(me == 0, came, own)], axis=0)


def unswap(whole, me):
    rows = whole.shape[0] // 2
    own = jnp.where(me == 0, whole[:rows], whole[rows:])
    other = jnp.where(me == 0, whole[rows:], whole[:rows])
    came = lax.ppermute(other, "half", [(0, 1), (1, 0)])
    return jnp.stack([jnp.where(me == 0, own, came), jnp.where(me == 0, came, own)])


def shards(hidden_in, boxes, lengths, cotangent, layout_weight, qkv_weight, qv_bias, bias_tables, out_weight,
           out_bias, norm1_gain, norm1_bias, ff_in, ff_in_bias, ff_out, ff_out_bias, norm2_gain, norm2_bias):
    width = hidden_in.shape[2]
    full = boxes.shape[2]
    heads = bias_tables.shape[2]
    me = lax.axis_index("half")
    hidden = swap(hidden_in, me)
    box = lax.dynamic_index_in_dim(boxes, me, 1, keepdims=False)
    length = lax.dynamic_slice_in_dim(lengths, me, 1, 0)
    feats = fourier(box).astype(BF)
    start = hidden.astype(F32) + nn(feats, layout_weight)
    start_low = start.astype(BF)
    bias3 = jnp.concatenate([qv_bias[0], jnp.zeros_like(qv_bias[0]), qv_bias[1]]).astype(F32)
    qkv = (nn(start_low, qkv_weight) + bias3).astype(BF)
    crow = jnp.stack([box[0] + box[2], box[1] + box[3]])
    ccol = jnp.broadcast_to(crow[:, :, None], (2, full, 128))
    pairs = heads // 2
    context, probs, linv = fwd_attention(
        qkv, qkv, qkv, 0, pairs, 2 * pairs, length, crow, ccol, consts(full), tables(bias_tables, full),
        near_idx(full), heads)
    upstream = swap(cotangent, me).astype(F32)
    attended = nn(context, out_weight) + out_bias.astype(F32)
    mid, norm1_pull = jax.vjp(layer_norm, start + attended, norm1_gain.astype(F32), norm1_bias.astype(F32))
    mid_low = mid.astype(BF)
    hidden_pre = nn(mid_low, ff_in) + ff_in_bias.astype(F32)
    activated, gelu_pull = jax.vjp(gelu_exact, hidden_pre)
    activated = activated.astype(BF)
    branch = nn(activated, ff_out) + ff_out_bias.astype(F32)
    result, norm2_pull = jax.vjp(layer_norm, mid + branch, norm2_gain.astype(F32), norm2_bias.astype(F32))
    layer_out = unswap(result.astype(BF), me)
    grad_r2, gain2_grad, shift2_grad = norm2_pull(upstream)
    grad_ff = grad_r2.astype(BF)
    ffout_grad = inner(activated, grad_ff)
    ffoutb_grad = jnp.sum(grad_ff.astype(F32), axis=0)
    grad_inner = gelu_pull(nt(grad_ff, ff_out))[0].astype(BF)
    ffin_grad = inner(mid_low, grad_inner)
    ffinb_grad = jnp.sum(grad_inner.astype(F32), axis=0)
    grad_mid = grad_r2 + nt(grad_inner, ff_in)
    grad_r1, gain1_grad, shift1_grad = norm1_pull(grad_mid)
    grad_att = grad_r1.astype(BF)
    outw_grad = inner(context, grad_att)
    outb_grad = jnp.sum(grad_att.astype(F32), axis=0)
    grad_context = nt(grad_att, out_weight).astype(BF)
    grad_q, grad_k, grad_v, gscores, diag = bwd_attention(
        qkv, qkv, qkv, 0, pairs, 2 * pairs, grad_context, context, probs, linv, heads)
    grad_qkv = jnp.concatenate([grad_q, grad_k, grad_v], axis=1)
    qkv_grad = inner(start_low, grad_qkv)
    qvb_grad = jnp.stack([jnp.sum(grad_q.astype(F32), axis=0), jnp.sum(grad_v.astype(F32), axis=0)])
    grad_start = (grad_r1 + nt(grad_qkv, qkv_weight)).astype(BF)
    input_grad = unswap(grad_start, me)
    lay_grad = inner(feats, grad_start)
    sums = jnp.sum(hist(gscores, crow, ccol, heads, dt=jnp.int16).reshape(2, 32, heads, 16), axis=3)
    offset = lax.broadcasted_iota(jnp.int32, (2 * full, 32), 0)
    bucket = lax.broadcasted_iota(jnp.int32, (2 * full, 32), 1)
    near_hot = (level(full - offset, NEAR_EDGES) == bucket).astype(F32)
    diag = diag[:, :2].reshape(heads, 2 * full)
    near_grad = lax.dot_general(near_hot, diag, (((0,), (1,)), ((), ())), precision=lax.Precision.HIGHEST)
    table_grad = jnp.stack([near_grad, far_table(sums[0]), far_table(sums[1])])
    both = ("docs", "half")
    low = lambda x: x.astype(BF)
    ffout_total, ffin_total, outw_total = lax.psum((low(ffout_grad), low(ffin_grad), low(outw_grad)), both)
    qkv_total, lay_total = lax.psum((low(qkv_grad), low(lay_grad)), both)
    (qvb_total, table_total, outb_total, gain1_total, shift1_total, ffinb_total, ffoutb_total, gain2_total,
     shift2_total) = lax.psum((qvb_grad, table_grad, outb_grad, gain1_grad, shift1_grad, ffinb_grad, ffoutb_grad,
                               gain2_grad, shift2_grad), both)
    wide = lambda x: x.astype(F32)
    return (layer_out, input_grad, wide(lay_total), wide(qkv_total), qvb_total, table_total, wide(outw_total),
            outb_total, gain1_total, shift1_total, wide(ffin_total), ffinb_total, wide(ffout_total), ffoutb_total,
            gain2_total, shift2_total)


def solution(mesh):
    placed = (P("docs", "half", None), P(None, "docs", None), P("docs"), P("docs", "half", None)) + (P(),) * 14
    return jax.shard_map(
        shards, mesh=mesh, in_specs=placed,
        out_specs=(P("docs", "half", None), P("docs", "half", None)) + (P(),) * 14, check_vma=False)
```

time: 1860 us -> 638 us (0.34)
  matrix products: 729 us -> 117 us
  waiting for transfers between devices: 527 us -> 102 us
  local copies, waits for them, and re-layouts: 340 us -> 52.2 us
  Pallas kernels: 0 us -> 216 us
  other arithmetic: 153 us -> 66.2 us
  loops' own time: 41.2 us -> 0 us
    dot_general x41 -> x10, matrix products: 698 us -> 90.3 us  [the longest x5 53.7 us: nn(): lax.dot_general(a, b, (((1,), (0,)), ((), ())), preferred_element_type=F32)]
    psum x1, waiting for transfers between devices: 387 us -> 102 us  [shards(): qkv_total, lay_total = lax.psum((low(qkv_grad), low(lay_grad)), both)]
    pallas_call x0 -> x3, Pallas kernels: none -> 216 us  [the longest x1 113 us: fwd_attention(): pl.pallas_call(fwd_kernel, grid=(pairs, nb), in_specs=[pl.BlockSpec(memor...]
    dot_general x6 -> x0, local copies, waits for them, and re-layouts: 182 us -> none  [raw_scores(): jnp.einsum('qkb,bh->hqk', hots[kind], tables[kind], preferred_element_typ...]
    all_gather x2 -> x0, waiting for transfers between devices: 74.8 us -> none  [the longest x1 47.1 us: shards(): lax.all_gather(values, 'half', axis=1, tiled=True)]
    reduce_scatter x2 -> x0, waiting for transfers between devices: 64.1 us -> none  [the longest x1 45.6 us: shards(): lax.psum_scatter(grad_value_all.astype(jnp.bfloat16), 'half', scatter_dim...]
    convert_element_type x2 -> x0, local copies, waits for them, and re-layouts: 46 us -> none  [attend_back(): grad_scores = (probs * (grad_probs - weighted)).astype(jnp.bfloat16)]
    add x12 -> x2, other arithmetic: 47 us -> 2.41 us  [level(): return result + 16 * (rel > 0).astype(jnp.int32)]
  transfers between devices with their start and end apart: 5 -> 5, of which waited for: 5 -> 1; matrix products, arithmetic and copies ran while one was open for 3% -> 21% of each run, Pallas kernels for 0% -> 27%
where the time goes in v1:
time: 638 us; the launch traced here: 630 us
  Pallas kernels  216 us (34%)
  matrix products  117 us (18%)
  waiting for transfers between devices  102 us (16%)
  other arithmetic  66.2 us (10%)
  blocking collectives  57.7 us (9%)
  local copies, waits for them, and re-layouts  52.2 us (8%)
  between operations  14.9 us (2%)
    pallas_call x1, Pallas kernels, fwd_attention(): pl.pallas_call(fwd_kernel, grid=(pairs, nb), in_specs=[pl.BlockSpec(memor...  113 us
    psum x1, waiting for transfers between devices, shards(): qkv_total, lay_total = lax.psum((low(qkv_grad), low(lay_grad)), both)  102 us
    psum x1, blocking collectives, shards(): lax.psum((qvb_grad, table_grad, outb_grad, gain1_grad, shift1_grad, ffinb...  57.7 us
    pallas_call x1, Pallas kernels, hist(): pl.pallas_call(functools.partial(hist_kernel, heads=heads, dt=dt), grid=(...  55.5 us
    dot_general x5, matrix products, nn(): lax.dot_general(a, b, (((1,), (0,)), ((), ())), preferred_element_type=F32)  53.7 us
    pallas_call x1, Pallas kernels, bwd_attention(): pl.pallas_call(bwd_kernel, grid=(pairs, nb), in_specs=[pl.BlockSpec((IB,...  47.7 us
    dot_general x4, matrix products, nt(): lax.dot_general(a, b, (((1,), (1,)), ((), ())), preferred_element_type=F32)  34.7 us
    dot_general x5, matrix products, inner(): lax.dot_general(left, right, (((0,), (0,)), ((), ())), preferred_element_...  26.6 us
  transfers between devices with their start and end apart: 5, of which 1 were waited for; matrix products, arithmetic and copies ran while one was open for 21% of the time, Pallas kernels for 27%

profile of v1, /device:TPU:0, one launch (start us, length us, event | category | flops | bytes accessed | tf_op | source)
XLA Modules:
  0.0 630.4 jit_solution(14747760901736816077)
XLA Ops:
  7.2 2.8 fusion.92
  16.8 3.0 collective-permute-start
  49.3 5.8 add_convert_fusion.1.q_ref.k_ref.v_ref
  55.6 112.6 %attend.1 = (bf16[1024,768]{1,0:T(8,128)(2,1)S(1)}, bf16[12,4,1024,256]{3,2,1,0:T(8,128)(2,1)}, f32[6,8,1024]{2,1,0:T(8,128)S(1)}) custom-call(s32[1]{0:T(128)} %dynamic_slice.8.len_ref, bf16[1024,2304]{1,0:T(8,128)(2,1)} %add_convert_fusion.1.q_ref.k_ref.v_ref, bf16[1024,2304]{1,0:T(8,128)(2,1)} %add_convert_fusion.1.q_ref.k_ref.v_ref, ...), custom_call_target="tpu_custom_call" | custom-call | flops 12884901888 | bytes 25165824 | tf_op jit(solution)/shard_map/attend/pallas_call | solution.py:89
  171.1 36.4 %multiply_convert_fusion = (bf16[1024,3072]{1,0:T(8,128)(2,1)}, f32[1024,3072]{1,0:T(8,128)}, f32[1024,3072]{1,0:T(8,128)}) fusion(f32[3072]{0:T(1024)S(1)} %convert_element_type.261, bf16[768,3072]{1,0:T(8,128)(2,1)S(1)} %bitcast.485, f32[1024,768]{0,1:T(8,128)S(1)} %get-tuple-element.298, f32[768]{0:T(1024)S(1)} %convert_element_type.259, ...), kind=kOutput, calls=%fused_computation.4 | convolution fusion | flops 5043388416 | bytes 39348224 | tf_op jit(solution)/shard_map/dot_general | solution.py:18
  207.6 8.0 %fusion.94 = (f32[1024]{0:T(1024)S(1)}, f32[1024,768]{0,1:T(8,128)S(1)}) fusion(f32[768]{0:T(1024)S(1)} %convert_element_type.263, bf16[1024,3072]{1,0:T(8,128)(2,1)} %get-tuple-element.220, bf16[3072,768]{1,0:T(8,128)(2,1)S(1)} %bitcast.483, f32[768]{0:T(1024)S(1)} %convert_element_type.259, f32[768]{0:T(1024)S(1)} %convert_element_type.258, ...), kind=kOutput, calls=%fused_computation.306 | convolution fusion | flops 4837342208 | bytes 17323008 | tf_op jit(solution)/shard_map/dot_general | solution.py:18
  220.9 3.3 convert_reduce_fusion.2
  224.2 7.0 %convolution_convert_fusion = bf16[3072,768]{1,0:T(8,128)(2,1)} fusion(bf16[1024,3072]{1,0:T(8,128)(2,1)S(1)} %bitcast.487, bf16[1024,768]{0,1:T(8,128)(2,1)S(1)} %get-tuple-element.211), kind=kOutput, calls=%fused_computation.19 | convolution fusion | flops 4834197504 | bytes 12582912 | tf_op jit(solution)/shard_map/dot_general | solution.py:276
  231.1 18.9 %convert_reduce_fusion = (f32[3072]{0:T(1024)}, bf16[1024,3072]{1,0:T(8,128)(2,1)}) fusion(f32[1024,3072]{1,0:T(8,128)} %get-tuple-element.221, bf16[1024,768]{0,1:T(8,128)(2,1)} %copy-done.30, bf16[3072,768]{1,0:T(8,128)(2,1)} %param.35, f32[1024,3072]{1,0:T(8,128)} %get-tuple-element.299, f32[3072]{0:T(1024)S(1)} %convert_element_type.261), kind=kOutput, calls=%fused_computation.2 | convolution fusion | flops 4885312512 | bytes 37773312 | tf_op jit(solution)/shard_map/dot_general | solution.py:16
  250.1 10.1 %convolution_convert_fusion.1 = bf16[768,3072]{1,0:T(8,128)(2,1)} fusion(bf16[1024,3072]{1,0:T(8,128)(2,1)} %get-tuple-element.304, f32[1024,768]{0,1:T(8,128)} %copy-done.17, f32[768]{0:T(1024)S(1)} %convert_element_type.259, f32[768]{0:T(1024)S(1)} %convert_element_type.258, f32[1024]{0:T(1024)S(1)} %fusion.53, f32[1024]{0:T(1024)S(1)} %broadcast_multiply_fusion.1), kind=kOutput, calls=%fused_computation.20 | convolution fusion | flops 4838129664 | bytes 14170112 | tf_op jit(solution)/shard_map/dot_general | solution.py:276
  260.2 9.3 %multiply_reduce_fusion = (f32[768]{0:T(1024)}, f32[1024]{0:T(1024)S(1)}, f32[768]{0:T(1024)}, f32[1024,768]{0,1:T(8,128)S(1)}) fusion(f32[1024,768]{0,1:T(8,128)S(1)} %copy-done.18, f32[1024]{0:T(1024)S(1)} %fusion.53, f32[1024]{0:T(1024)S(1)} %broadcast_multiply_fusion.1, f32[768]{0:T(1024)S(1)} %convert_element_type.258, ...), kind=kOutput, calls=%fused_computation.32 | convolution fusion | flops 4847563776 | bytes 22061056 | tf_op jit(solution)/shard_map/dot_general | solution.py:16
  271.6 2.6 convolution_convert_fusion.3.go_ref
  274.2 47.7 %attend_back.1 = (bf16[1024,768]{1,0:T(8,128)(2,1)S(1)}, bf16[1024,768]{1,0:T(8,128)(2,1)S(1)}, bf16[1024,768]{1,0:T(8,128)(2,1)S(1)}, bf16[12,4,1024,256]{3,2,1,0:T(8,128)(2,1)}, f32[6,8,2048]{2,1,0:T(8,128)S(1)}) custom-call(bf16[1024,2304]{1,0:T(8,128)(2,1)} %add_convert_fusion.1.q_ref.k_ref.v_ref, ...), custom_call_target="tpu_custom_call" | custom-call | flops 25769803776 | bytes 50331648 | tf_op jit(solution)/shard_map/attend_back/pallas_call | solution.py:171
  325.4 5.7 convolution_convert_fusion.2
  331.1 3.8 add_convert_fusion.2
  340.8 55.5 %bucket_sums.1 = f32[64,192]{1,0:T(8,128)S(1)} custom-call(bf16[12,4,1024,256]{3,2,1,0:T(8,128)(2,1)} %get-tuple-element.43.ds_ref, s32[2,1024]{1,0:T(2,128)S(1)} %copy-done.7, s32[2,1024,128]{2,1,0:T(8,128)S(1)} %copy-done.4), custom_call_target="tpu_custom_call" | custom-call | flops 34359738368 | bytes 25165824 | tf_op jit(solution)/shard_map/bucket_sums/pallas_call | solution.py:222
  417.8 2.9 stack.43
  423.5 5.2 stack.45
  433.2 57.7 %all-reduce.1 = (f32[2,768]{1,0:T(2,128)}, f32[3,32,12]{2,1,0:T(8,128)}, f32[768]{0:T(1024)}, f32[768]{0:T(1024)}, f32[768]{0:T(1024)}, /*index=5*/f32[3072]{0:T...) all-reduce(f32[2,768]{1,0:T(2,128)} %pad_maximum_fusion.6, ...), channel_id=1, replica_groups=mesh['docs'=16,'half'=2] {'docs','half'}, use_global_device_ids=true, to_apply=%region_12.13 | all-reduce | flops 10368 | bytes 82944 | tf_op jit(solution)/shard_map/psum | solution.py:372
  501.1 2.7 copy.571
  503.7 101.8 %all-reduce.5.cloned.1.call-done = (bf16[128,768]{1,0:T(8,128)(2,1)}, bf16[768,2304]{1,0:T(8,128)(2,1)}, bf16[768,768]{1,0:T(8,128)(2,1)}, bf16[768,3072]{1,0:T(8,128)(2,1)}, bf16[3072,768]{1,0:T(8,128)(2,1)}) async-done(((bf16[128,768]{1,0:T(8,128)(2,1)}, bf16[768,2304]{1,0:T(8,128)(2,1)}, bf16[768,768]{1,0:T(8,128)(2,1)}, bf16[768,3072]{1,0:T(8,128)(2,1)}, bf16[3072,768]{1,0:T(8,128)(2,1)}), ...) | async-done | bytes 14352400 | tf_op jit(solution)/shard_map/psum | solution.py:370
  605.5 7.5 %convert_element_type.298 = f32[768,3072]{1,0:T(8,128)} convert(bf16[768,3072]{1,0:T(8,128)(2,1)} %get-tuple-element.208) | non-fusion elementwise | flops 2359296 | bytes 14155776 | tf_op jit(solution)/shard_map/convert_element_type | solution.py:374
  613.1 4.5 convert_element_type.301
  617.5 3.5 convert_element_type.276
  (197 shorter events, 97.3 us)
Async XLA Ops:
  7.2 42.1 %copy-start = (bf16[768,2304]{1,0:T(8,128)(2,1)S(1)}, bf16[768,2304]{1,0:T(8,128)(2,1)}, u32[]{:S(2)}) copy-start(bf16[768,2304]{1,0:T(8,128)(2,1)} %param.26) | copy-start | bytes 10616836
  7.2 598.3 %all-reduce.5.cloned.1.call-start = ((), (), s32[]{:S(2)}) async-start(), calls=%async_computation | async-start | bytes 28704768 | tf_op jit(solution)/shard_map/psum | solution.py:370
  16.8 31.1 %collective-permute-start = (bf16[512,768]{0,1:T(8,128)(2,1)}, bf16[512,768]{0,1:T(8,128)(2,1)}, u32[]{:S(2)}, u32[]{:S(2)}) collective-permute-start(bf16[512,768]{0,1:T(8,128)(2,1)} %select_bitcast_fusion.5), channel_id=1, source_target_pairs={{0,1},{1,0},{2,3},{3,2},{4,5},{5,4},{6,7},{7,6},{8,9},{9,8},{10,11... | collective-permute-start | bytes 2359304 | tf_op jit(solution)/shard_map/ppermute | solution.py:297
  27.7 187.8 %collective-permute-start.2 = (bf16[512,768]{0,1:T(8,128)(2,1)}, bf16[512,768]{0,1:T(8,128)(2,1)}, u32[]{:S(2)}, u32[]{:S(2)}) collective-permute-start(bf16[512,768]{0,1:T(8,128)(2,1)} %select_bitcast_fusion.2), channel_id=1, source_target_pairs={{0,1},{1,0},{2,3},{3,2},{4,5},{5,4},{6,7},{7,6},{8,9},{9,8},{10,11... | collective-permute-start | bytes 2359304 | tf_op jit(solution)/shard_map/ppermute | solution.py:297
  35.5 10.6 %copy-start.40 = (s32[128]{0:T(128)S(1)}, s32[128]{0:T(128)}, u32[]{:S(2)}) copy-start(s32[128]{0:T(128)} %iota_add_fusion) | copy-start | bytes 1540
  35.5 12.5 %copy-start.21 = (bf16[1,512,768]{1,2,0:T(8,128)(2,1)S(1)}, bf16[1,512,768]{1,2,0:T(8,128)(2,1)}, u32[]{:S(2)}) copy-start(bf16[1,512,768]{1,2,0:T(8,128)(2,1)} %copy.578) | copy-start | bytes 2359300
  35.5 12.5 %copy-start.22 = (bf16[1,512,768]{1,2,0:T(8,128)(2,1)S(1)}, bf16[1,512,768]{1,2,0:T(8,128)(2,1)}, u32[]{:S(2)}) copy-start(bf16[1,512,768]{1,2,0:T(8,128)(2,1)} %copy.579) | copy-start | bytes 2359300
  43.8 11.7 %copy-start.6 = (s32[2,1024]{1,0:T(2,128)}, s32[2,1024]{1,0:T(2,128)S(1)}, u32[]{:S(2)}) copy-start(s32[2,1024]{1,0:T(2,128)S(1)} %pad_add_fusion.cq_ref.crow_ref) | copy-start | bytes 24580
  46.1 122.1 %copy-start.25 = (f32[1024,768]{0,1:T(8,128)}, f32[1024,768]{0,1:T(8,128)S(1)}, u32[]{:S(2)}) copy-start(f32[1024,768]{0,1:T(8,128)S(1)} %fusion.95) | copy-start | bytes 9437188
  49.3 118.9 %copy-start.32 = (bf16[512,768]{0,1:T(8,128)(2,1)}, bf16[512,768]{0,1:T(8,128)(2,1)S(1)}, u32[]{:S(2)}) copy-start(bf16[512,768]{0,1:T(8,128)(2,1)S(1)} %get-tuple-element.229) | copy-start | bytes 2359300
  49.3 118.9 %copy-start.34 = (bf16[512,768]{0,1:T(8,128)(2,1)}, bf16[512,768]{0,1:T(8,128)(2,1)S(1)}, u32[]{:S(2)}) copy-start(bf16[512,768]{0,1:T(8,128)(2,1)S(1)} %get-tuple-element.230) | copy-start | bytes 2359300
  55.5 112.7 %copy-start.3 = (s32[2,1024,128]{2,1,0:T(8,128)}, s32[2,1024,128]{2,1,0:T(8,128)S(1)}, u32[]{:S(2)}) copy-start(s32[2,1024,128]{2,1,0:T(8,128)S(1)} %broadcast_in_dim.17.ck_ref.ccol_ref) | copy-start | bytes 3145732
  55.5 112.7 %copy-start.41 = (bf16[768,768]{1,0:T(8,128)(2,1)S(1)}, bf16[768,768]{1,0:T(8,128)(2,1)}, u32[]{:S(2)}) copy-start(bf16[768,768]{1,0:T(8,128)(2,1)} %param.29) | copy-start | bytes 3538948
  168.2 39.3 %slice-start = ((s8[4718592]{0:T(1024)(128)(4,1)}), s8[524288]{0:T(1024)(128)(4,1)S(1)}, s32[]{:S(2)}) async-start(s8[4718592]{0:T(1024)(128)(4,1)} %bitcast.482), calls=%async_computation.1 | async-start | bytes 1048576
  170.1 37.4 %copy-start.17 = (f32[1024,768]{0,1:T(8,128)}, f32[1024,768]{0,1:T(8,128)S(1)}, u32[]{:S(2)}) copy-start(f32[1024,768]{0,1:T(8,128)S(1)} %get-tuple-element.298) | copy-start | bytes 9437188
  170.5 37.0 %copy-start.37 = (f32[1024]{0:T(1024)}, f32[1024]{0:T(1024)S(1)}, u32[]{:S(2)}) copy-start(f32[1024]{0:T(1024)S(1)} %multiply_reduce_fusion.3) | copy-start | bytes 12292
  171.1 36.5 %slice-start.1 = ((s8[4718592]{0:T(1024)(128)(4,1)}), s8[4194304]{0:T(1024)(128)(4,1)S(1)}, s32[]{:S(2)}) async-start(s8[4718592]{0:T(1024)(128)(4,1)} %bitcast.482), calls=%async_computation.2 | async-start | bytes 8388608
  207.5 8.0 %copy-start.19 = (bf16[1,512,768]{1,2,0:T(8,128)(2,1)S(1)}, bf16[1,512,768]{1,2,0:T(8,128)(2,1)}, u32[]{:S(2)}) copy-start(bf16[1,512,768]{1,2,0:T(8,128)(2,1)} %copy.580) | copy-start | bytes 2359300
  250.1 10.1 %copy-start.13 = (f32[1024,768]{0,1:T(8,128)S(1)}, f32[1024,768]{0,1:T(8,128)}, u32[]{:S(2)}) copy-start(f32[1024,768]{0,1:T(8,128)} %copy-done.12) | copy-start | bytes 9437188
  250.1 10.1 %copy-start.18 = (f32[1024,768]{0,1:T(8,128)S(1)}, f32[1024,768]{0,1:T(8,128)}, u32[]{:S(2)}) copy-start(f32[1024,768]{0,1:T(8,128)} %copy-done.17) | copy-start | bytes 9437188
  250.1 10.1 %copy-start.43 = (bf16[1024,3072]{1,0:T(8,128)(2,1)S(1)}, bf16[1024,3072]{1,0:T(8,128)(2,1)}, u32[]{:S(2)}) copy-start(bf16[1024,3072]{1,0:T(8,128)(2,1)} %get-tuple-element.304) | copy-start | bytes 18874372
  260.1 9.3 %copy-start.38 = (f32[1024]{0:T(1024)S(1)}, f32[1024]{0:T(1024)}, u32[]{:S(2)}) copy-start(f32[1024]{0:T(1024)} %copy-done.37) | copy-start | bytes 12292
  408.3 84.2 %collective-permute-start.3 = (bf16[512,768]{0,1:T(8,128)(2,1)}, bf16[512,768]{0,1:T(8,128)(2,1)}, u32[]{:S(2)}, u32[]{:S(2)}) collective-permute-start(bf16[512,768]{0,1:T(8,128)(2,1)} %broadcast_select_fusion.2), channel_id=1, source_target_pairs={{0,1},{1,0},{2,3},{3,2},{4,5},{5,4},{6,7},{7,6},{8,9},{9,8},{10,11... | collective-permute-start | bytes 2359304 | tf_op jit(solution)/shard_map/ppermute | solution.py:305
  411.2 86.8 %collective-permute-start.1 = (bf16[512,768]{0,1:T(8,128)(2,1)}, bf16[512,768]{0,1:T(8,128)(2,1)}, u32[]{:S(2)}, u32[]{:S(2)}) collective-permute-start(bf16[512,768]{0,1:T(8,128)(2,1)} %broadcast_select_fusion.4), channel_id=1, source_target_pairs={{0,1},{1,0},{2,3},{3,2},{4,5},{5,4},{6,7},{7,6},{8,9},{9,8},{10,11... | collective-permute-start | bytes 2359304 | tf_op jit(solution)/shard_map/ppermute | solution.py:305
  (31 other events, 105.6 us)
Sparse Core Ops, SparseCore 0:
  339.0 266.4 all-reduce.4

commit v2 on v1

v2 whole, which is shorter than its diff:
```python
import functools, math
import numpy as np
import jax, jax.numpy as jnp
from jax import lax
from jax.experimental import pallas as pl
from jax.experimental.pallas import tpu as pltpu

BF=jnp.bfloat16; F32=jnp.float32
NEAR_EDGES = (1, 2, 3, 4, 5, 6, 7, 8, 12, 16, 24, 32, 64, 128, 256)
FAR_EDGES = (1, 2, 4, 8, 16, 32, 64, 96, 128, 192, 256, 384, 512, 768, 1024)
LOG2E=math.log2(math.e)
HISTF=15*10**9
IB=256
JC=128

def nt(a,b):
    return lax.dot_general(a,b,(((1,),(1,)),((),())),preferred_element_type=F32)
def nn(a,b):
    return lax.dot_general(a,b,(((1,),(0,)),((),())),preferred_element_type=F32)
def level(rel, edges):
    magnitude = jnp.abs(rel)
    result = jnp.zeros(rel.shape, jnp.int32)
    for edge in edges:
        result = result + (magnitude >= edge).astype(jnp.int32)
    return result + 16 * (rel > 0).astype(jnp.int32)

def lookup(table, idx):
    rows=idx.shape[0]
    t=jnp.broadcast_to(table[0:1], (rows,128))
    return jnp.take_along_axis(t, idx, axis=1, mode="promise_in_bounds")

UNIT=2048.0

def far_lane(d):
    a=jnp.abs(d)
    e=32-lax.clz(a)
    half=lax.shift_right_logical(a,jnp.maximum(e-2,0))&1
    return 2*e+half+jnp.where(d>0,32,0)

def fwd_kernel(len_ref, q_ref, k_ref, v_ref, cq_ref, ck_ref, tab_ref, nidx_ref,
               ctx_ref, p_ref, linv_ref, idx_ref, wide_ref, vt_ref, ka_ref, s0_ref, s1_ref, top_ref):
    t=pl.program_id(0)
    full=k_ref.shape[0]
    nj=full//JC; nb=full//IB
    last=pl.num_programs(0)-2
    now=jnp.minimum(t,last); before=jnp.maximum(t-1,0)
    g=now//nb; b=now%nb
    @pl.when(t<nb)
    def _():
        for m in range(nj):
            rows=slice(m*JC,(m+1)*JC)
            for c in range(IB//128):
                for kind in range(2):
                    idx_ref[kind,b,rows,c*128:(c+1)*128]=far_lane(ck_ref[kind,rows,:]-cq_ref[kind:kind+1,c*128:(c+1)*128])
    @pl.when(t==0)
    def _():
        key=lax.broadcasted_iota(jnp.int32,(full,128),0); lane=lax.broadcasted_iota(jnp.int32,(full,128),1)
        ka_ref[:,128:]=jnp.where((key>=len_ref[0])&(lane==0),-1e30,0.0).astype(BF)
        vt_ref[128:144,:]=jnp.ones((16,full),BF)
        s1_ref[...]=jnp.zeros_like(s1_ref)
        top_ref[...]=jnp.zeros_like(top_ref)
    @pl.when(b==0)
    def _():
        ka_ref[:,:128]=k_ref[...]
        for c in range(2*full//128):
            wide_ref[:,c*128:(c+1)*128]=lookup(tab_ref[0,0],nidx_ref[:,c*128:(c+1)*128])
    @pl.when(before%nb==0)
    def _():
        vt_ref[0:128,:]=v_ref[...].T
    scale=LOG2E/UNIT
    def body(cur_ref,prev_ref):
        rowi=lax.broadcasted_iota(jnp.int32,(128,IB),0)
        qt=(q_ref[...]*jnp.asarray(0.125*UNIT,BF)).T
        for h in range(2):
            qh=jnp.where((rowi<64)==(h==0),qt,jnp.zeros_like(qt))
            cur_ref[h]=nn(ka_ref[...],jnp.concatenate([qh,jnp.ones_like(qt)],axis=0))
        mx=[top_ref[h:h+1,:]*scale for h in range(2)]
        top=[jnp.full((8,IB),-jnp.inf,F32)]*2
        for m in range(nj):
            rows=slice(m*JC,(m+1)*JC)
            for h in range(2):
                p_ref[h,0,rows,:]=jnp.exp2(prev_ref[h,rows,:]*scale-mx[h]).astype(BF)
            x=wide_ref[:,pl.ds(pl.multiple_of(b*IB+(full-m*JC),128),IB)]
            x=x+jnp.concatenate([lookup(tab_ref[0,1],idx_ref[0,b,rows,c*128:(c+1)*128])+lookup(tab_ref[0,2],idx_ref[1,b,rows,c*128:(c+1)*128]) for c in range(IB//128)],axis=1)
            for h in range(2):
                y=(x&0xffff) if h==0 else lax.shift_right_logical(x,16)
                s=cur_ref[h,rows,:]+y.astype(F32)
                cur_ref[h,rows,:]=s
                top[h]=jnp.maximum(top[h],jnp.max(s.reshape(JC//8,8,IB),axis=0))
        for h in range(2):
            top_ref[h:h+1,:]=jnp.max(top[h],axis=0,keepdims=True)
        outs=[]
        for h in range(2):
            lhs=jnp.concatenate([vt_ref[64*h:64*h+64,:],vt_ref[128:144,:]],axis=0)
            r=nn(lhs,p_ref[h,0])
            inv=1.0/r[64:65]
            linv_ref[0,h:h+1,:]=inv
            outs.append(r[:64]*inv)
        ctx_ref[...]=jnp.concatenate(outs,axis=0).T.astype(BF)
    @pl.when(t%2==0)
    def _(): body(s0_ref,s1_ref)
    @pl.when(t%2==1)
    def _(): body(s1_ref,s0_ref)

def fwd_attention(q,k,v,qcol,kcol,vcol,length,crow,ccol,tab,nidx,heads=12):
    full=q.shape[0]; width=heads*64; pairs=heads//2; nb=full//IB; last=pairs*nb-1
    now=lambda t: jnp.minimum(t,last)
    was=lambda t: jnp.maximum(t-1,0)
    return pl.pallas_call(
        fwd_kernel, grid=(pairs*nb+1,),
        in_specs=[pl.BlockSpec(memory_space=pltpu.SMEM),
          pl.BlockSpec((IB,128),lambda t:(now(t)%nb,qcol+now(t)//nb)),
          pl.BlockSpec((full,128),lambda t:(0,kcol+now(t)//nb)),
          pl.BlockSpec((full,128),lambda t:(0,vcol+was(t)//nb)),
          pl.BlockSpec((2,IB),lambda t:(0,now(t)%nb)),
          pl.BlockSpec((2,full,128),lambda t:(0,0,0)),
          pl.BlockSpec((1,3,8,128),lambda t:(now(t)//nb,0,0,0)),
          pl.BlockSpec((128,2*full),lambda t:(0,0))],
        out_specs=[pl.BlockSpec((IB,128),lambda t:(was(t)%nb,was(t)//nb)),
          pl.BlockSpec((2,1,full,IB),lambda t:(was(t)//nb,was(t)%nb,0,0)),
          pl.BlockSpec((1,8,IB),lambda t:(was(t)//nb,0,was(t)%nb))],
        out_shape=[jax.ShapeDtypeStruct((full,width),BF),
          jax.ShapeDtypeStruct((heads,nb,full,IB),BF),
          jax.ShapeDtypeStruct((pairs,8,full),F32)],
        scratch_shapes=[pltpu.VMEM((2,nb,full,IB),jnp.int32),pltpu.VMEM((128,2*full),jnp.int32),
          pltpu.VMEM((144,full),BF),pltpu.VMEM((full,256),BF),pltpu.VMEM((2,full,IB),F32),pltpu.VMEM((2,full,IB),F32),
          pltpu.VMEM((8,IB),F32)],
        compiler_params=pltpu.CompilerParams(vmem_limit_bytes=48*1024*1024),
        cost_estimate=pl.CostEstimate(flops=1000,bytes_accessed=1000,transcendentals=0),
        name="attend",
    )(length,q,k,v,crow,ccol,tab,nidx)

def bwd_kernel(q_ref,k_ref,v_ref,go_ref,ctx_ref,p_ref,linv_ref,
               g3_ref,ds_ref,diag_ref,
               kt_ref,acc_ref,wide_ref,gp_ref):
    g=pl.program_id(0); b=pl.program_id(1); nb=pl.num_programs(1)
    full=k_ref.shape[0]
    nj=full//JC
    @pl.when(b==0)
    def _():
        kt_ref[...]=k_ref[...].T
        acc_ref[...]=jnp.zeros_like(acc_ref)
        wide_ref[...]=jnp.zeros_like(wide_ref)
    gt=go_ref[...].astype(F32).T
    ct=ctx_ref[...].astype(F32).T
    rowi=lax.broadcasted_iota(jnp.int32,(128,IB),0)
    inv=jnp.where(rowi<64,jnp.broadcast_to(linv_ref[0,0:1,:],(128,IB)),jnp.broadcast_to(linv_ref[0,1:2,:],(128,IB)))
    gs=gt*inv
    pr=gs*ct
    gsb=gs.astype(BF)
    gos=gs.T.astype(BF)
    lane=lax.broadcasted_iota(jnp.int32,(IB,128),1)
    q2=q_ref[...]
    zero=jnp.zeros_like(q2)
    qs=[];gg=[];dqs=[];dds=[]
    for h in range(2):
        keep=(lane<64)==(h==0)
        qs.append(jnp.where(keep,q2,zero)); gg.append(jnp.where(keep,gos,zero))
        dd=jnp.sum(pr[64*h:64*h+64],axis=0,keepdims=True)
        gh=jnp.where((rowi<64)==(h==0),gsb,jnp.zeros_like(gsb))
        gp_ref[h]=nn(v_ref[...],gh)
        dds.append(dd)
    for h in range(2):
        for m in range(nj):
            rows=slice(m*JC,(m+1)*JC)
            ds=p_ref[h,0,rows,:].astype(F32)*(gp_ref[h,rows,:]-dds[h])
            ds_ref[h,0,rows,:]=ds.astype(BF)
            sl=pl.ds(pl.multiple_of(b*IB+(full-m*JC),128),IB)
            wide_ref[h,:,sl]=wide_ref[h,:,sl]+ds
        dqs.append(nn(kt_ref[64*h:64*h+64,:],ds_ref[h,0]))
    qcat=jnp.concatenate(qs,axis=0); gcat=jnp.concatenate(gg,axis=0)
    acc_ref[0]+=nn(jnp.concatenate([ds_ref[0,0],ds_ref[1,0]],axis=1),qcat)
    acc_ref[1]+=nn(jnp.concatenate([p_ref[0,0],p_ref[1,0]],axis=1),gcat)
    g3_ref[0,pl.ds(pl.multiple_of(b*IB,IB),IB),:]=(jnp.concatenate(dqs,axis=0)*0.125).T.astype(BF)
    @pl.when(b==nb-1)
    def _():
        g3_ref[1]=(acc_ref[0]*0.125).astype(BF)
        g3_ref[2]=acc_ref[1].astype(BF)
        for h in range(2):
            tot=jnp.zeros((8,2*full),F32)
            for r in range(16):
                x=wide_ref[h,r*8:(r+1)*8,:]
                tot=tot+pltpu.roll(x,2*full-r*8,1) if r else tot+x
            one=tot[0:1]
            for r in range(1,8):
                one=one+pltpu.roll(tot[r:r+1],2*full-r,1)
            diag_ref[0,h:h+1,:]=one

def bwd_attention(q,k,v,qcol,kcol,vcol,go,ctx,p,linv,heads=12):
    full=q.shape[0]; width=heads*64; pairs=heads//2; nb=full//IB
    return pl.pallas_call(
        bwd_kernel, grid=(pairs,nb),
        in_specs=[pl.BlockSpec((IB,128),lambda g,b:(b,qcol+g)),
          pl.BlockSpec((full,128),lambda g,b:(0,kcol+g)),
          pl.BlockSpec((full,128),lambda g,b:(0,vcol+g)),
          pl.BlockSpec((IB,128),lambda g,b:(b,g)),
          pl.BlockSpec((IB,128),lambda g,b:(b,g)),
          pl.BlockSpec((2,1,full,IB),lambda g,b:(g,b,0,0)),
          pl.BlockSpec((1,8,IB),lambda g,b:(g,0,b))],
        out_specs=[pl.BlockSpec((3,full,128),lambda g,b:(0,0,g)),
          pl.BlockSpec((2,1,full,IB),lambda g,b:(g,b,0,0)),
          pl.BlockSpec((1,8,2*full),lambda g,b:(g,0,0))],
        out_shape=[jax.ShapeDtypeStruct((3,full,width),BF),
          jax.ShapeDtypeStruct((heads,nb,full,IB),BF),
          jax.ShapeDtypeStruct((pairs,8,2*full),F32)],
        scratch_shapes=[pltpu.VMEM((128,full),BF),pltpu.VMEM((2,full,128),F32),pltpu.VMEM((2,128,2*full),F32),pltpu.VMEM((2,full,IB),F32)],
        compiler_params=pltpu.CompilerParams(vmem_limit_bytes=48*1024*1024),
        cost_estimate=pl.CostEstimate(flops=1000,bytes_accessed=1000,transcendentals=0),
        input_output_aliases={5:1}, name="attend_back",
    )(q,k,v,go,ctx,p,linv)

THRESH=[-8192]+[1-e for e in reversed(FAR_EDGES)]+list(FAR_EDGES)
def hist_kernel(ds_ref, crow_ref, ccol_ref, out_ref, acc_ref, *, heads, dt):
    t=pl.program_id(0)
    nb=ds_ref.shape[1]
    sub=ds_ref.shape[2]//16
    @pl.when(t==0)
    def _(): acc_ref[...]=jnp.zeros_like(acc_ref)
    one=jnp.ones((16,IB),BF); zero=jnp.zeros((16,IB),BF)
    for u in range(sub):
        for kb in range(nb):
            parts=[]
            for kind in range(2):
                row=jnp.broadcast_to(crow_ref[kind:kind+1,kb*IB:(kb+1)*IB],(16,IB)).astype(dt)
                col=jnp.concatenate([ccol_ref[kind,u*16:(u+1)*16,:]]*(IB//128),axis=1)
                for e in range(32):
                    th=THRESH[min(e,30)]
                    parts.append(jnp.where(row<=(col-th).astype(dt),one,zero))
            lhs=jnp.concatenate(parts,axis=0)
            rhs=ds_ref[:,kb,u*16:(u+1)*16,:].reshape(heads*16,IB)
            acc_ref[...]+=nt(lhs,rhs)
    @pl.when(t==pl.num_programs(0)-1)
    def _():
        r=lax.broadcasted_iota(jnp.int32,(1024,heads*16),0); c=lax.broadcasted_iota(jnp.int32,(1024,heads*16),1)
        a=jnp.where((r%16)==(c%16),acc_ref[...],0.0)
        a=jnp.sum(a.reshape(64,16,heads*16),axis=1)
        out_ref[...]=a
def hist(ds,crow,ccol,heads=12,jb=32,dt=jnp.int32,part=0,parts=1):
    nb,full=ds.shape[1:3]; steps=full//jb//parts; at=part*steps
    return pl.pallas_call(functools.partial(hist_kernel,heads=heads,dt=dt),grid=(steps,),
        in_specs=[pl.BlockSpec((heads,nb,jb,IB),lambda t:(0,0,t+at,0)),
          pl.BlockSpec((2,full),lambda t:(0,0)),
          pl.BlockSpec((2,jb,128),lambda t:(0,t+at,0))],
        out_specs=pl.BlockSpec((64,heads*16),lambda t:(0,0)),
        out_shape=jax.ShapeDtypeStruct((64,heads*16),F32),
        scratch_shapes=[pltpu.VMEM((1024,heads*16),F32)],
        compiler_params=pltpu.CompilerParams(vmem_limit_bytes=48*1024*1024),
        cost_estimate=pl.CostEstimate(flops=HISTF,bytes_accessed=1000,transcendentals=0),
        name="bucket_sums")(ds,crow,ccol)

def np_level(d,edges):
    a=np.abs(d); r=np.zeros(d.shape,np.int32)
    for e in edges: r+=(a>=e)
    return r+16*(d>0)
def lanes_of():
    lane=np.arange(128)
    e=(lane%32)//2; half=lane%2
    a=np.where(e==0,0,np.where(e==1,1,2**np.maximum(e-1,0)+half*2**np.maximum(e-2,0)))
    return np_level(np.where((lane//32)%2==1,a,-a),FAR_EDGES)
def tables(bias_tables):
    near=np.arange(128)%32; far=lanes_of()
    hot=np.stack([near,far,far])[:,:,None]==np.arange(32)
    t=jnp.einsum('klb,kbh->hkl',jnp.asarray(hot,BF),bias_tables,preferred_element_type=F32)
    t=jnp.round((t+4.0)*UNIT).astype(jnp.int32)
    t=t[0::2]+(t[1::2]<<16)
    return jnp.broadcast_to(t[:,:,None,:],(t.shape[0],3,8,128))
def near_idx(full):
    r=lax.broadcasted_iota(jnp.int32,(128,2*full),0); u=lax.broadcasted_iota(jnp.int32,(128,2*full),1)
    return level(r+full-u,NEAR_EDGES)


from jax.sharding import PartitionSpec as P

BOXQ = 1000
BOTH = ("docs", "half")
TIE = -1


def fourier(coords):
    scaled = coords.astype(F32) / BOXQ
    freqs = (jnp.arange(16, dtype=F32) + 1.0) * math.pi
    angle = scaled[:, :, None] * freqs[None, None, :]
    waves = jnp.concatenate([jnp.sin(angle), jnp.cos(angle)], axis=2)
    return jnp.transpose(waves, (1, 0, 2)).reshape(coords.shape[1], 128)


def layer_norm(resid, gain, shift):
    centre = resid - jnp.mean(resid, axis=-1, keepdims=True)
    spread = jnp.mean(centre * centre, axis=-1, keepdims=True)
    return centre * lax.rsqrt(spread + 1e-06) * gain + shift


def gelu_pair(x):
    bell = jnp.exp2(x * x * (-0.5 * LOG2E))
    t = 1.0 / (1.0 + (0.3275911 * math.sqrt(0.5)) * jnp.abs(x))
    poly = t * (0.254829592 + t * (-0.284496736 + t * (1.421413741 + t * (-1.453152027 + t * 1.061405429))))
    tail = 0.5 * poly * bell
    cdf = jnp.where(x < 0, tail, 1.0 - tail)
    return x * cdf, cdf + x * bell * (1.0 / math.sqrt(2.0 * math.pi))


def inner(left, right):
    return lax.dot_general(left, right, (((0,), (0,)), ((), ())), preferred_element_type=F32)


def far_table(sums):
    total = sums[0]
    count = len(FAR_EDGES)
    below = [total - sums[count - i] for i in range(count)]
    above = [sums[count + 1 + i] for i in range(count)]
    zero = jnp.zeros_like(total)
    rows = [total - below[0] - above[0]]
    for side in (below, above):
        edges = side + [zero]
        rows += [edges[i] - edges[i + 1] for i in range(count)]
        if side is below:
            rows.append(zero)
    return jnp.stack(rows)


def swap(part, me):
    own = jnp.where(me == 0, part[0], part[1])
    other = jnp.where(me == 0, part[1], part[0])
    came = lax.ppermute(other, "half", [(0, 1), (1, 0)])
    return jnp.concatenate([jnp.where(me == 0, own, came), jnp.where(me == 0, came, own)], axis=0)


def unswap(whole, me):
    rows = whole.shape[0] // 2
    own = jnp.where(me == 0, whole[:rows], whole[rows:])
    other = jnp.where(me == 0, whole[rows:], whole[:rows])
    came = lax.ppermute(other, "half", [(0, 1), (1, 0)])
    return jnp.stack([jnp.where(me == 0, own, came), jnp.where(me == 0, came, own)])


class Route:
    def __init__(self):
        docs = lax.axis_size("docs")
        bits = [("docs", 1 << i) for i in range(docs.bit_length() - 1)]
        self.core = bits[0]
        y = ("half", 1)
        self.orders = [bits[1:2] + [y] + bits[2:], [y] + bits[1:], bits[2:] + bits[1:2] + [y]]
        self.all = bits + [y]
        self.pieces = docs * 2 // 2

    def mine(self, step):
        return (lax.axis_index(step[0]) // step[1]) % 2

    def move(self, x, step):
        axis, bit = step
        return lax.ppermute(x, axis, [(i, i ^ bit) for i in range(lax.axis_size(axis))])

    def product(self, left, right):
        mine = self.mine(self.core)
        cols = left.shape[1] // 2
        dot = lambda at: jnp.einsum("td,...tf->...df", lax.dynamic_slice_in_dim(left, at * cols, cols, 1), right,
                                    preferred_element_type=F32)
        send = dot(1 - mine).astype(BF)
        keep = dot(mine)
        return (keep + self.move(send, self.core).astype(F32)).astype(BF)

    def scatter(self, x, step):
        mine = self.mine(step)
        half = x.shape[0] // 2
        send = lax.dynamic_slice_in_dim(x, (1 - mine) * half, half, 0)
        keep = lax.dynamic_slice_in_dim(x, mine * half, half, 0)
        return (keep.astype(F32) + self.move(send, step).astype(F32)).astype(BF)

    def gather(self, x, step):
        mine = self.mine(step)
        came = self.move(x, step)
        return jnp.concatenate([jnp.where(mine == 0, x, came), jnp.where(mine == 0, came, x)], axis=0)

    def total(self, parts, between=None, tie=None):
        rows = [p.shape[0] // self.pieces for p in parts]
        x = jnp.concatenate([p.reshape(self.pieces, r, p.shape[1]) for p, r in zip(parts, rows)], axis=1)
        count = x.shape[1]
        x = jnp.pad(x, ((0, 0), (0, -count % 16), (0, 0)))
        cut = x.shape[1] // 2
        lanes = [x[:, :cut], x[:, cut:]]
        for i in range(len(self.orders[0])):
            if between and i < 4:
                lanes = between(i, 4, lanes)
            lanes = [self.scatter(x, order[i]) for x, order in zip(lanes, self.orders)]
        for i in reversed(range(len(self.orders[0]))):
            if tie and i == TIE:
                lanes = tie(lanes)
            lanes = [self.gather(x, order[i]) for x, order in zip(lanes, self.orders)]
        came = [self.move(x, self.core) for x in lanes]
        mine = self.mine(self.core)
        own, came = jnp.concatenate(lanes, axis=1), jnp.concatenate(came, axis=1)
        whole = jnp.concatenate([jnp.where(mine == 0, own, came), jnp.where(mine == 0, came, own)], axis=0)
        out = []
        at = 0
        for p, r in zip(parts, rows):
            out.append(whole[:, at:at + r].reshape(-1, p.shape[1]).astype(F32))
            at += r
        return out

    def small(self, parts):
        sizes = [p.size for p in parts]
        flat = jnp.concatenate([p.reshape(-1) for p in parts])
        count = flat.shape[0]
        flat = jnp.pad(flat, (0, -count % 1024)).reshape(-1, 128)
        for step in self.all:
            flat = flat + self.move(flat, step)
        flat = flat.reshape(-1)
        out = []
        at = 0
        for p, n in zip(parts, sizes):
            out.append(flat[at:at + n].reshape(p.shape))
            at += n
        return out


def shards(hidden_in, boxes, lengths, cotangent, layout_weight, qkv_weight, qv_bias, bias_tables, out_weight,
           out_bias, norm1_gain, norm1_bias, ff_in, ff_in_bias, ff_out, ff_out_bias, norm2_gain, norm2_bias):
    width = hidden_in.shape[2]
    full = boxes.shape[2]
    heads = bias_tables.shape[2]
    me = lax.axis_index("half")
    route = Route()
    hidden = swap(hidden_in, me)
    box = lax.dynamic_index_in_dim(boxes, me, 1, keepdims=False)
    length = lax.dynamic_slice_in_dim(lengths, me, 1, 0)
    feats = fourier(box).astype(BF)
    start = hidden.astype(F32) + nn(feats, layout_weight)
    start_low = start.astype(BF)
    bias3 = jnp.concatenate([qv_bias[0], jnp.zeros_like(qv_bias[0]), qv_bias[1]]).astype(F32)
    qkv = (nn(start_low, qkv_weight) + bias3).astype(BF)
    crow = jnp.stack([box[0] + box[2], box[1] + box[3]])
    ccol = jnp.broadcast_to(crow[:, :, None], (2, full, 128))
    pairs = heads // 2
    context, probs, linv = fwd_attention(
        qkv, qkv, qkv, 0, pairs, 2 * pairs, length, crow, ccol, tables(bias_tables), near_idx(full), heads)
    upstream = swap(cotangent, me).astype(F32)
    attended = nn(context, out_weight) + out_bias.astype(F32)
    mid, norm1_pull = jax.vjp(layer_norm, start + attended, norm1_gain.astype(F32), norm1_bias.astype(F32))
    mid_low = mid.astype(BF)
    hidden_pre = nn(mid_low, ff_in) + ff_in_bias.astype(F32)
    activated, slope = gelu_pair(hidden_pre)
    activated = activated.astype(BF)
    slope = slope.astype(BF)
    branch = nn(activated, ff_out) + ff_out_bias.astype(F32)
    result, norm2_pull = jax.vjp(layer_norm, mid + branch, norm2_gain.astype(F32), norm2_bias.astype(F32))
    layer_out = unswap(result.astype(BF), me)
    grad_r2, gain2_grad, shift2_grad = norm2_pull(upstream)
    grad_ff = grad_r2.astype(BF)
    ffout_part = inner(activated, grad_ff).astype(BF)
    ffoutb_grad = jnp.sum(grad_ff.astype(F32), axis=0)
    grad_inner = (nt(grad_ff, ff_out) * slope.astype(F32)).astype(BF)
    ffin_part = inner(mid_low, grad_inner).astype(BF)
    ffinb_grad = jnp.sum(grad_inner.astype(F32), axis=0)
    grad_mid = grad_r2 + nt(grad_inner, ff_in)
    grad_r1, gain1_grad, shift1_grad = norm1_pull(grad_mid)
    grad_att = grad_r1.astype(BF)
    outw_part = inner(context, grad_att).astype(BF)
    outb_grad = jnp.sum(grad_att.astype(F32), axis=0)
    grad_context = nt(grad_att, out_weight).astype(BF)
    early = jnp.concatenate([ffout_part] + [ffin_part[:, c * width:(c + 1) * width] for c in range(ffin_part.shape[1] // width)] + [outw_part], axis=0)
    grad_context = lax.optimization_barrier((early, grad_context))[1]
    early = lax.psum(early, BOTH)
    grad3, gscores, diag = bwd_attention(
        qkv, qkv, qkv, 0, pairs, 2 * pairs, grad_context, context, probs, linv, heads)
    qkv_part = route.product(start_low, grad3)
    qvb_grad = jnp.sum(grad3.astype(F32), axis=1)[0::2]
    grad_start = (grad_r1 + sum(nt(grad3[c], qkv_weight[:, c * width:(c + 1) * width]) for c in range(3))).astype(BF)
    input_grad = unswap(grad_start, me)
    lay_part = route.product(feats, grad_start)
    bucket_parts = []

    def between(i, count, lanes):
        row = crow
        if i:
            row, *lanes = lax.optimization_barrier((crow, *lanes))
        bucket_parts.append(hist(gscores, row, ccol, heads, dt=jnp.int16, part=i, parts=count))
        return lanes

    held = [early]

    def tie(lanes):
        held[0], *lanes = lax.optimization_barrier((held[0], *lanes))
        return lanes

    groups = route.total([qkv_part[0], qkv_part[1], qkv_part[2], lay_part], between, tie)
    early = held[0]
    sums = jnp.sum(sum(bucket_parts).reshape(2, 32, heads, 16), axis=3)
    offset = lax.broadcasted_iota(jnp.int32, (2 * full, 32), 0)
    bucket = lax.broadcasted_iota(jnp.int32, (2 * full, 32), 1)
    near_hot = (level(full - offset, NEAR_EDGES) == bucket).astype(F32)
    diag = diag[:, :2].reshape(heads, 2 * full)
    near_grad = lax.dot_general(near_hot, diag, (((0,), (1,)), ((), ())), precision=lax.Precision.HIGHEST)
    table_grad = jnp.stack([near_grad, far_table(sums[0]), far_table(sums[1])])

    qkv_total = jnp.concatenate(groups[:3], axis=1)
    lay_total = groups[3]
    (ffinb_total, ffoutb_total, gain2_total, shift2_total, outb_total, gain1_total, shift1_total, qvb_total,
     table_total) = route.small([ffinb_grad, ffoutb_grad, gain2_grad, shift2_grad, outb_grad, gain1_grad, shift1_grad,
                                 qvb_grad, table_grad])
    ff = ffin_part.shape[1]
    ffout_total = early[:ff].astype(F32)
    ffin_total = jnp.concatenate([early[ff + c * width:ff + (c + 1) * width] for c in range(ff // width)], axis=1).astype(F32)
    outw_total = early[2 * ff:].astype(F32)
    return (layer_out, input_grad, lay_total, qkv_total, qvb_total, table_total, outw_total,
            outb_total, gain1_total, shift1_total, ffin_total, ffinb_total, ffout_total, ffoutb_total,
            gain2_total, shift2_total)


def solution(mesh):
    placed = (P("docs", "half", None), P(None, "docs", None), P("docs"), P("docs", "half", None)) + (P(),) * 14
    return jax.shard_map(
        shards, mesh=mesh, in_specs=placed,
        out_specs=(P("docs", "half", None), P("docs", "half", None)) + (P(),) * 14, check_vma=False)
```

time: 638 us -> 522 us (0.82)
  blocking collectives: 57.7 us -> 0 us
  Pallas kernels: 216 us -> 169 us
  starting transfers between devices: 5.03 us -> 28 us
  waiting for transfers between devices: 102 us -> 86.7 us
  local copies, waits for them, and re-layouts: 52.2 us -> 39.8 us
    psum x1, waiting for transfers between devices: 102 us -> 27.3 us  [shards(): early = lax.psum(early, BOTH)]
    ppermute x0 -> x25, waiting for transfers between devices: none -> 59.4 us  [move(): lax.ppermute(x, axis, [(i, i ^ bit) for i in range(lax.axis_size(axis))])]
    psum x1 -> x0, blocking collectives: 57.7 us -> none  [shards(): lax.psum((qvb_grad, table_grad, outb_grad, gain1_grad, shift1_grad, ffinb...]
    pallas_call x1, Pallas kernels: 113 us -> 61.9 us  [fwd_attention(): pl.pallas_call(fwd_kernel, grid=(pairs * nb + 1,), in_specs=[pl.BlockSpec...]
    ppermute x0 -> x25, starting transfers between devices: none -> 22.3 us  [move(): lax.ppermute(x, axis, [(i, i ^ bit) for i in range(lax.axis_size(axis))])]
    dot_general x5, matrix products: 53.7 us -> 34.6 us  [nn(): lax.dot_general(a, b, (((1,), (0,)), ((), ())), preferred_element_type=F32)]
    dot_general x4 -> x6, matrix products: 34.7 us -> 46.1 us  [nt(): lax.dot_general(a, b, (((1,), (1,)), ((), ())), preferred_element_type=F32)]
    dot_general x0 -> x5, matrix products: none -> 11.2 us  [the longest x4 9.76 us: product(): jnp.einsum('td,...tf->...df', lax.dynamic_slice_in_dim(left, at * cols, c...]
  transfers between devices with their start and end apart: 5 -> 30, of which waited for: 1 -> 13; matrix products, arithmetic and copies ran while one was open for 21% -> 23% of each run, Pallas kernels for 27% -> 24%
where the time goes in v2:
time: 522 us; the launch traced here: 517 us
  Pallas kernels  169 us (32%)
  matrix products  111 us (21%)
  waiting for transfers between devices  86.7 us (17%)
  other arithmetic  66.6 us (13%)
  local copies, waits for them, and re-layouts  39.8 us (8%)
  starting transfers between devices  28 us (5%)
  between operations  15.6 us (3%)
    pallas_call x1, Pallas kernels, fwd_attention(): pl.pallas_call(fwd_kernel, grid=(pairs * nb + 1,), in_specs=[pl.BlockSpec...  61.9 us
    pallas_call x4, Pallas kernels, hist(): pl.pallas_call(functools.partial(hist_kernel, heads=heads, dt=dt), grid=(...  60.2 us
    ppermute x25, waiting for transfers between devices, move(): lax.ppermute(x, axis, [(i, i ^ bit) for i in range(lax.axis_size(axis))])  59.4 us
    pallas_call x1, Pallas kernels, bwd_attention(): pl.pallas_call(bwd_kernel, grid=(pairs, nb), in_specs=[pl.BlockSpec((IB,...  47.3 us
    dot_general x6, matrix products, nt(): lax.dot_general(a, b, (((1,), (1,)), ((), ())), preferred_element_type=F32)  46.1 us
    dot_general x5, matrix products, nn(): lax.dot_general(a, b, (((1,), (0,)), ((), ())), preferred_element_type=F32)  34.6 us
    psum x1, waiting for transfers between devices, shards(): early = lax.psum(early, BOTH)  27.3 us
    ppermute x25, starting transfers between devices, move(): lax.ppermute(x, axis, [(i, i ^ bit) for i in range(lax.axis_size(axis))])  22.3 us
  transfers between devices with their start and end apart: 30, of which 13 were waited for; matrix products, arithmetic and copies ran while one was open for 23% of the time, Pallas kernels for 24%

profile of v2, /device:TPU:0, one launch (start us, length us, event | category | flops | bytes accessed | tf_op | source)
XLA Modules:
  0.0 517.3 jit_solution(8043543948057664674)
XLA Ops:
  45.4 5.6 %add_convert_fusion.1.q_ref.k_ref.v_ref = bf16[1024,2304]{1,0:T(8,128)(2,1)} fusion(bf16[1024,768]{0,1:T(8,128)(2,1)S(1)} %get-tuple-element.320, bf16[768,2304]{1,0:T(8,128)(2,1)S(1)} %copy-done.26, f32[2304]{0:T(1024)S(1)} %maximum_convert_fusion.3), kind=kOutput, calls=%fused_computation.8 | convolution fusion | flops 3628597248 | bytes 9839616 | tf_op jit(solution)/shard_map/dot_general | solution.py:19
  51.3 61.9 %attend.1 = (bf16[1024,768]{1,0:T(8,128)(2,1)S(1)}, bf16[12,4,1024,256]{3,2,1,0:T(8,128)(2,1)}, f32[6,8,1024]{2,1,0:T(8,128)S(1)}) custom-call(s32[1]{0:T(128)} %dynamic_slice.68.len_ref, bf16[1024,2304]{1,0:T(8,128)(2,1)} %add_convert_fusion.1.q_ref.k_ref.v_ref, bf16[1024,2304]{1,0:T(8,128)(2,1)} %add_convert_fusion.1.q_ref.k_ref.v_ref, ...), custom_call_target="tpu_custom_call" | custom-call | flops 1000 | bytes 1000 | tf_op jit(solution)/shard_map/attend/pallas_call | solution.py:109
  116.0 18.4 %multiply_convert_fusion.1 = (bf16[1024,3072]{1,0:T(8,128)(2,1)}, f32[1024,3072]{1,0:T(8,128)}) fusion(f32[3072]{0:T(1024)S(1)} %copy-done.34, bf16[768,3072]{1,0:T(8,128)(2,1)S(1)} %bitcast.547, f32[1024,768]{0,1:T(8,128)S(1)} %get-tuple-element.323, f32[768]{0:T(1024)S(1)} %copy-done.39, f32[768]{0:T(1024)S(1)} %convert_element_type.369, ...), kind=kOutput, calls=%fused_computation.4 | convolution fusion | flops 4908122112 | bytes 26765312 | tf_op jit(solution)/shard_map/dot_general | solution.py:19
  134.4 8.1 %fusion.130 = (f32[1024]{0:T(1024)S(1)}, f32[1024,768]{0,1:T(8,128)S(1)}) fusion(f32[768]{0:T(1024)S(1)} %copy-done.40, bf16[1024,3072]{1,0:T(8,128)(2,1)} %get-tuple-element.324, bf16[3072,768]{1,0:T(8,128)(2,1)S(1)} %bitcast.545, f32[768]{0:T(1024)S(1)} %copy-done.39, f32[768]{0:T(1024)S(1)} %convert_element_type.369, f32[1024]{0:T(1024)S(1)} %fusion.89, ...), kind=kOutput, calls=%fused_computation.417 | convolution fusion | flops 4837342208 | bytes 17323008 | tf_op jit(solution)/shard_map/dot_general | solution.py:19
  150.5 6.9 %fusion = bf16[6912,768]{1,0:T(8,128)(2,1)} fusion(bf16[1024,3072]{1,0:T(8,128)(2,1)S(1)} %bitcast.549, bf16[1024,768]{0,1:T(8,128)(2,1)S(1)} %get-tuple-element.207), kind=kOutput, calls=%fused_computation.11 | convolution fusion | flops 4834197504 | bytes 12582912 | tf_op jit(solution)/shard_map/dot_general | solution.py:303
  157.4 18.7 %convert_reduce_fusion = (f32[3072]{0:T(1024)}, bf16[1024,3072]{1,0:T(8,128)(2,1)}) fusion(f32[1024,3072]{1,0:T(8,128)} %get-tuple-element.325, f32[3072]{0:T(1024)S(1)} %copy-done.34, bf16[1024,768]{0,1:T(8,128)(2,1)S(1)} %get-tuple-element.207, bf16[3072,768]{1,0:T(8,128)(2,1)S(1)} %bitcast.545), kind=kOutput, calls=%fused_computation.1 | convolution fusion | flops 4926206976 | bytes 25190400 | tf_op jit(solution)/shard_map/dot_general | solution.py:17
  176.0 8.5 %convolution_convert_fusion = bf16[768,3072]{1,0:T(8,128)(2,1)S(1)} fusion(bf16[1024,3072]{1,0:T(8,128)(2,1)} %get-tuple-element.330, f32[1024,768]{0,1:T(8,128)S(1)} %get-tuple-element.323, f32[768]{0:T(1024)S(1)} %copy-done.39, f32[768]{0:T(1024)S(1)} %convert_element_type.369, f32[1024]{0:T(1024)S(1)} %fusion.89, f32[1024]{0:T(1024)S(1)} %broadcast_multiply_fusion.1), kind=kOutput, calls=%fused_computation.9 | convolution fusion | flops 4838129664 | bytes 14170112 | tf_op jit(solution)/shard_map/dot_general | solution.py:303
  184.6 9.8 %multiply_reduce_fusion = (f32[768]{0:T(1024)}, f32[1024]{0:T(1024)S(1)}, f32[768]{0:T(1024)}, f32[1024,768]{0,1:T(8,128)S(1)}) fusion(f32[1024,768]{0,1:T(8,128)S(1)} %get-tuple-element.323, f32[1024]{0:T(1024)S(1)} %fusion.89, f32[1024]{0:T(1024)S(1)} %broadcast_multiply_fusion.1, f32[768]{0:T(1024)S(1)} %convert_element_type.369, ...), kind=kOutput, calls=%fused_computation.26 | convolution fusion | flops 4847563776 | bytes 22061056 | tf_op jit(solution)/shard_map/dot_general | solution.py:17
  206.6 47.3 %attend_back.1 = (bf16[3,1024,768]{2,1,0:T(8,128)(2,1)}, bf16[12,4,1024,256]{3,2,1,0:T(8,128)(2,1)}, f32[6,8,2048]{2,1,0:T(8,128)S(1)}) custom-call(bf16[1024,2304]{1,0:T(8,128)(2,1)} %add_convert_fusion.1.q_ref.k_ref.v_ref, bf16[1024,2304]{1,0:T(8,128)(2,1)} %add_convert_fusion.1.q_ref.k_ref.v_ref, ...), custom_call_target="tpu_custom_call", output_to_operand_aliasing={{1}: (5, {})} | custom-call | flops 1000 | bytes 1000 | tf_op jit(solution)/shard_map/attend_back/pallas_call | solution.py:191
  253.9 4.6 fusion.15
  265.5 7.3 %add_convert_fusion.2 = bf16[1024,768]{0,1:T(8,128)(2,1)S(1)} fusion(f32[1024,768]{0,1:T(8,128)} %fusion.15, f32[1024,768]{0,1:T(8,128)} %fusion.13, f32[1024,768]{0,1:T(8,128)} %copy-done.5, bf16[3,1024,768]{2,1,0:T(8,128)(2,1)} %get-tuple-element.36, f32[1024]{0:T(1024)S(1)} %negate_multiply_fusion, bf16[768,2304]{1,0:T(8,128)(2,1)} %param.24), kind=kOutput, calls=%fused_computation.29 | convolution fusion | flops 1211891712 | bytes 13766656 | tf_op jit(solution)/shard_map/dot_general | solution.py:17
  281.1 15.0 %bucket_sums.4 = f32[64,192]{1,0:T(8,128)S(1)} custom-call(bf16[12,4,1024,256]{3,2,1,0:T(8,128)(2,1)} %get-tuple-element.44.ds_ref, s32[2,1024]{1,0:T(2,128)S(1)} %pad_add_fusion.cq_ref.crow_ref, s32[2,1024,128]{2,1,0:T(8,128)S(1)} %copy-done.3), custom_call_target="tpu_custom_call" | custom-call | flops 15000000512 | bytes 1000 | tf_op jit(solution)/shard_map/bucket_sums/pallas_call | solution.py:240
  296.9 5.3 %fusion.3 = bf16[3,384,768]{2,1,0:T(8,128)(2,1)S(1)} fusion(bf16[3,384,768]{2,1,0:T(8,128)(2,1)} %collective-permute-done.4, bf16[3,1024,768]{2,1,0:T(8,128)(2,1)} %get-tuple-element.36, bf16[1024,768]{0,1:T(8,128)(2,1)} %copy-done.22, s32[]{:T(128)S(6)} %select_n.353), kind=kOutput, calls=%fused_computation.23 | convolution fusion | flops 1814593536 | bytes 9043972 | tf_op jit(solution)/shard_map/td,...tf->...df/dot_general | solution.py:356
  307.6 15.7 %collective-permute-done.5 = bf16[8,40,768]{2,1,0:T(8,128)(2,1)S(1)} collective-permute-done((bf16[8,40,768]{2,1,0:T(8,128)(2,1)S(1)}, bf16[8,40,768]{2,1,0:T(8,128)(2,1)S(1)}, u32[]{:S(2)}, u32[]{:S(2)}) %collective-permute-start.5) | collective-permute-done | bytes 491552 | tf_op jit(solution)/shard_map/ppermute | solution.py:351
  323.5 9.4 %collective-permute-done.7 = bf16[8,40,768]{2,1,0:T(8,128)(2,1)S(1)} collective-permute-done((bf16[8,40,768]{2,1,0:T(8,128)(2,1)S(1)}, bf16[8,40,768]{2,1,0:T(8,128)(2,1)S(1)}, u32[]{:S(2)}, u32[]{:S(2)}) %collective-permute-start.7) | collective-permute-done | bytes 491552 | tf_op jit(solution)/shard_map/ppermute | solution.py:351
  335.1 15.1 %bucket_sums.5 = f32[64,192]{1,0:T(8,128)S(1)} custom-call(bf16[12,4,1024,256]{3,2,1,0:T(8,128)(2,1)} %get-tuple-element.44.ds_ref, s32[2,1024]{1,0:T(2,128)S(1)} %pad_add_fusion.cq_ref.crow_ref, s32[2,1024,128]{2,1,0:T(8,128)S(1)} %copy-done.3), custom_call_target="tpu_custom_call" | custom-call | flops 15000000512 | bytes 1000 | tf_op jit(solution)/shard_map/bucket_sums/pallas_call | solution.py:240
  352.6 15.0 %bucket_sums.6 = f32[64,192]{1,0:T(8,128)S(1)} custom-call(bf16[12,4,1024,256]{3,2,1,0:T(8,128)(2,1)} %get-tuple-element.44.ds_ref, s32[2,1024]{1,0:T(2,128)S(1)} %pad_add_fusion.cq_ref.crow_ref, s32[2,1024,128]{2,1,0:T(8,128)S(1)} %copy-done.3), custom_call_target="tpu_custom_call" | custom-call | flops 15000000512 | bytes 1000 | tf_op jit(solution)/shard_map/bucket_sums/pallas_call | solution.py:240
  369.0 15.0 %bucket_sums.7 = f32[64,192]{1,0:T(8,128)S(1)} custom-call(bf16[12,4,1024,256]{3,2,1,0:T(8,128)(2,1)} %get-tuple-element.44.ds_ref, s32[2,1024]{1,0:T(2,128)S(1)} %pad_add_fusion.cq_ref.crow_ref, s32[2,1024,128]{2,1,0:T(8,128)S(1)} %copy-done.3), custom_call_target="tpu_custom_call" | custom-call | flops 15000000512 | bytes 1000 | tf_op jit(solution)/shard_map/bucket_sums/pallas_call | solution.py:240
  425.5 9.6 %collective-permute-done.16 = bf16[8,40,768]{2,1,0:T(8,128)(2,1)S(1)} collective-permute-done((bf16[8,40,768]{2,1,0:T(8,128)(2,1)S(1)}, bf16[8,40,768]{2,1,0:T(8,128)(2,1)S(1)}, u32[]{:S(2)}, u32[]{:S(2)}) %collective-permute-start.16) | collective-permute-done | bytes 491552 | tf_op jit(solution)/shard_map/ppermute | solution.py:351
  441.0 6.1 %collective-permute-done.27 = f32[88,128]{1,0:T(8,128)S(1)} collective-permute-done((f32[88,128]{1,0:T(8,128)S(1)}, f32[88,128]{1,0:T(8,128)S(1)}, u32[]{:S(2)}, u32[]{:S(2)}) %collective-permute-start.27) | collective-permute-done | bytes 45088 | tf_op jit(solution)/shard_map/ppermute | solution.py:351
  467.2 27.3 %all-reduce.4.cloned.1.call-done = bf16[6912,768]{1,0:T(8,128)(2,1)} async-done(((bf16[6912,768]{1,0:T(8,128)(2,1)}), bf16[6912,768]{1,0:T(8,128)(2,1)}) %all-reduce.4.cloned.1.call-update) | async-done | bytes 10616848 | tf_op jit(solution)/shard_map/psum | solution.py:462
  494.5 4.6 fusion.125
  499.1 4.3 maximum_convert_fusion
  503.4 6.9 %slice_convert_fusion = f32[3072,768]{1,0:T(8,128)} fusion(bf16[6912,768]{1,0:T(8,128)(2,1)} %all-reduce.4.cloned.1.call-done), kind=kLoop, calls=%fused_computation.17 | loop fusion | flops 2359296 | bytes 14155776 | tf_op jit(solution)/shard_map/convert_element_type | solution.py:501
  (326 shorter events, 155.2 us)
Async XLA Ops:
  7.2 487.3 %all-reduce.4.cloned.1.call-start = ((), (), s32[]{:S(2)}) async-start(), calls=%async_computation | async-start | bytes 21233664 | tf_op jit(solution)/shard_map/psum | solution.py:462
  10.4 30.8 %collective-permute-start = (bf16[512,768]{0,1:T(8,128)(2,1)}, bf16[512,768]{0,1:T(8,128)(2,1)}, u32[]{:S(2)}, u32[]{:S(2)}) collective-permute-start(bf16[512,768]{0,1:T(8,128)(2,1)} %select_bitcast_fusion.5), channel_id=1, source_target_pairs={{0,1},{1,0},{2,3},{3,2},{4,5},{5,4},{6,7},{7,6},{8,9},{9,8},{10,11... | collective-permute-start | bytes 2359304 | tf_op jit(solution)/shard_map/ppermute | solution.py:324
  17.4 125.1 %collective-permute-start.2 = (bf16[512,768]{0,1:T(8,128)(2,1)}, bf16[512,768]{0,1:T(8,128)(2,1)}, u32[]{:S(2)}, u32[]{:S(2)}) collective-permute-start(bf16[512,768]{0,1:T(8,128)(2,1)} %select_bitcast_fusion.2), channel_id=1, source_target_pairs={{0,1},{1,0},{2,3},{3,2},{4,5},{5,4},{6,7},{7,6},{8,9},{9,8},{10,11... | collective-permute-start | bytes 2359304 | tf_op jit(solution)/shard_map/ppermute | solution.py:324
  264.7 40.6 %collective-permute-start.1 = (bf16[512,768]{0,1:T(8,128)(2,1)}, bf16[512,768]{0,1:T(8,128)(2,1)}, u32[]{:S(2)}, u32[]{:S(2)}) collective-permute-start(bf16[512,768]{0,1:T(8,128)(2,1)} %broadcast_select_fusion.6), channel_id=1, source_target_pairs={{0,1},{1,0},{2,3},{3,2},{4,5},{5,4},{6,7},{7,6},{8,9},{9,8},{10,11... | collective-permute-start | bytes 2359304 | tf_op jit(solution)/shard_map/ppermute | solution.py:332
  273.9 165.5 %collective-permute-start.3 = (bf16[512,768]{0,1:T(8,128)(2,1)}, bf16[512,768]{0,1:T(8,128)(2,1)}, u32[]{:S(2)}, u32[]{:S(2)}) collective-permute-start(bf16[512,768]{0,1:T(8,128)(2,1)} %broadcast_select_fusion.4), channel_id=1, source_target_pairs={{0,1},{1,0},{2,3},{3,2},{4,5},{5,4},{6,7},{7,6},{8,9},{9,8},{10,11... | collective-permute-start | bytes 2359304 | tf_op jit(solution)/shard_map/ppermute | solution.py:332
  278.0 18.8 %collective-permute-start.4 = (bf16[3,384,768]{2,1,0:T(8,128)(2,1)}, bf16[3,384,768]{2,1,0:T(8,128)(2,1)}, u32[]{:S(2)}, u32[]{:S(2)}) collective-permute-start(bf16[3,384,768]{2,1,0:T(8,128)(2,1)} %convert_bitcast_fusion), channel_id=1, source_target_pairs={{0,2},{2,0},{4,6},{6,4},{8,10},{10,8},{12,14},{14,12},{16,18},{18,... | collective-permute-start | bytes 5308424 | tf_op jit(solution)/shard_map/ppermute | solution.py:351
  278.7 17.6 %collective-permute-start.6 = (bf16[64,768]{1,0:T(8,128)(2,1)S(1)}, bf16[64,768]{1,0:T(8,128)(2,1)S(1)}, u32[]{:S(2)}, u32[]{:S(2)}) collective-permute-start(bf16[64,768]{1,0:T(8,128)(2,1)S(1)} %convolution_convert_fusion.4), channel_id=1, source_target_pairs={{0,2},{2,0},{4,6},{6,4},{8,10},{10,8},{12,14},{14,12},{16,18},{18,... | collective-permute-start | bytes 294920 | tf_op jit(solution)/shard_map/ppermute | solution.py:351
  302.4 20.9 %collective-permute-start.5 = (bf16[8,40,768]{2,1,0:T(8,128)(2,1)S(1)}, bf16[8,40,768]{2,1,0:T(8,128)(2,1)S(1)}, u32[]{:S(2)}, u32[]{:S(2)}) collective-permute-start(bf16[8,40,768]{2,1,0:T(8,128)(2,1)S(1)} %fusion.55), channel_id=1, source_target_pairs={{0,4},{2,6},{4,0},{6,2},{8,12},{10,14},{12,8},{14,10},{16,20},{18,... | collective-permute-start | bytes 1474568 | tf_op jit(solution)/shard_map/ppermute | solution.py:351
  304.1 28.8 %collective-permute-start.7 = (bf16[8,40,768]{2,1,0:T(8,128)(2,1)S(1)}, bf16[8,40,768]{2,1,0:T(8,128)(2,1)S(1)}, u32[]{:S(2)}, u32[]{:S(2)}) collective-permute-start(bf16[8,40,768]{2,1,0:T(8,128)(2,1)S(1)} %constant_dynamic-slice_fusion.10), channel_id=1, source_target_pairs={{0,1},{1,0},{2,3},{3,2},{4,5},{5,4},{6,7},{7,6},{8,9},{9,8},{10,11... | collective-permute-start | bytes 1474568 | tf_op jit(solution)/shard_map/ppermute | solution.py:351
  333.1 17.2 %collective-permute-start.8 = (bf16[4,40,768]{2,1,0:T(8,128)(2,1)S(1)}, bf16[4,40,768]{2,1,0:T(8,128)(2,1)S(1)}, u32[]{:S(2)}, u32[]{:S(2)}) collective-permute-start(bf16[4,40,768]{2,1,0:T(8,128)(2,1)S(1)} %constant_dynamic-slice_fusion.9), channel_id=1, source_target_pairs={{0,1},{1,0},{2,3},{3,2},{4,5},{5,4},{6,7},{7,6},{8,9},{9,8},{10,11... | collective-permute-start | bytes 737288 | tf_op jit(solution)/shard_map/ppermute | solution.py:351
  333.5 16.8 %collective-permute-start.9 = (bf16[4,40,768]{2,1,0:T(8,128)(2,1)S(1)}, bf16[4,40,768]{2,1,0:T(8,128)(2,1)S(1)}, u32[]{:S(2)}, u32[]{:S(2)}) collective-permute-start(bf16[4,40,768]{2,1,0:T(8,128)(2,1)S(1)} %constant_dynamic-slice_fusion.8), channel_id=1, source_target_pairs={{0,4},{2,6},{4,0},{6,2},{8,12},{10,14},{12,8},{14,10},{16,20},{18,... | collective-permute-start | bytes 737288 | tf_op jit(solution)/shard_map/ppermute | solution.py:351
  350.4 17.2 %collective-permute-start.10 = (bf16[2,40,768]{2,1,0:T(8,128)(2,1)S(1)}, bf16[2,40,768]{2,1,0:T(8,128)(2,1)S(1)}, u32[]{:S(2)}, u32[]{:S(2)}) collective-permute-start(bf16[2,40,768]{2,1,0:T(8,128)(2,1)S(1)} %constant_dynamic-slice_fusion.7), channel_id=1, source_target_pairs={{0,8},{2,10},{4,12},{6,14},{8,0},{10,2},{12,4},{14,6},{16,24},{18,... | collective-permute-start | bytes 368648 | tf_op jit(solution)/shard_map/ppermute | solution.py:351
  352.1 16.2 %collective-permute-start.11 = (bf16[2,40,768]{2,1,0:T(8,128)(2,1)S(1)}, bf16[2,40,768]{2,1,0:T(8,128)(2,1)S(1)}, u32[]{:S(2)}, u32[]{:S(2)}) collective-permute-start(bf16[2,40,768]{2,1,0:T(8,128)(2,1)S(1)} %constant_dynamic-slice_fusion.6), channel_id=1, source_target_pairs={{0,8},{2,10},{4,12},{6,14},{8,0},{10,2},{12,4},{14,6},{16,24},{18,... | collective-permute-start | bytes 368648 | tf_op jit(solution)/shard_map/ppermute | solution.py:351
  393.7 8.1 %collective-permute-start.17 = (bf16[1,40,768]{2,1,0:T(8,128)(2,1)S(1)}, bf16[1,40,768]{2,1,0:T(8,128)(2,1)S(1)}, u32[]{:S(2)}, u32[]{:S(2)}) collective-permute-start(bf16[1,40,768]{2,1,0:T(8,128)(2,1)S(1)} %constant_dynamic-slice_fusion.4), channel_id=1, source_target_pairs={{0,16},{2,18},{4,20},{6,22},{8,24},{10,26},{12,28},{14,30},{16,0},... | collective-permute-start | bytes 184328 | tf_op jit(solution)/shard_map/ppermute | solution.py:351
  394.9 30.3 %collective-permute-start.25 = (f32[88,128]{1,0:T(8,128)S(1)}, f32[88,128]{1,0:T(8,128)S(1)}, u32[]{:S(2)}, u32[]{:S(2)}) collective-permute-start(f32[88,128]{1,0:T(8,128)S(1)} %fusion.119), channel_id=1, source_target_pairs={{0,4},{2,6},{4,0},{6,2},{8,12},{10,14},{12,8},{14,10},{16,20},{18,... | collective-permute-start | bytes 135176 | tf_op jit(solution)/shard_map/ppermute | solution.py:351
  403.5 8.1 %collective-permute-start.14 = (bf16[2,40,768]{2,1,0:T(8,128)(2,1)S(1)}, bf16[2,40,768]{2,1,0:T(8,128)(2,1)S(1)}, u32[]{:S(2)}, u32[]{:S(2)}) collective-permute-start(bf16[2,40,768]{2,1,0:T(8,128)(2,1)S(1)} %pad_maximum_fusion.14), channel_id=1, source_target_pairs={{0,8},{2,10},{4,12},{6,14},{8,0},{10,2},{12,4},{14,6},{16,24},{18,... | collective-permute-start | bytes 368648 | tf_op jit(solution)/shard_map/ppermute | solution.py:351
  407.9 8.2 %collective-permute-start.19 = (bf16[2,40,768]{2,1,0:T(8,128)(2,1)S(1)}, bf16[2,40,768]{2,1,0:T(8,128)(2,1)S(1)}, u32[]{:S(2)}, u32[]{:S(2)}) collective-permute-start(bf16[2,40,768]{2,1,0:T(8,128)(2,1)S(1)} %pad_maximum_fusion.15), channel_id=1, source_target_pairs={{0,8},{2,10},{4,12},{6,14},{8,0},{10,2},{12,4},{14,6},{16,24},{18,... | collective-permute-start | bytes 368648 | tf_op jit(solution)/shard_map/ppermute | solution.py:351
  411.6 9.9 %collective-permute-start.15 = (bf16[4,40,768]{2,1,0:T(8,128)(2,1)S(1)}, bf16[4,40,768]{2,1,0:T(8,128)(2,1)S(1)}, u32[]{:S(2)}, u32[]{:S(2)}) collective-permute-start(bf16[4,40,768]{2,1,0:T(8,128)(2,1)S(1)} %pad_maximum_fusion.12), channel_id=1, source_target_pairs={{0,1},{1,0},{2,3},{3,2},{4,5},{5,4},{6,7},{7,6},{8,9},{9,8},{10,11... | collective-permute-start | bytes 737288 | tf_op jit(solution)/shard_map/ppermute | solution.py:351
  416.1 8.9 %collective-permute-start.20 = (bf16[4,40,768]{2,1,0:T(8,128)(2,1)S(1)}, bf16[4,40,768]{2,1,0:T(8,128)(2,1)S(1)}, u32[]{:S(2)}, u32[]{:S(2)}) collective-permute-start(bf16[4,40,768]{2,1,0:T(8,128)(2,1)S(1)} %pad_maximum_fusion.13), channel_id=1, source_target_pairs={{0,4},{2,6},{4,0},{6,2},{8,12},{10,14},{12,8},{14,10},{16,20},{18,... | collective-permute-start | bytes 737288 | tf_op jit(solution)/shard_map/ppermute | solution.py:351
  421.6 13.5 %collective-permute-start.16 = (bf16[8,40,768]{2,1,0:T(8,128)(2,1)S(1)}, bf16[8,40,768]{2,1,0:T(8,128)(2,1)S(1)}, u32[]{:S(2)}, u32[]{:S(2)}) collective-permute-start(bf16[8,40,768]{2,1,0:T(8,128)(2,1)S(1)} %pad_maximum_fusion.9), channel_id=1, source_target_pairs={{0,4},{2,6},{4,0},{6,2},{8,12},{10,14},{12,8},{14,10},{16,20},{18,... | collective-permute-start | bytes 1474568 | tf_op jit(solution)/shard_map/ppermute | solution.py:351
  425.1 12.5 %collective-permute-start.21 = (bf16[8,40,768]{2,1,0:T(8,128)(2,1)S(1)}, bf16[8,40,768]{2,1,0:T(8,128)(2,1)S(1)}, u32[]{:S(2)}, u32[]{:S(2)}) collective-permute-start(bf16[8,40,768]{2,1,0:T(8,128)(2,1)S(1)} %pad_maximum_fusion.10), channel_id=1, source_target_pairs={{0,1},{1,0},{2,3},{3,2},{4,5},{5,4},{6,7},{7,6},{8,9},{9,8},{10,11... | collective-permute-start | bytes 1474568 | tf_op jit(solution)/shard_map/ppermute | solution.py:351
  425.2 15.6 %collective-permute-start.26 = (f32[88,128]{1,0:T(8,128)S(1)}, f32[88,128]{1,0:T(8,128)S(1)}, u32[]{:S(2)}, u32[]{:S(2)}) collective-permute-start(f32[88,128]{1,0:T(8,128)S(1)} %fusion.158), channel_id=1, source_target_pairs={{0,8},{2,10},{4,12},{6,14},{8,0},{10,2},{12,4},{14,6},{16,24},{18,... | collective-permute-start | bytes 135176 | tf_op jit(solution)/shard_map/ppermute | solution.py:351
  436.2 19.4 %collective-permute-start.22 = (bf16[16,40,768]{2,1,0:T(8,128)(2,1)}, bf16[16,40,768]{2,1,0:T(8,128)(2,1)}, u32[]{:S(2)}, u32[]{:S(2)}) collective-permute-start(bf16[16,40,768]{2,1,0:T(8,128)(2,1)} %pad_maximum_fusion.7), channel_id=1, source_target_pairs={{0,2},{2,0},{4,6},{6,4},{8,10},{10,8},{12,14},{14,12},{16,18},{18,... | collective-permute-start | bytes 2949128 | tf_op jit(solution)/shard_map/ppermute | solution.py:351
  439.5 17.4 %collective-permute-start.23 = (bf16[16,40,768]{2,1,0:T(8,128)(2,1)}, bf16[16,40,768]{2,1,0:T(8,128)(2,1)}, u32[]{:S(2)}, u32[]{:S(2)}) collective-permute-start(bf16[16,40,768]{2,1,0:T(8,128)(2,1)} %pad_maximum_fusion.8), channel_id=1, source_target_pairs={{0,2},{2,0},{4,6},{6,4},{8,10},{10,8},{12,14},{14,12},{16,18},{18,... | collective-permute-start | bytes 2949128 | tf_op jit(solution)/shard_map/ppermute | solution.py:351
  (60 other events, 685.9 us)
Sparse Core Ops, SparseCore 0:
  262.5 231.9 all-reduce.3

commit v3 on v2

--- a/solution.py
+++ b/solution.py
@@ -11,6 +11,7 @@
 LOG2E=math.log2(math.e)
 HISTF=15*10**9
 IB=256
+FC=256
 JC=128
 
 def nt(a,b):
@@ -51,7 +52,7 @@
             rows=slice(m*JC,(m+1)*JC)
             for c in range(IB//128):
                 for kind in range(2):
-                    idx_ref[kind,b,rows,c*128:(c+1)*128]=far_lane(ck_ref[kind,rows,:]-cq_ref[kind:kind+1,c*128:(c+1)*128])
+                    idx_ref[kind,b,rows,c*128:(c+1)*128]=far_lane(ck_ref[kind,rows,:]-cq_ref[kind:kind+1,c*128:(c+1)*128])+64*kind
     @pl.when(t==0)
     def _():
         key=lax.broadcasted_iota(jnp.int32,(full,128),0); lane=lax.broadcasted_iota(jnp.int32,(full,128),1)
@@ -71,31 +72,31 @@
     def body(cur_ref,prev_ref):
         rowi=lax.broadcasted_iota(jnp.int32,(128,IB),0)
         qt=(q_ref[...]*jnp.asarray(0.125*UNIT,BF)).T
-        for h in range(2):
-            qh=jnp.where((rowi<64)==(h==0),qt,jnp.zeros_like(qt))
-            cur_ref[h]=nn(ka_ref[...],jnp.concatenate([qh,jnp.ones_like(qt)],axis=0))
+        qh=[jnp.concatenate([jnp.where((rowi<64)==(h==0),qt,jnp.zeros_like(qt)),jnp.ones_like(qt)],axis=0) for h in range(2)]
         mx=[top_ref[h:h+1,:]*scale for h in range(2)]
         top=[jnp.full((8,IB),-jnp.inf,F32)]*2
-        for m in range(nj):
-            rows=slice(m*JC,(m+1)*JC)
+        lhs=[jnp.concatenate([vt_ref[64*h:64*h+64,:],vt_ref[128:144,:]],axis=0) for h in range(2)]
+        acc=[jnp.zeros((80,IB),F32)]*2
+        for m in range(full//FC):
+            rows=slice(m*FC,(m+1)*FC)
+            raw=[nn(ka_ref[rows,:],qh[h]) for h in range(2)]
             for h in range(2):
-                p_ref[h,0,rows,:]=jnp.exp2(prev_ref[h,rows,:]*scale-mx[h]).astype(BF)
-            x=wide_ref[:,pl.ds(pl.multiple_of(b*IB+(full-m*JC),128),IB)]
-            x=x+jnp.concatenate([lookup(tab_ref[0,1],idx_ref[0,b,rows,c*128:(c+1)*128])+lookup(tab_ref[0,2],idx_ref[1,b,rows,c*128:(c+1)*128]) for c in range(IB//128)],axis=1)
+                p=jnp.exp2(prev_ref[h,rows,:]*scale-mx[h]).astype(BF)
+                p_ref[h,0,rows,:]=p
+                acc[h]=acc[h]+nn(lhs[h][:,rows],p)
+            near=jnp.concatenate([wide_ref[:,pl.ds(pl.multiple_of(b*IB+(full-w*JC),128),IB)] for w in range(m*FC//JC,(m+1)*FC//JC)],axis=0)
+            x=near+jnp.concatenate([lookup(tab_ref[0,1],idx_ref[0,b,rows,c*128:(c+1)*128])+lookup(tab_ref[0,1],idx_ref[1,b,rows,c*128:(c+1)*128]) for c in range(IB//128)],axis=1)
             for h in range(2):
                 y=(x&0xffff) if h==0 else lax.shift_right_logical(x,16)
-                s=cur_ref[h,rows,:]+y.astype(F32)
+                s=raw[h]+y.astype(F32)
                 cur_ref[h,rows,:]=s
-                top[h]=jnp.maximum(top[h],jnp.max(s.reshape(JC//8,8,IB),axis=0))
+                top[h]=jnp.maximum(top[h],jnp.max(s.reshape(FC//8,8,IB),axis=0))
+        outs=[]
         for h in range(2):
             top_ref[h:h+1,:]=jnp.max(top[h],axis=0,keepdims=True)
-        outs=[]
-        for h in range(2):
-            lhs=jnp.concatenate([vt_ref[64*h:64*h+64,:],vt_ref[128:144,:]],axis=0)
-            r=nn(lhs,p_ref[h,0])
-            inv=1.0/r[64:65]
+            inv=1.0/acc[h][64:65]
             linv_ref[0,h:h+1,:]=inv
-            outs.append(r[:64]*inv)
+            outs.append(acc[h][:64]*inv)
         ctx_ref[...]=jnp.concatenate(outs,axis=0).T.astype(BF)
     @pl.when(t%2==0)
     def _(): body(s0_ref,s1_ref)
@@ -114,7 +115,7 @@
           pl.BlockSpec((full,128),lambda t:(0,vcol+was(t)//nb)),
           pl.BlockSpec((2,IB),lambda t:(0,now(t)%nb)),
           pl.BlockSpec((2,full,128),lambda t:(0,0,0)),
-          pl.BlockSpec((1,3,8,128),lambda t:(now(t)//nb,0,0,0)),
+          pl.BlockSpec((1,2,8,128),lambda t:(now(t)//nb,0,0,0)),
           pl.BlockSpec((128,2*full),lambda t:(0,0))],
         out_specs=[pl.BlockSpec((IB,128),lambda t:(was(t)%nb,was(t)//nb)),
           pl.BlockSpec((2,1,full,IB),lambda t:(was(t)//nb,was(t)%nb,0,0)),
@@ -259,11 +260,12 @@
     return np_level(np.where((lane//32)%2==1,a,-a),FAR_EDGES)
 def tables(bias_tables):
     near=np.arange(128)%32; far=lanes_of()
-    hot=np.stack([near,far,far])[:,:,None]==np.arange(32)
-    t=jnp.einsum('klb,kbh->hkl',jnp.asarray(hot,BF),bias_tables,preferred_element_type=F32)
+    spot=np.arange(96)
+    hot=np.stack([spot==near[:,None],spot==(np.where(np.arange(128)<64,32,64)+far)[:,None]])
+    t=jnp.einsum('klb,bh->hkl',jnp.asarray(hot,BF),bias_tables.reshape(96,-1),preferred_element_type=F32)
     t=jnp.round((t+4.0)*UNIT).astype(jnp.int32)
     t=t[0::2]+(t[1::2]<<16)
-    return jnp.broadcast_to(t[:,:,None,:],(t.shape[0],3,8,128))
+    return jnp.broadcast_to(t[:,:,None,:],(t.shape[0],2,8,128))
 def near_idx(full):
     r=lax.broadcasted_iota(jnp.int32,(128,2*full),0); u=lax.broadcasted_iota(jnp.int32,(128,2*full),1)
     return level(r+full-u,NEAR_EDGES)
@@ -371,20 +373,21 @@
         came = self.move(x, step)
         return jnp.concatenate([jnp.where(mine == 0, x, came), jnp.where(mine == 0, came, x)], axis=0)
 
-    def total(self, parts, between=None, tie=None):
+    def total(self, parts, between=None):
         rows = [p.shape[0] // self.pieces for p in parts]
         x = jnp.concatenate([p.reshape(self.pieces, r, p.shape[1]) for p, r in zip(parts, rows)], axis=1)
         count = x.shape[1]
         x = jnp.pad(x, ((0, 0), (0, -count % 16), (0, 0)))
         cut = x.shape[1] // 2
         lanes = [x[:, :cut], x[:, cut:]]
-        for i in range(len(self.orders[0])):
-            if between and i < 4:
-                lanes = between(i, 4, lanes)
+        hold = lambda i, lanes: between(i, lanes) if between and i < 7 else lanes
+        lanes = hold(0, lanes)
+        stages = len(self.orders[0])
+        for i in range(stages):
+            lanes = hold(1 + i, lanes)
             lanes = [self.scatter(x, order[i]) for x, order in zip(lanes, self.orders)]
-        for i in reversed(range(len(self.orders[0]))):
-            if tie and i == TIE:
-                lanes = tie(lanes)
+        for i in reversed(range(stages)):
+            lanes = hold(2 * stages - i, lanes) if stages == 4 else lanes
             lanes = [self.gather(x, order[i]) for x, order in zip(lanes, self.orders)]
         came = [self.move(x, self.core) for x in lanes]
         mine = self.mine(self.core)
@@ -424,15 +427,18 @@
     box = lax.dynamic_index_in_dim(boxes, me, 1, keepdims=False)
     length = lax.dynamic_slice_in_dim(lengths, me, 1, 0)
     feats = fourier(box).astype(BF)
+    crow = jnp.stack([box[0] + box[2], box[1] + box[3]])
+    ccol = jnp.broadcast_to(crow[:, :, None], (2, full, 128))
+    packed = tables(bias_tables)
+    skew = near_idx(full)
+    bias3 = jnp.concatenate([qv_bias[0], jnp.zeros_like(qv_bias[0]), qv_bias[1]]).astype(F32)
+    hidden, feats, ccol, packed, skew, bias3 = lax.optimization_barrier((hidden, feats, ccol, packed, skew, bias3))
     start = hidden.astype(F32) + nn(feats, layout_weight)
     start_low = start.astype(BF)
-    bias3 = jnp.concatenate([qv_bias[0], jnp.zeros_like(qv_bias[0]), qv_bias[1]]).astype(F32)
     qkv = (nn(start_low, qkv_weight) + bias3).astype(BF)
-    crow = jnp.stack([box[0] + box[2], box[1] + box[3]])
-    ccol = jnp.broadcast_to(crow[:, :, None], (2, full, 128))
     pairs = heads // 2
     context, probs, linv = fwd_attention(
-        qkv, qkv, qkv, 0, pairs, 2 * pairs, length, crow, ccol, tables(bias_tables), near_idx(full), heads)
+        qkv, qkv, qkv, 0, pairs, 2 * pairs, length, crow, ccol, packed, skew, heads)
     upstream = swap(cotangent, me).astype(F32)
     attended = nn(context, out_weight) + out_bias.astype(F32)
     mid, norm1_pull = jax.vjp(layer_norm, start + attended, norm1_gain.astype(F32), norm1_bias.astype(F32))
@@ -440,7 +446,7 @@
     hidden_pre = nn(mid_low, ff_in) + ff_in_bias.astype(F32)
     activated, slope = gelu_pair(hidden_pre)
     activated = activated.astype(BF)
-    slope = slope.astype(BF)
+    activated, slope = lax.optimization_barrier((activated, slope.astype(BF)))
     branch = nn(activated, ff_out) + ff_out_bias.astype(F32)
     result, norm2_pull = jax.vjp(layer_norm, mid + branch, norm2_gain.astype(F32), norm2_bias.astype(F32))
     layer_out = unswap(result.astype(BF), me)
@@ -450,15 +456,15 @@
     ffoutb_grad = jnp.sum(grad_ff.astype(F32), axis=0)
     grad_inner = (nt(grad_ff, ff_out) * slope.astype(F32)).astype(BF)
     ffin_part = inner(mid_low, grad_inner).astype(BF)
-    ffinb_grad = jnp.sum(grad_inner.astype(F32), axis=0)
+    ffinb_grad = nn(jnp.ones((8, full), BF), grad_inner)[0]
     grad_mid = grad_r2 + nt(grad_inner, ff_in)
     grad_r1, gain1_grad, shift1_grad = norm1_pull(grad_mid)
     grad_att = grad_r1.astype(BF)
     outw_part = inner(context, grad_att).astype(BF)
     outb_grad = jnp.sum(grad_att.astype(F32), axis=0)
     grad_context = nt(grad_att, out_weight).astype(BF)
-    early = jnp.concatenate([ffout_part] + [ffin_part[:, c * width:(c + 1) * width] for c in range(ffin_part.shape[1] // width)] + [outw_part], axis=0)
-    grad_context = lax.optimization_barrier((early, grad_context))[1]
+    early = (ffout_part, ffin_part, outw_part)
+    grad_context = lax.optimization_barrier((*early, grad_context))[-1]
     early = lax.psum(early, BOTH)
     grad3, gscores, diag = bwd_attention(
         qkv, qkv, qkv, 0, pairs, 2 * pairs, grad_context, context, probs, linv, heads)
@@ -467,23 +473,20 @@
     grad_start = (grad_r1 + sum(nt(grad3[c], qkv_weight[:, c * width:(c + 1) * width]) for c in range(3))).astype(BF)
     input_grad = unswap(grad_start, me)
     lay_part = route.product(feats, grad_start)
+    plan = [1, 2, 1, 1, 1, 1, 1]
     bucket_parts = []
 
-    def between(i, count, lanes):
+    def between(i, lanes):
         row = crow
         if i:
             row, *lanes = lax.optimization_barrier((crow, *lanes))
-        bucket_parts.append(hist(gscores, row, ccol, heads, dt=jnp.int16, part=i, parts=count))
+        for _ in range(plan[i]):
+            bucket_parts.append(hist(gscores, row, ccol, heads, dt=jnp.int16, part=len(bucket_parts), parts=sum(plan)))
         return lanes
 
-    held = [early]
-
-    def tie(lanes):
-        held[0], *lanes = lax.optimization_barrier((held[0], *lanes))
-        return lanes
-
-    groups = route.total([qkv_part[0], qkv_part[1], qkv_part[2], lay_part], between, tie)
-    early = held[0]
+    late = [qkv_part[0], qkv_part[1], qkv_part[2], lay_part]
+    groups = route.total(late, between)
+    assert len(bucket_parts) == sum(plan)
     sums = jnp.sum(sum(bucket_parts).reshape(2, 32, heads, 16), axis=3)
     offset = lax.broadcasted_iota(jnp.int32, (2 * full, 32), 0)
     bucket = lax.broadcasted_iota(jnp.int32, (2 * full, 32), 1)
@@ -497,10 +500,7 @@
     (ffinb_total, ffoutb_total, gain2_total, shift2_total, outb_total, gain1_total, shift1_total, qvb_total,
      table_total) = route.small([ffinb_grad, ffoutb_grad, gain2_grad, shift2_grad, outb_grad, gain1_grad, shift1_grad,
                                  qvb_grad, table_grad])
-    ff = ffin_part.shape[1]
-    ffout_total = early[:ff].astype(F32)
-    ffin_total = jnp.concatenate([early[ff + c * width:ff + (c + 1) * width] for c in range(ff // width)], axis=1).astype(F32)
-    outw_total = early[2 * ff:].astype(F32)
+    ffout_total, ffin_total, outw_total = (x.astype(F32) for x in early)
     return (layer_out, input_grad, lay_total, qkv_total, qvb_total, table_total, outw_total,
             outb_total, gain1_total, shift1_total, ffin_total, ffinb_total, ffout_total, ffoutb_total,
             gain2_total, shift2_total)

time: 522 us -> 487 us (0.933)
  waiting for transfers between devices: 86.7 us -> 58.1 us
  matrix products: 111 us -> 97.6 us
  starting transfers between devices: 28 us -> 35.6 us
  Pallas kernels: 169 us -> 175 us
    psum x1, waiting for transfers between devices: 27.3 us -> 0.01 us  [shards(): early = lax.psum(early, BOTH)]
    dot_general x6, matrix products: 46.1 us -> 31.1 us  [nt(): lax.dot_general(a, b, (((1,), (1,)), ((), ())), preferred_element_type=F32)]
    ppermute x25, starting transfers between devices: 22.3 us -> 29.6 us  [move(): lax.ppermute(x, axis, [(i, i ^ bit) for i in range(lax.axis_size(axis))])]
    pallas_call x4 -> x8, Pallas kernels: 60.2 us -> 66.6 us  [hist(): pl.pallas_call(functools.partial(hist_kernel, heads=heads, dt=dt), grid=(...]
    convert_element_type x2 -> x3, other arithmetic: 11.2 us -> 14.9 us  [shards(): ffout_total, ffin_total, outw_total = (x.astype(F32) for x in early)]
    dot_general x5 -> x6, matrix products: 34.6 us -> 35.8 us  [nn(): lax.dot_general(a, b, (((1,), (0,)), ((), ())), preferred_element_type=F32)]
    unnamed x129 -> x108, local copies, waits for them, and re-layouts: 21.2 us -> 20 us
  transfers between devices with their start and end apart: 30 -> 30, of which waited for: 13 -> 11; matrix products, arithmetic and copies ran while one was open for 23% -> 25% of each run, Pallas kernels for 24% -> 36%
where the time goes in v3:
time: 487 us; the launch traced here: 482 us
  Pallas kernels  175 us (36%)
  matrix products  97.6 us (20%)
  other arithmetic  64.4 us (13%)
  waiting for transfers between devices  58.1 us (12%)
  starting transfers between devices  35.6 us (7%)
  local copies, waits for them, and re-layouts  35.5 us (7%)
  between operations  15.6 us (3%)
    pallas_call x8, Pallas kernels, hist(): pl.pallas_call(functools.partial(hist_kernel, heads=heads, dt=dt), grid=(...  66.6 us
    pallas_call x1, Pallas kernels, fwd_attention(): pl.pallas_call(fwd_kernel, grid=(pairs * nb + 1,), in_specs=[pl.BlockSpec...  60.8 us
    ppermute x25, waiting for transfers between devices, move(): lax.ppermute(x, axis, [(i, i ^ bit) for i in range(lax.axis_size(axis))])  58.1 us
    pallas_call x1, Pallas kernels, bwd_attention(): pl.pallas_call(bwd_kernel, grid=(pairs, nb), in_specs=[pl.BlockSpec((IB,...  47.5 us
    dot_general x6, matrix products, nn(): lax.dot_general(a, b, (((1,), (0,)), ((), ())), preferred_element_type=F32)  35.8 us
    dot_general x6, matrix products, nt(): lax.dot_general(a, b, (((1,), (1,)), ((), ())), preferred_element_type=F32)  31.1 us
    ppermute x25, starting transfers between devices, move(): lax.ppermute(x, axis, [(i, i ^ bit) for i in range(lax.axis_size(axis))])  29.6 us
    unnamed x108, local copies, waits for them, and re-layouts  20 us
  transfers between devices with their start and end apart: 30, of which 11 were waited for; matrix products, arithmetic and copies ran while one was open for 25% of the time, Pallas kernels for 36%

profile of v3, /device:TPU:0, one launch (start us, length us, event | category | flops | bytes accessed | tf_op | source)
XLA Modules:
  0.0 481.8 jit_solution(5816763795451749932)
XLA Ops:
  47.5 5.6 %add_convert_fusion.1.q_ref.k_ref.v_ref = bf16[1024,2304]{1,0:T(8,128)(2,1)} fusion(bf16[1024,768]{0,1:T(8,128)(2,1)S(1)} %get-tuple-element.356, bf16[768,2304]{1,0:T(8,128)(2,1)S(1)} %copy-done.25, f32[2304]{0:T(1024)S(1)} %maximum_convert_fusion.2), kind=kOutput, calls=%fused_computation.7 | convolution fusion | flops 3628597248 | bytes 9839616 | tf_op jit(solution)/shard_map/dot_general | solution.py:20
  53.1 60.8 %attend.1 = (bf16[1024,768]{1,0:T(8,128)(2,1)S(1)}, bf16[12,4,1024,256]{3,2,1,0:T(8,128)(2,1)}, f32[6,8,1024]{2,1,0:T(8,128)S(1)}) custom-call(s32[1]{0:T(128)} %dynamic_slice.68.len_ref, bf16[1024,2304]{1,0:T(8,128)(2,1)} %add_convert_fusion.1.q_ref.k_ref.v_ref, bf16[1024,2304]{1,0:T(8,128)(2,1)} %add_convert_fusion.1.q_ref.k_ref.v_ref, ...), custom_call_target="tpu_custom_call" | custom-call | flops 1000 | bytes 1000 | tf_op jit(solution)/shard_map/attend/pallas_call | solution.py:110
  116.9 18.8 %add_convert_fusion = (bf16[1024,3072]{1,0:T(8,128)(2,1)}, bf16[1024,3072]{1,0:T(8,128)(2,1)}) fusion(f32[3072]{0:T(1024)S(1)} %copy-done.32, bf16[768,3072]{1,0:T(8,128)(2,1)S(1)} %bitcast.548, f32[1024,768]{0,1:T(8,128)S(1)} %get-tuple-element.359, f32[768]{0:T(1024)S(1)} %copy-done.34, f32[768]{0:T(1024)S(1)} %copy-done.30, f32[1024]{0:T(1024)S(1)} %fusion.85, ...), kind=kOutput, calls=%fused_computation.2 | convolution fusion | flops 4920705024 | bytes 20473856 | tf_op jit(solution)/shard_map/dot_general | solution.py:20
  135.7 8.0 %fusion.128 = (f32[1024]{0:T(1024)S(1)}, f32[1024,768]{0,1:T(8,128)S(1)}) fusion(f32[768]{0:T(1024)S(1)} %copy-done.35, bf16[1024,3072]{1,0:T(8,128)(2,1)} %get-tuple-element.56, bf16[3072,768]{1,0:T(8,128)(2,1)S(1)} %bitcast.546, f32[768]{0:T(1024)S(1)} %copy-done.34, f32[768]{0:T(1024)S(1)} %copy-done.30, f32[1024]{0:T(1024)S(1)} %fusion.85, ...), kind=kOutput, calls=%fused_computation.405 | convolution fusion | flops 4837342208 | bytes 17323008 | tf_op jit(solution)/shard_map/dot_general | solution.py:20
  150.6 6.9 %convolution_convert_fusion.1 = bf16[3072,768]{1,0:T(8,128)(2,1)} fusion(bf16[1024,3072]{1,0:T(8,128)(2,1)S(1)} %bitcast.550, bf16[1024,768]{0,1:T(8,128)(2,1)S(1)} %get-tuple-element.244), kind=kOutput, calls=%fused_computation.9 | convolution fusion | flops 4834197504 | bytes 12582912 | tf_op jit(solution)/shard_map/dot_general | solution.py:305
  157.5 8.7 %multiply_convert_fusion = bf16[1024,3072]{1,0:T(8,128)(2,1)S(1)} fusion(bf16[1024,3072]{1,0:T(8,128)(2,1)} %get-tuple-element.57, bf16[1024,768]{0,1:T(8,128)(2,1)S(1)} %get-tuple-element.244, bf16[3072,768]{1,0:T(8,128)(2,1)} %param.33), kind=kOutput, calls=%fused_computation.1 | convolution fusion | flops 4841275392 | bytes 18874368 | tf_op jit(solution)/shard_map/dot_general | solution.py:18
  166.2 8.9 %multiply_reduce_fusion = (f32[768]{0:T(1024)S(1)}, f32[1024]{0:T(1024)S(1)}, f32[768]{0:T(1024)S(1)}, f32[1024,768]{0,1:T(8,128)S(1)}) fusion(f32[1024,768]{0,1:T(8,128)S(1)} %get-tuple-element.359, f32[1024]{0:T(1024)S(1)} %fusion.85, f32[1024]{0:T(1024)S(1)} %broadcast_multiply_fusion.1, f32[768]{0:T(1024)S(1)} %copy-done.30, ...), kind=kOutput, calls=%fused_computation.22 | convolution fusion | flops 4847563776 | bytes 22061056 | tf_op jit(solution)/shard_map/dot_general | solution.py:18
  176.0 7.0 %convolution_convert_fusion = bf16[768,3072]{1,0:T(8,128)(2,1)} fusion(bf16[1024,3072]{1,0:T(8,128)(2,1)S(1)} %multiply_convert_fusion, f32[1024,768]{0,1:T(8,128)S(1)} %get-tuple-element.359, f32[768]{0:T(1024)S(1)} %copy-done.34, f32[768]{0:T(1024)S(1)} %copy-done.30, f32[1024]{0:T(1024)S(1)} %fusion.85, f32[1024]{0:T(1024)S(1)} %broadcast_multiply_fusion.1), kind=kOutput, calls=%fused_computation.8 | convolution fusion | flops 4838129664 | bytes 14170112 | tf_op jit(solution)/shard_map/dot_general | solution.py:305
  196.3 47.5 %attend_back.1 = (bf16[3,1024,768]{2,1,0:T(8,128)(2,1)}, bf16[12,4,1024,256]{3,2,1,0:T(8,128)(2,1)}, f32[6,8,2048]{2,1,0:T(8,128)S(1)}) custom-call(bf16[1024,2304]{1,0:T(8,128)(2,1)} %add_convert_fusion.1.q_ref.k_ref.v_ref, bf16[1024,2304]{1,0:T(8,128)(2,1)} %add_convert_fusion.1.q_ref.k_ref.v_ref, ...), custom_call_target="tpu_custom_call", output_to_operand_aliasing={{1}: (5, {})} | custom-call | flops 1000 | bytes 1000 | tf_op jit(solution)/shard_map/attend_back/pallas_call | solution.py:192
  256.4 6.0 %convert_bitcast_fusion = bf16[3,384,768]{2,1,0:T(8,128)(2,1)} fusion(bf16[3,1024,768]{2,1,0:T(8,128)(2,1)} %get-tuple-element.61, bf16[1024,768]{0,1:T(8,128)(2,1)} %copy-done.23, s32[]{:T(128)S(6)} %select_n.354), kind=kOutput, calls=%fused_computation.47 | convolution fusion | flops 1812824064 | bytes 7274500 | tf_op jit(solution)/shard_map/td,...tf->...df/dot_general | solution.py:358
  269.9 8.6 %bucket_sums.8 = f32[64,192]{1,0:T(8,128)S(1)} custom-call(bf16[12,4,1024,256]{3,2,1,0:T(8,128)(2,1)} %get-tuple-element.75.ds_ref, s32[2,1024]{1,0:T(2,128)S(1)} %pad_add_fusion.cq_ref.crow_ref, s32[2,1024,128]{2,1,0:T(8,128)S(1)} %broadcast_in_dim.16.ck_ref.ccol_ref), custom_call_target="tpu_custom_call" | custom-call | flops 15000000512 | bytes 1000 | tf_op jit(solution)/shard_map/bucket_sums/pallas_call | solution.py:241
  279.2 5.1 %fusion.2 = bf16[3,384,768]{2,1,0:T(8,128)(2,1)S(1)} fusion(bf16[3,384,768]{2,1,0:T(8,128)(2,1)} %collective-permute-done.4, bf16[3,1024,768]{2,1,0:T(8,128)(2,1)} %get-tuple-element.61, bf16[1024,768]{0,1:T(8,128)(2,1)} %copy-done.23, s32[]{:T(128)S(6)} %select_n.353), kind=kOutput, calls=%fused_computation.19 | convolution fusion | flops 1814593536 | bytes 9043972 | tf_op jit(solution)/shard_map/td,...tf->...df/dot_general | solution.py:358
  284.6 8.2 %bucket_sums.10 = f32[64,192]{1,0:T(8,128)S(1)} custom-call(bf16[12,4,1024,256]{3,2,1,0:T(8,128)(2,1)} %get-tuple-element.75.ds_ref, s32[2,1024]{1,0:T(2,128)S(1)} %pad_add_fusion.cq_ref.crow_ref, s32[2,1024,128]{2,1,0:T(8,128)S(1)} %broadcast_in_dim.16.ck_ref.ccol_ref), custom_call_target="tpu_custom_call" | custom-call | flops 15000000512 | bytes 1000 | tf_op jit(solution)/shard_map/bucket_sums/pallas_call | solution.py:241
  296.0 8.2 %bucket_sums.9 = f32[64,192]{1,0:T(8,128)S(1)} custom-call(bf16[12,4,1024,256]{3,2,1,0:T(8,128)(2,1)} %get-tuple-element.75.ds_ref, s32[2,1024]{1,0:T(2,128)S(1)} %pad_add_fusion.cq_ref.crow_ref, s32[2,1024,128]{2,1,0:T(8,128)S(1)} %broadcast_in_dim.16.ck_ref.ccol_ref), custom_call_target="tpu_custom_call" | custom-call | flops 15000000512 | bytes 1000 | tf_op jit(solution)/shard_map/bucket_sums/pallas_call | solution.py:241
  304.2 8.2 %collective-permute-done.7 = bf16[8,40,768]{2,1,0:T(8,128)(2,1)S(1)} collective-permute-done((bf16[8,40,768]{2,1,0:T(8,128)(2,1)S(1)}, bf16[8,40,768]{2,1,0:T(8,128)(2,1)S(1)}, u32[]{:S(2)}, u32[]{:S(2)}) %collective-permute-start.7) | collective-permute-done | bytes 491552 | tf_op jit(solution)/shard_map/ppermute | solution.py:353
  315.0 8.2 %bucket_sums.11 = f32[64,192]{1,0:T(8,128)S(1)} custom-call(bf16[12,4,1024,256]{3,2,1,0:T(8,128)(2,1)} %get-tuple-element.75.ds_ref, s32[2,1024]{1,0:T(2,128)S(1)} %pad_add_fusion.cq_ref.crow_ref, s32[2,1024,128]{2,1,0:T(8,128)S(1)} %broadcast_in_dim.16.ck_ref.ccol_ref), custom_call_target="tpu_custom_call" | custom-call | flops 15000000512 | bytes 1000 | tf_op jit(solution)/shard_map/bucket_sums/pallas_call | solution.py:241
  325.2 8.2 %bucket_sums.12 = f32[64,192]{1,0:T(8,128)S(1)} custom-call(bf16[12,4,1024,256]{3,2,1,0:T(8,128)(2,1)} %get-tuple-element.75.ds_ref, s32[2,1024]{1,0:T(2,128)S(1)} %pad_add_fusion.cq_ref.crow_ref, s32[2,1024,128]{2,1,0:T(8,128)S(1)} %broadcast_in_dim.16.ck_ref.ccol_ref), custom_call_target="tpu_custom_call" | custom-call | flops 15000000512 | bytes 1000 | tf_op jit(solution)/shard_map/bucket_sums/pallas_call | solution.py:241
  338.4 8.4 %bucket_sums.13 = f32[64,192]{1,0:T(8,128)S(1)} custom-call(bf16[12,4,1024,256]{3,2,1,0:T(8,128)(2,1)} %get-tuple-element.75.ds_ref, s32[2,1024]{1,0:T(2,128)S(1)} %pad_add_fusion.cq_ref.crow_ref, s32[2,1024,128]{2,1,0:T(8,128)S(1)} %broadcast_in_dim.16.ck_ref.ccol_ref), custom_call_target="tpu_custom_call" | custom-call | flops 15000000512 | bytes 1000 | tf_op jit(solution)/shard_map/bucket_sums/pallas_call | solution.py:241
  349.8 7.4 %collective-permute-done.13 = bf16[1,40,768]{2,1,0:T(8,128)(2,1)S(1)} collective-permute-done((bf16[1,40,768]{2,1,0:T(8,128)(2,1)S(1)}, bf16[1,40,768]{2,1,0:T(8,128)(2,1)S(1)}, u32[]{:S(2)}, u32[]{:S(2)}) %collective-permute-start.13) | collective-permute-done | bytes 61472 | tf_op jit(solution)/shard_map/ppermute | solution.py:353
  359.9 8.4 %bucket_sums.14 = f32[64,192]{1,0:T(8,128)S(1)} custom-call(bf16[12,4,1024,256]{3,2,1,0:T(8,128)(2,1)} %get-tuple-element.75.ds_ref, s32[2,1024]{1,0:T(2,128)S(1)} %pad_add_fusion.cq_ref.crow_ref, s32[2,1024,128]{2,1,0:T(8,128)S(1)} %broadcast_in_dim.16.ck_ref.ccol_ref), custom_call_target="tpu_custom_call" | custom-call | flops 15000000512 | bytes 1000 | tf_op jit(solution)/shard_map/bucket_sums/pallas_call | solution.py:241
  374.8 8.2 %bucket_sums.15 = f32[64,192]{1,0:T(8,128)S(1)} custom-call(bf16[12,4,1024,256]{3,2,1,0:T(8,128)(2,1)} %get-tuple-element.75.ds_ref, s32[2,1024]{1,0:T(2,128)S(1)} %pad_add_fusion.cq_ref.crow_ref, s32[2,1024,128]{2,1,0:T(8,128)S(1)} %broadcast_in_dim.16.ck_ref.ccol_ref), custom_call_target="tpu_custom_call" | custom-call | flops 15000000512 | bytes 1000 | tf_op jit(solution)/shard_map/bucket_sums/pallas_call | solution.py:241
  403.2 5.6 %collective-permute-done.17 = bf16[4,40,768]{2,1,0:T(8,128)(2,1)S(1)} collective-permute-done((bf16[4,40,768]{2,1,0:T(8,128)(2,1)S(1)}, bf16[4,40,768]{2,1,0:T(8,128)(2,1)S(1)}, u32[]{:S(2)}, u32[]{:S(2)}) %collective-permute-start.17) | collective-permute-done | bytes 245792 | tf_op jit(solution)/shard_map/ppermute | solution.py:353
  418.2 9.8 %collective-permute-done.18 = bf16[8,40,768]{2,1,0:T(8,128)(2,1)S(1)} collective-permute-done((bf16[8,40,768]{2,1,0:T(8,128)(2,1)S(1)}, bf16[8,40,768]{2,1,0:T(8,128)(2,1)S(1)}, u32[]{:S(2)}, u32[]{:S(2)}) %collective-permute-start.18) | collective-permute-done | bytes 491552 | tf_op jit(solution)/shard_map/ppermute | solution.py:353
  462.8 7.4 %convert_element_type.433 = f32[768,3072]{1,0:T(8,128)} convert(bf16[768,3072]{1,0:T(8,128)(2,1)} %get-tuple-element.235) | non-fusion elementwise | flops 2359296 | bytes 14155776 | tf_op jit(solution)/shard_map/convert_element_type | solution.py:503
  (311 shorter events, 177.8 us)
Async XLA Ops:
  7.2 452.6 %all-reduce.5.cloned.1.call-start = ((), (), s32[]{:S(2)}) async-start(), calls=%async_computation | async-start | bytes 21233664 | tf_op jit(solution)/shard_map/psum | solution.py:468
  10.4 32.6 %collective-permute-start = (bf16[512,768]{0,1:T(8,128)(2,1)}, bf16[512,768]{0,1:T(8,128)(2,1)}, u32[]{:S(2)}, u32[]{:S(2)}) collective-permute-start(bf16[512,768]{0,1:T(8,128)(2,1)} %select_bitcast_fusion.5), channel_id=1, source_target_pairs={{0,1},{1,0},{2,3},{3,2},{4,5},{5,4},{6,7},{7,6},{8,9},{9,8},{10,11... | collective-permute-start | bytes 2359304 | tf_op jit(solution)/shard_map/ppermute | solution.py:326
  17.1 126.7 %collective-permute-start.2 = (bf16[512,768]{0,1:T(8,128)(2,1)}, bf16[512,768]{0,1:T(8,128)(2,1)}, u32[]{:S(2)}, u32[]{:S(2)}) collective-permute-start(bf16[512,768]{0,1:T(8,128)(2,1)} %select_bitcast_fusion.2), channel_id=1, source_target_pairs={{0,1},{1,0},{2,3},{3,2},{4,5},{5,4},{6,7},{7,6},{8,9},{9,8},{10,11... | collective-permute-start | bytes 2359304 | tf_op jit(solution)/shard_map/ppermute | solution.py:326
  254.8 131.6 %collective-permute-start.1 = (bf16[512,768]{0,1:T(8,128)(2,1)}, bf16[512,768]{0,1:T(8,128)(2,1)}, u32[]{:S(2)}, u32[]{:S(2)}) collective-permute-start(bf16[512,768]{0,1:T(8,128)(2,1)} %broadcast_select_fusion.6), channel_id=1, source_target_pairs={{0,1},{1,0},{2,3},{3,2},{4,5},{5,4},{6,7},{7,6},{8,9},{9,8},{10,11... | collective-permute-start | bytes 2359304 | tf_op jit(solution)/shard_map/ppermute | solution.py:334
  262.4 16.8 %collective-permute-start.4 = (bf16[3,384,768]{2,1,0:T(8,128)(2,1)}, bf16[3,384,768]{2,1,0:T(8,128)(2,1)}, u32[]{:S(2)}, u32[]{:S(2)}) collective-permute-start(bf16[3,384,768]{2,1,0:T(8,128)(2,1)} %convert_bitcast_fusion), channel_id=1, source_target_pairs={{0,2},{2,0},{4,6},{6,4},{8,10},{10,8},{12,14},{14,12},{16,18},{18,... | collective-permute-start | bytes 5308424 | tf_op jit(solution)/shard_map/ppermute | solution.py:353
  267.6 10.9 %collective-permute-start.5 = (bf16[64,768]{1,0:T(8,128)(2,1)S(1)}, bf16[64,768]{1,0:T(8,128)(2,1)S(1)}, u32[]{:S(2)}, u32[]{:S(2)}) collective-permute-start(bf16[64,768]{1,0:T(8,128)(2,1)S(1)} %convolution_convert_fusion.4), channel_id=1, source_target_pairs={{0,2},{2,0},{4,6},{6,4},{8,10},{10,8},{12,14},{14,12},{16,18},{18,... | collective-permute-start | bytes 294920 | tf_op jit(solution)/shard_map/ppermute | solution.py:353
  268.1 163.4 %collective-permute-start.3 = (bf16[512,768]{0,1:T(8,128)(2,1)}, bf16[512,768]{0,1:T(8,128)(2,1)}, u32[]{:S(2)}, u32[]{:S(2)}) collective-permute-start(bf16[512,768]{0,1:T(8,128)(2,1)} %broadcast_select_fusion.4), channel_id=1, source_target_pairs={{0,1},{1,0},{2,3},{3,2},{4,5},{5,4},{6,7},{7,6},{8,9},{9,8},{10,11... | collective-permute-start | bytes 2359304 | tf_op jit(solution)/shard_map/ppermute | solution.py:334
  292.9 19.5 %collective-permute-start.7 = (bf16[8,40,768]{2,1,0:T(8,128)(2,1)S(1)}, bf16[8,40,768]{2,1,0:T(8,128)(2,1)S(1)}, u32[]{:S(2)}, u32[]{:S(2)}) collective-permute-start(bf16[8,40,768]{2,1,0:T(8,128)(2,1)S(1)} %constant_dynamic-slice_fusion.10), channel_id=1, source_target_pairs={{0,1},{1,0},{2,3},{3,2},{4,5},{5,4},{6,7},{7,6},{8,9},{9,8},{10,11... | collective-permute-start | bytes 1474568 | tf_op jit(solution)/shard_map/ppermute | solution.py:353
  294.5 18.0 %collective-permute-start.6 = (bf16[8,40,768]{2,1,0:T(8,128)(2,1)S(1)}, bf16[8,40,768]{2,1,0:T(8,128)(2,1)S(1)}, u32[]{:S(2)}, u32[]{:S(2)}) collective-permute-start(bf16[8,40,768]{2,1,0:T(8,128)(2,1)S(1)} %constant_dynamic-slice_fusion.11), channel_id=1, source_target_pairs={{0,4},{2,6},{4,0},{6,2},{8,12},{10,14},{12,8},{14,10},{16,20},{18,... | collective-permute-start | bytes 1474568 | tf_op jit(solution)/shard_map/ppermute | solution.py:353
  312.7 10.5 %collective-permute-start.9 = (bf16[4,40,768]{2,1,0:T(8,128)(2,1)S(1)}, bf16[4,40,768]{2,1,0:T(8,128)(2,1)S(1)}, u32[]{:S(2)}, u32[]{:S(2)}) collective-permute-start(bf16[4,40,768]{2,1,0:T(8,128)(2,1)S(1)} %constant_dynamic-slice_fusion.8), channel_id=1, source_target_pairs={{0,4},{2,6},{4,0},{6,2},{8,12},{10,14},{12,8},{14,10},{16,20},{18,... | collective-permute-start | bytes 737288 | tf_op jit(solution)/shard_map/ppermute | solution.py:353
  314.3 9.1 %collective-permute-start.8 = (bf16[4,40,768]{2,1,0:T(8,128)(2,1)S(1)}, bf16[4,40,768]{2,1,0:T(8,128)(2,1)S(1)}, u32[]{:S(2)}, u32[]{:S(2)}) collective-permute-start(bf16[4,40,768]{2,1,0:T(8,128)(2,1)S(1)} %constant_dynamic-slice_fusion.9), channel_id=1, source_target_pairs={{0,1},{1,0},{2,3},{3,2},{4,5},{5,4},{6,7},{7,6},{8,9},{9,8},{10,11... | collective-permute-start | bytes 737288 | tf_op jit(solution)/shard_map/ppermute | solution.py:353
  323.4 10.4 %collective-permute-start.11 = (bf16[2,40,768]{2,1,0:T(8,128)(2,1)S(1)}, bf16[2,40,768]{2,1,0:T(8,128)(2,1)S(1)}, u32[]{:S(2)}, u32[]{:S(2)}) collective-permute-start(bf16[2,40,768]{2,1,0:T(8,128)(2,1)S(1)} %constant_dynamic-slice_fusion.6), channel_id=1, source_target_pairs={{0,8},{2,10},{4,12},{6,14},{8,0},{10,2},{12,4},{14,6},{16,24},{18,... | collective-permute-start | bytes 368648 | tf_op jit(solution)/shard_map/ppermute | solution.py:353
  346.8 10.4 %collective-permute-start.13 = (bf16[1,40,768]{2,1,0:T(8,128)(2,1)S(1)}, bf16[1,40,768]{2,1,0:T(8,128)(2,1)S(1)}, u32[]{:S(2)}, u32[]{:S(2)}) collective-permute-start(bf16[1,40,768]{2,1,0:T(8,128)(2,1)S(1)} %constant_dynamic-slice_fusion.4), channel_id=1, source_target_pairs={{0,16},{2,18},{4,20},{6,22},{8,24},{10,26},{12,28},{14,30},{16,0},... | collective-permute-start | bytes 184328 | tf_op jit(solution)/shard_map/ppermute | solution.py:353
  349.3 10.5 %collective-permute-start.12 = (bf16[1,40,768]{2,1,0:T(8,128)(2,1)S(1)}, bf16[1,40,768]{2,1,0:T(8,128)(2,1)S(1)}, u32[]{:S(2)}, u32[]{:S(2)}) collective-permute-start(bf16[1,40,768]{2,1,0:T(8,128)(2,1)S(1)} %constant_dynamic-slice_fusion.5), channel_id=1, source_target_pairs={{0,16},{2,18},{4,20},{6,22},{8,24},{10,26},{12,28},{14,30},{16,0},... | collective-permute-start | bytes 184328 | tf_op jit(solution)/shard_map/ppermute | solution.py:353
  359.8 11.5 %collective-permute-start.14 = (bf16[1,40,768]{2,1,0:T(8,128)(2,1)S(1)}, bf16[1,40,768]{2,1,0:T(8,128)(2,1)S(1)}, u32[]{:S(2)}, u32[]{:S(2)}) collective-permute-start(bf16[1,40,768]{2,1,0:T(8,128)(2,1)S(1)} %add_convert_fusion.14), channel_id=1, source_target_pairs={{0,16},{2,18},{4,20},{6,22},{8,24},{10,26},{12,28},{14,30},{16,0},... | collective-permute-start | bytes 184328 | tf_op jit(solution)/shard_map/ppermute | solution.py:353
  390.1 11.7 %collective-permute-start.19 = (bf16[2,40,768]{2,1,0:T(8,128)(2,1)S(1)}, bf16[2,40,768]{2,1,0:T(8,128)(2,1)S(1)}, u32[]{:S(2)}, u32[]{:S(2)}) collective-permute-start(bf16[2,40,768]{2,1,0:T(8,128)(2,1)S(1)} %get-tuple-element.73), channel_id=1, source_target_pairs={{0,8},{2,10},{4,12},{6,14},{8,0},{10,2},{12,4},{14,6},{16,24},{18,... | collective-permute-start | bytes 368648 | tf_op jit(solution)/shard_map/ppermute | solution.py:353
  390.2 27.2 %collective-permute-start.25 = (f32[88,128]{1,0:T(8,128)S(1)}, f32[88,128]{1,0:T(8,128)S(1)}, u32[]{:S(2)}, u32[]{:S(2)}) collective-permute-start(f32[88,128]{1,0:T(8,128)S(1)} %fusion.118), channel_id=1, source_target_pairs={{0,4},{2,6},{4,0},{6,2},{8,12},{10,14},{12,8},{14,10},{16,20},{18,... | collective-permute-start | bytes 135176 | tf_op jit(solution)/shard_map/ppermute | solution.py:353
  396.6 12.2 %collective-permute-start.17 = (bf16[4,40,768]{2,1,0:T(8,128)(2,1)S(1)}, bf16[4,40,768]{2,1,0:T(8,128)(2,1)S(1)}, u32[]{:S(2)}, u32[]{:S(2)}) collective-permute-start(bf16[4,40,768]{2,1,0:T(8,128)(2,1)S(1)} %pad_maximum_fusion.13), channel_id=1, source_target_pairs={{0,1},{1,0},{2,3},{3,2},{4,5},{5,4},{6,7},{7,6},{8,9},{9,8},{10,11... | collective-permute-start | bytes 737288 | tf_op jit(solution)/shard_map/ppermute | solution.py:353
  401.8 13.1 %collective-permute-start.20 = (bf16[4,40,768]{2,1,0:T(8,128)(2,1)S(1)}, bf16[4,40,768]{2,1,0:T(8,128)(2,1)S(1)}, u32[]{:S(2)}, u32[]{:S(2)}) collective-permute-start(bf16[4,40,768]{2,1,0:T(8,128)(2,1)S(1)} %pad_maximum_fusion.14), channel_id=1, source_target_pairs={{0,4},{2,6},{4,0},{6,2},{8,12},{10,14},{12,8},{14,10},{16,20},{18,... | collective-permute-start | bytes 737288 | tf_op jit(solution)/shard_map/ppermute | solution.py:353
  408.9 19.1 %collective-permute-start.18 = (bf16[8,40,768]{2,1,0:T(8,128)(2,1)S(1)}, bf16[8,40,768]{2,1,0:T(8,128)(2,1)S(1)}, u32[]{:S(2)}, u32[]{:S(2)}) collective-permute-start(bf16[8,40,768]{2,1,0:T(8,128)(2,1)S(1)} %pad_maximum_fusion.10), channel_id=1, source_target_pairs={{0,4},{2,6},{4,0},{6,2},{8,12},{10,14},{12,8},{14,10},{16,20},{18,... | collective-permute-start | bytes 1474568 | tf_op jit(solution)/shard_map/ppermute | solution.py:353
  415.0 14.2 %collective-permute-start.21 = (bf16[8,40,768]{2,1,0:T(8,128)(2,1)S(1)}, bf16[8,40,768]{2,1,0:T(8,128)(2,1)S(1)}, u32[]{:S(2)}, u32[]{:S(2)}) collective-permute-start(bf16[8,40,768]{2,1,0:T(8,128)(2,1)S(1)} %pad_maximum_fusion.11), channel_id=1, source_target_pairs={{0,1},{1,0},{2,3},{3,2},{4,5},{5,4},{6,7},{7,6},{8,9},{9,8},{10,11... | collective-permute-start | bytes 1474568 | tf_op jit(solution)/shard_map/ppermute | solution.py:353
  417.4 15.6 %collective-permute-start.26 = (f32[88,128]{1,0:T(8,128)S(1)}, f32[88,128]{1,0:T(8,128)S(1)}, u32[]{:S(2)}, u32[]{:S(2)}) collective-permute-start(f32[88,128]{1,0:T(8,128)S(1)} %fusion.157), channel_id=1, source_target_pairs={{0,8},{2,10},{4,12},{6,14},{8,0},{10,2},{12,4},{14,6},{16,24},{18,... | collective-permute-start | bytes 135176 | tf_op jit(solution)/shard_map/ppermute | solution.py:353
  429.2 19.1 %collective-permute-start.22 = (bf16[16,40,768]{2,1,0:T(8,128)(2,1)}, bf16[16,40,768]{2,1,0:T(8,128)(2,1)}, u32[]{:S(2)}, u32[]{:S(2)}) collective-permute-start(bf16[16,40,768]{2,1,0:T(8,128)(2,1)} %pad_maximum_fusion.8), channel_id=1, source_target_pairs={{0,2},{2,0},{4,6},{6,4},{8,10},{10,8},{12,14},{14,12},{16,18},{18,... | collective-permute-start | bytes 2949128 | tf_op jit(solution)/shard_map/ppermute | solution.py:353
  431.1 18.5 %collective-permute-start.23 = (bf16[16,40,768]{2,1,0:T(8,128)(2,1)}, bf16[16,40,768]{2,1,0:T(8,128)(2,1)}, u32[]{:S(2)}, u32[]{:S(2)}) collective-permute-start(bf16[16,40,768]{2,1,0:T(8,128)(2,1)} %pad_maximum_fusion.9), channel_id=1, source_target_pairs={{0,2},{2,0},{4,6},{6,4},{8,10},{10,8},{12,14},{14,12},{16,18},{18,... | collective-permute-start | bytes 2949128 | tf_op jit(solution)/shard_map/ppermute | solution.py:353
  (51 other events, 544.6 us)
Sparse Core Ops, SparseCore 0:
  193.6 237.4 all-reduce.4

commit v4 on v3

--- a/solution.py
+++ b/solution.py
@@ -63,8 +63,13 @@
     @pl.when(b==0)
     def _():
         ka_ref[:,:128]=k_ref[...]
-        for c in range(2*full//128):
-            wide_ref[:,c*128:(c+1)*128]=lookup(tab_ref[0,0],nidx_ref[:,c*128:(c+1)*128])
+        first,count=near_span(full)
+        table=tab_ref[0,0]
+        wide_ref[:,:first*128]=jnp.broadcast_to(table[0:1,31:32],(128,first*128))
+        for c in range(count):
+            wide_ref[:,(first+c)*128:(first+c+1)*128]=lookup(table,nidx_ref[:,c*128:(c+1)*128])
+        rest=2*full-(first+count)*128
+        wide_ref[:,2*full-rest:]=jnp.broadcast_to(table[0:1,15:16],(128,rest))
     @pl.when(before%nb==0)
     def _():
         vt_ref[0:128,:]=v_ref[...].T
@@ -116,7 +121,7 @@
           pl.BlockSpec((2,IB),lambda t:(0,now(t)%nb)),
           pl.BlockSpec((2,full,128),lambda t:(0,0,0)),
           pl.BlockSpec((1,2,8,128),lambda t:(now(t)//nb,0,0,0)),
-          pl.BlockSpec((128,2*full),lambda t:(0,0))],
+          pl.BlockSpec((128,nidx.shape[1]),lambda t:(0,0))],
         out_specs=[pl.BlockSpec((IB,128),lambda t:(was(t)%nb,was(t)//nb)),
           pl.BlockSpec((2,1,full,IB),lambda t:(was(t)//nb,was(t)%nb,0,0)),
           pl.BlockSpec((1,8,IB),lambda t:(was(t)//nb,0,was(t)%nb))],
@@ -211,7 +216,7 @@
     )(q,k,v,go,ctx,p,linv)
 
 THRESH=[-8192]+[1-e for e in reversed(FAR_EDGES)]+list(FAR_EDGES)
-def hist_kernel(ds_ref, crow_ref, ccol_ref, out_ref, acc_ref, *, heads, dt):
+def hist_kernel(ds_ref, crow_ref, ccol_ref, out_ref, acc_ref, lhs_ref, *, heads, dt):
     t=pl.program_id(0)
     nb=ds_ref.shape[1]
     sub=ds_ref.shape[2]//16
@@ -219,17 +224,18 @@
     def _(): acc_ref[...]=jnp.zeros_like(acc_ref)
     one=jnp.ones((16,IB),BF); zero=jnp.zeros((16,IB),BF)
     for u in range(sub):
+        total=None
         for kb in range(nb):
             parts=[]
             for kind in range(2):
                 row=jnp.broadcast_to(crow_ref[kind:kind+1,kb*IB:(kb+1)*IB],(16,IB)).astype(dt)
                 col=jnp.concatenate([ccol_ref[kind,u*16:(u+1)*16,:]]*(IB//128),axis=1)
+                less=row-col.astype(dt)
                 for e in range(32):
-                    th=THRESH[min(e,30)]
-                    parts.append(jnp.where(row<=(col-th).astype(dt),one,zero))
-            lhs=jnp.concatenate(parts,axis=0)
-            rhs=ds_ref[:,kb,u*16:(u+1)*16,:].reshape(heads*16,IB)
-            acc_ref[...]+=nt(lhs,rhs)
+                    parts.append(jnp.where(less<=jnp.asarray(-THRESH[min(e,30)],dt),one,zero))
+            lhs_ref[u%2,:,kb*IB:(kb+1)*IB]=jnp.concatenate(parts,axis=0)
+        rhs=jnp.concatenate([ds_ref[:,kb,u*16:(u+1)*16,:].reshape(heads*16,IB) for kb in range(nb)],axis=1)
+        acc_ref[...]+=nt(lhs_ref[u%2],rhs)
     @pl.when(t==pl.num_programs(0)-1)
     def _():
         r=lax.broadcasted_iota(jnp.int32,(1024,heads*16),0); c=lax.broadcasted_iota(jnp.int32,(1024,heads*16),1)
@@ -244,7 +250,7 @@
           pl.BlockSpec((2,jb,128),lambda t:(0,t+at,0))],
         out_specs=pl.BlockSpec((64,heads*16),lambda t:(0,0)),
         out_shape=jax.ShapeDtypeStruct((64,heads*16),F32),
-        scratch_shapes=[pltpu.VMEM((1024,heads*16),F32)],
+        scratch_shapes=[pltpu.VMEM((1024,heads*16),F32),pltpu.VMEM((2,1024,full),BF)],
         compiler_params=pltpu.CompilerParams(vmem_limit_bytes=48*1024*1024),
         cost_estimate=pl.CostEstimate(flops=HISTF,bytes_accessed=1000,transcendentals=0),
         name="bucket_sums")(ds,crow,ccol)
@@ -266,8 +272,12 @@
     t=jnp.round((t+4.0)*UNIT).astype(jnp.int32)
     t=t[0::2]+(t[1::2]<<16)
     return jnp.broadcast_to(t[:,:,None,:],(t.shape[0],2,8,128))
+def near_span(full):
+    kept=[c for c in range(2*full//128) if full-128*c-127<NEAR_EDGES[-1] and full-128*c+127>-NEAR_EDGES[-1]]
+    return kept[0],len(kept)
 def near_idx(full):
-    r=lax.broadcasted_iota(jnp.int32,(128,2*full),0); u=lax.broadcasted_iota(jnp.int32,(128,2*full),1)
+    first,count=near_span(full)
+    r=lax.broadcasted_iota(jnp.int32,(128,count*128),0); u=first*128+lax.broadcasted_iota(jnp.int32,(128,count*128),1)
     return level(r+full-u,NEAR_EDGES)
 
 
@@ -373,7 +383,7 @@
         came = self.move(x, step)
         return jnp.concatenate([jnp.where(mine == 0, x, came), jnp.where(mine == 0, came, x)], axis=0)
 
-    def total(self, parts, between=None):
+    def total(self, parts, between=None, last=None):
         rows = [p.shape[0] // self.pieces for p in parts]
         x = jnp.concatenate([p.reshape(self.pieces, r, p.shape[1]) for p, r in zip(parts, rows)], axis=1)
         count = x.shape[1]
@@ -389,6 +399,7 @@
         for i in reversed(range(stages)):
             lanes = hold(2 * stages - i, lanes) if stages == 4 else lanes
             lanes = [self.gather(x, order[i]) for x, order in zip(lanes, self.orders)]
+        lanes = last(lanes) if last else lanes
         came = [self.move(x, self.core) for x in lanes]
         mine = self.mine(self.core)
         own, came = jnp.concatenate(lanes, axis=1), jnp.concatenate(came, axis=1)
@@ -485,7 +496,12 @@
         return lanes
 
     late = [qkv_part[0], qkv_part[1], qkv_part[2], lay_part]
-    groups = route.total(late, between)
+    def last(lanes):
+        nonlocal early
+        *early, a, b = lax.optimization_barrier((*early, *lanes))
+        return [a, b]
+
+    groups = route.total(late, between, last)
     assert len(bucket_parts) == sum(plan)
     sums = jnp.sum(sum(bucket_parts).reshape(2, 32, heads, 16), axis=3)
     offset = lax.broadcasted_iota(jnp.int32, (2 * full, 32), 0)

time: 487 us -> 466 us (0.957)
  other arithmetic: 64.4 us -> 49.5 us
  Pallas kernels: 175 us -> 162 us
  waiting for transfers between devices: 58.1 us -> 66.6 us
    pallas_call x8, Pallas kernels: 66.6 us -> 57 us  [hist(): pl.pallas_call(functools.partial(hist_kernel, heads=heads, dt=dt), grid=(...]
    ppermute x2, waiting for transfers between devices: 0.01 us -> 8.45 us  [swap(): came = lax.ppermute(other, 'half', [(0, 1), (1, 0)])]
    unnamed x108 -> x121, local copies, waits for them, and re-layouts: 20 us -> 18.9 us
  transfers between devices with their start and end apart: 30 -> 30, of which waited for: 11 -> 11; matrix products, arithmetic and copies ran while one was open for 25% -> 25% of each run, Pallas kernels for 36% -> 35%
where the time goes in v4:
time: 466 us; the launch traced here: 462 us
  Pallas kernels  162 us (35%)
  matrix products  97 us (21%)
  waiting for transfers between devices  66.6 us (14%)
  other arithmetic  49.5 us (11%)
  starting transfers between devices  35.7 us (8%)
  local copies, waits for them, and re-layouts  34.7 us (7%)
  between operations  15.7 us (3%)
    pallas_call x1, Pallas kernels, fwd_attention(): pl.pallas_call(fwd_kernel, grid=(pairs * nb + 1,), in_specs=[pl.BlockSpec...  57.7 us
    pallas_call x8, Pallas kernels, hist(): pl.pallas_call(functools.partial(hist_kernel, heads=heads, dt=dt), grid=(...  57 us
    ppermute x25, waiting for transfers between devices, move(): lax.ppermute(x, axis, [(i, i ^ bit) for i in range(lax.axis_size(axis))])  53.9 us
    pallas_call x1, Pallas kernels, bwd_attention(): pl.pallas_call(bwd_kernel, grid=(pairs, nb), in_specs=[pl.BlockSpec((IB,...  47.6 us
    dot_general x6, matrix products, nn(): lax.dot_general(a, b, (((1,), (0,)), ((), ())), preferred_element_type=F32)  35.7 us
    dot_general x6, matrix products, nt(): lax.dot_general(a, b, (((1,), (1,)), ((), ())), preferred_element_type=F32)  31.2 us
    ppermute x25, starting transfers between devices, move(): lax.ppermute(x, axis, [(i, i ^ bit) for i in range(lax.axis_size(axis))])  27.3 us
    unnamed x121, local copies, waits for them, and re-layouts  18.9 us
  transfers between devices with their start and end apart: 30, of which 11 were waited for; matrix products, arithmetic and copies ran while one was open for 25% of the time, Pallas kernels for 35%

profile of v4, /device:TPU:0, one launch (start us, length us, event | category | flops | bytes accessed | tf_op | source)
XLA Modules:
  0.0 461.5 jit_solution(9952705746494971449)
XLA Ops:
  23.6 8.4 %collective-permute-done = bf16[512,768]{0,1:T(8,128)(2,1)} collective-permute-done((bf16[512,768]{0,1:T(8,128)(2,1)}, bf16[512,768]{0,1:T(8,128)(2,1)}, u32[]{:S(2)}, u32[]{:S(2)}) %collective-permute-start) | collective-permute-done | bytes 786464 | tf_op jit(solution)/shard_map/ppermute | solution.py:336
  42.3 57.7 %attend.1 = (bf16[1024,768]{1,0:T(8,128)(2,1)S(1)}, bf16[12,4,1024,256]{3,2,1,0:T(8,128)(2,1)}, f32[6,8,1024]{2,1,0:T(8,128)S(1)}) custom-call(s32[1]{0:T(128)} %dynamic_slice.68.len_ref, bf16[1024,2304]{1,0:T(8,128)(2,1)} %add_convert_fusion.1.q_ref.k_ref.v_ref, bf16[1024,2304]{1,0:T(8,128)(2,1)} %add_convert_fusion.1.q_ref.k_ref.v_ref, ...), custom_call_target="tpu_custom_call" | custom-call | flops 1000 | bytes 1000 | tf_op jit(solution)/shard_map/attend/pallas_call | solution.py:115
  103.0 19.0 %add_convert_fusion = (bf16[1024,3072]{1,0:T(8,128)(2,1)}, bf16[1024,3072]{1,0:T(8,128)(2,1)}) fusion(f32[3072]{0:T(1024)S(1)} %convert_element_type.361, bf16[768,3072]{1,0:T(8,128)(2,1)S(1)} %bitcast.548, f32[1024,768]{0,1:T(8,128)S(1)} %get-tuple-element.369, f32[768]{0:T(1024)S(1)} %convert_element_type.359, f32[768]{0:T(1024)S(1)} %convert_element_type.358, ...), kind=kOutput, calls=%fused_computation.2 | convolution fusion | flops 4920705024 | bytes 20473856 | tf_op jit(solution)/shard_map/dot_general | solution.py:20
  122.0 7.7 %fusion.126 = (f32[1024]{0:T(1024)S(1)}, f32[1024,768]{0,1:T(8,128)S(1)}) fusion(f32[768]{0:T(1024)S(1)} %convert_element_type.364, bf16[1024,3072]{1,0:T(8,128)(2,1)} %get-tuple-element.61, bf16[3072,768]{1,0:T(8,128)(2,1)S(1)} %bitcast.546, f32[768]{0:T(1024)S(1)} %convert_element_type.359, f32[768]{0:T(1024)S(1)} %convert_element_type.358, ...), kind=kOutput, calls=%fused_computation.406 | convolution fusion | flops 4837342208 | bytes 17323008 | tf_op jit(solution)/shard_map/dot_general | solution.py:20
  137.0 6.9 %convolution_convert_fusion.1 = bf16[3072,768]{1,0:T(8,128)(2,1)} fusion(bf16[1024,3072]{1,0:T(8,128)(2,1)S(1)} %bitcast.550, bf16[1024,768]{0,1:T(8,128)(2,1)S(1)} %get-tuple-element.254), kind=kOutput, calls=%fused_computation.9 | convolution fusion | flops 4834197504 | bytes 12582912 | tf_op jit(solution)/shard_map/dot_general | solution.py:315
  143.9 8.7 %multiply_convert_fusion = bf16[1024,3072]{1,0:T(8,128)(2,1)S(1)} fusion(bf16[1024,3072]{1,0:T(8,128)(2,1)} %get-tuple-element.62, bf16[1024,768]{0,1:T(8,128)(2,1)S(1)} %get-tuple-element.254, bf16[3072,768]{1,0:T(8,128)(2,1)} %param.33), kind=kOutput, calls=%fused_computation.1 | convolution fusion | flops 4841275392 | bytes 18874368 | tf_op jit(solution)/shard_map/dot_general | solution.py:18
  152.6 9.0 %multiply_reduce_fusion = (f32[768]{0:T(1024)S(1)}, f32[1024]{0:T(1024)S(1)}, f32[768]{0:T(1024)S(1)}, f32[1024,768]{0,1:T(8,128)S(1)}) fusion(f32[1024,768]{0,1:T(8,128)S(1)} %get-tuple-element.369, f32[1024]{0:T(1024)S(1)} %fusion.83, f32[1024]{0:T(1024)S(1)} %broadcast_multiply_fusion.1, f32[768]{0:T(1024)S(1)} %convert_element_type.358, ...), kind=kOutput, calls=%fused_computation.22 | convolution fusion | flops 4847563776 | bytes 22061056 | tf_op jit(solution)/shard_map/dot_general | solution.py:18
  162.5 7.2 %convolution_convert_fusion = bf16[768,3072]{1,0:T(8,128)(2,1)} fusion(bf16[1024,3072]{1,0:T(8,128)(2,1)S(1)} %multiply_convert_fusion, f32[1024,768]{0,1:T(8,128)S(1)} %get-tuple-element.369, f32[768]{0:T(1024)S(1)} %convert_element_type.359, f32[768]{0:T(1024)S(1)} %convert_element_type.358, f32[1024]{0:T(1024)S(1)} %fusion.83, ...), kind=kOutput, calls=%fused_computation.8 | convolution fusion | flops 4838129664 | bytes 14170112 | tf_op jit(solution)/shard_map/dot_general | solution.py:315
  183.0 47.6 %attend_back.1 = (bf16[3,1024,768]{2,1,0:T(8,128)(2,1)}, bf16[12,4,1024,256]{3,2,1,0:T(8,128)(2,1)}, f32[6,8,2048]{2,1,0:T(8,128)S(1)}) custom-call(bf16[1024,2304]{1,0:T(8,128)(2,1)} %add_convert_fusion.1.q_ref.k_ref.v_ref, bf16[1024,2304]{1,0:T(8,128)(2,1)} %add_convert_fusion.1.q_ref.k_ref.v_ref, ...), custom_call_target="tpu_custom_call", output_to_operand_aliasing={{1}: (5, {})} | custom-call | flops 1000 | bytes 1000 | tf_op jit(solution)/shard_map/attend_back/pallas_call | solution.py:197
  243.9 6.0 %convert_bitcast_fusion = bf16[3,384,768]{2,1,0:T(8,128)(2,1)} fusion(bf16[3,1024,768]{2,1,0:T(8,128)(2,1)} %get-tuple-element.66, bf16[1024,768]{0,1:T(8,128)(2,1)} %copy-done.23, s32[]{:T(128)S(6)} %select_n.354), kind=kOutput, calls=%fused_computation.46 | convolution fusion | flops 1812824064 | bytes 7274500 | tf_op jit(solution)/shard_map/td,...tf->...df/dot_general | solution.py:368
  255.6 7.0 %bucket_sums.8 = f32[64,192]{1,0:T(8,128)S(1)} custom-call(bf16[12,4,1024,256]{3,2,1,0:T(8,128)(2,1)} %get-tuple-element.82.ds_ref, s32[2,1024]{1,0:T(2,128)S(1)} %pad_add_fusion.cq_ref.crow_ref, s32[2,1024,128]{2,1,0:T(8,128)S(1)} %broadcast_in_dim.16.ck_ref.ccol_ref), custom_call_target="tpu_custom_call" | custom-call | flops 15000000512 | bytes 1000 | tf_op jit(solution)/shard_map/bucket_sums/pallas_call | solution.py:247
  268.8 7.1 %bucket_sums.10 = f32[64,192]{1,0:T(8,128)S(1)} custom-call(bf16[12,4,1024,256]{3,2,1,0:T(8,128)(2,1)} %get-tuple-element.82.ds_ref, s32[2,1024]{1,0:T(2,128)S(1)} %pad_add_fusion.cq_ref.crow_ref, s32[2,1024,128]{2,1,0:T(8,128)S(1)} %broadcast_in_dim.16.ck_ref.ccol_ref), custom_call_target="tpu_custom_call" | custom-call | flops 15000000512 | bytes 1000 | tf_op jit(solution)/shard_map/bucket_sums/pallas_call | solution.py:247
  278.0 7.4 %bucket_sums.9 = f32[64,192]{1,0:T(8,128)S(1)} custom-call(bf16[12,4,1024,256]{3,2,1,0:T(8,128)(2,1)} %get-tuple-element.82.ds_ref, s32[2,1024]{1,0:T(2,128)S(1)} %pad_add_fusion.cq_ref.crow_ref, s32[2,1024,128]{2,1,0:T(8,128)S(1)} %broadcast_in_dim.16.ck_ref.ccol_ref), custom_call_target="tpu_custom_call" | custom-call | flops 15000000512 | bytes 1000 | tf_op jit(solution)/shard_map/bucket_sums/pallas_call | solution.py:247
  285.5 7.4 %collective-permute-done.7 = bf16[8,40,768]{2,1,0:T(8,128)(2,1)S(1)} collective-permute-done((bf16[8,40,768]{2,1,0:T(8,128)(2,1)S(1)}, bf16[8,40,768]{2,1,0:T(8,128)(2,1)S(1)}, u32[]{:S(2)}, u32[]{:S(2)}) %collective-permute-start.7) | collective-permute-done | bytes 491552 | tf_op jit(solution)/shard_map/ppermute | solution.py:363
  295.1 7.0 %bucket_sums.11 = f32[64,192]{1,0:T(8,128)S(1)} custom-call(bf16[12,4,1024,256]{3,2,1,0:T(8,128)(2,1)} %get-tuple-element.82.ds_ref, s32[2,1024]{1,0:T(2,128)S(1)} %pad_add_fusion.cq_ref.crow_ref, s32[2,1024,128]{2,1,0:T(8,128)S(1)} %broadcast_in_dim.16.ck_ref.ccol_ref), custom_call_target="tpu_custom_call" | custom-call | flops 15000000512 | bytes 1000 | tf_op jit(solution)/shard_map/bucket_sums/pallas_call | solution.py:247
  304.0 7.1 %bucket_sums.12 = f32[64,192]{1,0:T(8,128)S(1)} custom-call(bf16[12,4,1024,256]{3,2,1,0:T(8,128)(2,1)} %get-tuple-element.82.ds_ref, s32[2,1024]{1,0:T(2,128)S(1)} %pad_add_fusion.cq_ref.crow_ref, s32[2,1024,128]{2,1,0:T(8,128)S(1)} %broadcast_in_dim.16.ck_ref.ccol_ref), custom_call_target="tpu_custom_call" | custom-call | flops 15000000512 | bytes 1000 | tf_op jit(solution)/shard_map/bucket_sums/pallas_call | solution.py:247
  311.6 6.0 %collective-permute-done.10 = bf16[2,40,768]{2,1,0:T(8,128)(2,1)S(1)} collective-permute-done((bf16[2,40,768]{2,1,0:T(8,128)(2,1)S(1)}, bf16[2,40,768]{2,1,0:T(8,128)(2,1)S(1)}, u32[]{:S(2)}, u32[]{:S(2)}) %collective-permute-start.10) | collective-permute-done | bytes 122912 | tf_op jit(solution)/shard_map/ppermute | solution.py:363
  317.7 7.0 %bucket_sums.13 = f32[64,192]{1,0:T(8,128)S(1)} custom-call(bf16[12,4,1024,256]{3,2,1,0:T(8,128)(2,1)} %get-tuple-element.82.ds_ref, s32[2,1024]{1,0:T(2,128)S(1)} %pad_add_fusion.cq_ref.crow_ref, s32[2,1024,128]{2,1,0:T(8,128)S(1)} %broadcast_in_dim.16.ck_ref.ccol_ref), custom_call_target="tpu_custom_call" | custom-call | flops 15000000512 | bytes 1000 | tf_op jit(solution)/shard_map/bucket_sums/pallas_call | solution.py:247
  327.7 8.1 %collective-permute-done.13 = bf16[1,40,768]{2,1,0:T(8,128)(2,1)S(1)} collective-permute-done((bf16[1,40,768]{2,1,0:T(8,128)(2,1)S(1)}, bf16[1,40,768]{2,1,0:T(8,128)(2,1)S(1)}, u32[]{:S(2)}, u32[]{:S(2)}) %collective-permute-start.13) | collective-permute-done | bytes 61472 | tf_op jit(solution)/shard_map/ppermute | solution.py:363
  338.6 7.0 %bucket_sums.14 = f32[64,192]{1,0:T(8,128)S(1)} custom-call(bf16[12,4,1024,256]{3,2,1,0:T(8,128)(2,1)} %get-tuple-element.82.ds_ref, s32[2,1024]{1,0:T(2,128)S(1)} %pad_add_fusion.cq_ref.crow_ref, s32[2,1024,128]{2,1,0:T(8,128)S(1)} %broadcast_in_dim.16.ck_ref.ccol_ref), custom_call_target="tpu_custom_call" | custom-call | flops 15000000512 | bytes 1000 | tf_op jit(solution)/shard_map/bucket_sums/pallas_call | solution.py:247
  351.6 7.3 %bucket_sums.15 = f32[64,192]{1,0:T(8,128)S(1)} custom-call(bf16[12,4,1024,256]{3,2,1,0:T(8,128)(2,1)} %get-tuple-element.82.ds_ref, s32[2,1024]{1,0:T(2,128)S(1)} %pad_add_fusion.cq_ref.crow_ref, s32[2,1024,128]{2,1,0:T(8,128)S(1)} %broadcast_in_dim.16.ck_ref.ccol_ref), custom_call_target="tpu_custom_call" | custom-call | flops 15000000512 | bytes 1000 | tf_op jit(solution)/shard_map/bucket_sums/pallas_call | solution.py:247
  387.0 10.5 %collective-permute-done.17 = bf16[4,40,768]{2,1,0:T(8,128)(2,1)S(1)} collective-permute-done((bf16[4,40,768]{2,1,0:T(8,128)(2,1)S(1)}, bf16[4,40,768]{2,1,0:T(8,128)(2,1)S(1)}, u32[]{:S(2)}, u32[]{:S(2)}) %collective-permute-start.17) | collective-permute-done | bytes 245792 | tf_op jit(solution)/shard_map/ppermute | solution.py:363
  405.1 8.5 %collective-permute-done.18 = bf16[8,40,768]{2,1,0:T(8,128)(2,1)S(1)} collective-permute-done((bf16[8,40,768]{2,1,0:T(8,128)(2,1)S(1)}, bf16[8,40,768]{2,1,0:T(8,128)(2,1)S(1)}, u32[]{:S(2)}, u32[]{:S(2)}) %collective-permute-start.18) | collective-permute-done | bytes 491552 | tf_op jit(solution)/shard_map/ppermute | solution.py:363
  430.2 7.9 %convert_element_type.433 = f32[768,3072]{1,0:T(8,128)} convert(bf16[768,3072]{1,0:T(8,128)(2,1)} %get-tuple-element.90) | non-fusion elementwise | flops 2359296 | bytes 14155776 | tf_op jit(solution)/shard_map/convert_element_type | solution.py:519
  (326 shorter events, 162.0 us)
Async XLA Ops:
  7.2 412.8 %all-reduce.5.cloned.1.call-start = ((), (), s32[]{:S(2)}) async-start(), calls=%async_computation | async-start | bytes 21233664 | tf_op jit(solution)/shard_map/psum | solution.py:479
  10.4 21.6 %collective-permute-start = (bf16[512,768]{0,1:T(8,128)(2,1)}, bf16[512,768]{0,1:T(8,128)(2,1)}, u32[]{:S(2)}, u32[]{:S(2)}) collective-permute-start(bf16[512,768]{0,1:T(8,128)(2,1)} %select_bitcast_fusion.5), channel_id=1, source_target_pairs={{0,1},{1,0},{2,3},{3,2},{4,5},{5,4},{6,7},{7,6},{8,9},{9,8},{10,11... | collective-permute-start | bytes 2359304 | tf_op jit(solution)/shard_map/ppermute | solution.py:336
  18.7 111.0 %collective-permute-start.2 = (bf16[512,768]{0,1:T(8,128)(2,1)}, bf16[512,768]{0,1:T(8,128)(2,1)}, u32[]{:S(2)}, u32[]{:S(2)}) collective-permute-start(bf16[512,768]{0,1:T(8,128)(2,1)} %select_bitcast_fusion.2), channel_id=1, source_target_pairs={{0,1},{1,0},{2,3},{3,2},{4,5},{5,4},{6,7},{7,6},{8,9},{9,8},{10,11... | collective-permute-start | bytes 2359304 | tf_op jit(solution)/shard_map/ppermute | solution.py:336
  241.7 126.9 %collective-permute-start.1 = (bf16[512,768]{0,1:T(8,128)(2,1)}, bf16[512,768]{0,1:T(8,128)(2,1)}, u32[]{:S(2)}, u32[]{:S(2)}) collective-permute-start(bf16[512,768]{0,1:T(8,128)(2,1)} %broadcast_select_fusion.6), channel_id=1, source_target_pairs={{0,1},{1,0},{2,3},{3,2},{4,5},{5,4},{6,7},{7,6},{8,9},{9,8},{10,11... | collective-permute-start | bytes 2359304 | tf_op jit(solution)/shard_map/ppermute | solution.py:344
  249.9 13.4 %collective-permute-start.4 = (bf16[3,384,768]{2,1,0:T(8,128)(2,1)}, bf16[3,384,768]{2,1,0:T(8,128)(2,1)}, u32[]{:S(2)}, u32[]{:S(2)}) collective-permute-start(bf16[3,384,768]{2,1,0:T(8,128)(2,1)} %convert_bitcast_fusion), channel_id=1, source_target_pairs={{0,2},{2,0},{4,6},{6,4},{8,10},{10,8},{12,14},{14,12},{16,18},{18,... | collective-permute-start | bytes 5308424 | tf_op jit(solution)/shard_map/ppermute | solution.py:363
  254.0 8.7 %collective-permute-start.5 = (bf16[64,768]{1,0:T(8,128)(2,1)S(1)}, bf16[64,768]{1,0:T(8,128)(2,1)S(1)}, u32[]{:S(2)}, u32[]{:S(2)}) collective-permute-start(bf16[64,768]{1,0:T(8,128)(2,1)S(1)} %convolution_convert_fusion.4), channel_id=1, source_target_pairs={{0,2},{2,0},{4,6},{6,4},{8,10},{10,8},{12,14},{14,12},{16,18},{18,... | collective-permute-start | bytes 294920 | tf_op jit(solution)/shard_map/ppermute | solution.py:363
  275.9 16.9 %collective-permute-start.7 = (bf16[8,40,768]{2,1,0:T(8,128)(2,1)S(1)}, bf16[8,40,768]{2,1,0:T(8,128)(2,1)S(1)}, u32[]{:S(2)}, u32[]{:S(2)}) collective-permute-start(bf16[8,40,768]{2,1,0:T(8,128)(2,1)S(1)} %constant_dynamic-slice_fusion.10), channel_id=1, source_target_pairs={{0,1},{1,0},{2,3},{3,2},{4,5},{5,4},{6,7},{7,6},{8,9},{9,8},{10,11... | collective-permute-start | bytes 1474568 | tf_op jit(solution)/shard_map/ppermute | solution.py:363
  276.0 16.9 %collective-permute-start.6 = (bf16[8,40,768]{2,1,0:T(8,128)(2,1)S(1)}, bf16[8,40,768]{2,1,0:T(8,128)(2,1)S(1)}, u32[]{:S(2)}, u32[]{:S(2)}) collective-permute-start(bf16[8,40,768]{2,1,0:T(8,128)(2,1)S(1)} %constant_dynamic-slice_fusion.11), channel_id=1, source_target_pairs={{0,4},{2,6},{4,0},{6,2},{8,12},{10,14},{12,8},{14,10},{16,20},{18,... | collective-permute-start | bytes 1474568 | tf_op jit(solution)/shard_map/ppermute | solution.py:363
  293.2 9.0 %collective-permute-start.9 = (bf16[4,40,768]{2,1,0:T(8,128)(2,1)S(1)}, bf16[4,40,768]{2,1,0:T(8,128)(2,1)S(1)}, u32[]{:S(2)}, u32[]{:S(2)}) collective-permute-start(bf16[4,40,768]{2,1,0:T(8,128)(2,1)S(1)} %constant_dynamic-slice_fusion.8), channel_id=1, source_target_pairs={{0,4},{2,6},{4,0},{6,2},{8,12},{10,14},{12,8},{14,10},{16,20},{18,... | collective-permute-start | bytes 737288 | tf_op jit(solution)/shard_map/ppermute | solution.py:363
  302.4 9.2 %collective-permute-start.11 = (bf16[2,40,768]{2,1,0:T(8,128)(2,1)S(1)}, bf16[2,40,768]{2,1,0:T(8,128)(2,1)S(1)}, u32[]{:S(2)}, u32[]{:S(2)}) collective-permute-start(bf16[2,40,768]{2,1,0:T(8,128)(2,1)S(1)} %constant_dynamic-slice_fusion.6), channel_id=1, source_target_pairs={{0,8},{2,10},{4,12},{6,14},{8,0},{10,2},{12,4},{14,6},{16,24},{18,... | collective-permute-start | bytes 368648 | tf_op jit(solution)/shard_map/ppermute | solution.py:363
  324.7 11.1 %collective-permute-start.13 = (bf16[1,40,768]{2,1,0:T(8,128)(2,1)S(1)}, bf16[1,40,768]{2,1,0:T(8,128)(2,1)S(1)}, u32[]{:S(2)}, u32[]{:S(2)}) collective-permute-start(bf16[1,40,768]{2,1,0:T(8,128)(2,1)S(1)} %constant_dynamic-slice_fusion.4), channel_id=1, source_target_pairs={{0,16},{2,18},{4,20},{6,22},{8,24},{10,26},{12,28},{14,30},{16,0},... | collective-permute-start | bytes 184328 | tf_op jit(solution)/shard_map/ppermute | solution.py:363
  326.9 11.6 %collective-permute-start.12 = (bf16[1,40,768]{2,1,0:T(8,128)(2,1)S(1)}, bf16[1,40,768]{2,1,0:T(8,128)(2,1)S(1)}, u32[]{:S(2)}, u32[]{:S(2)}) collective-permute-start(bf16[1,40,768]{2,1,0:T(8,128)(2,1)S(1)} %constant_dynamic-slice_fusion.5), channel_id=1, source_target_pairs={{0,16},{2,18},{4,20},{6,22},{8,24},{10,26},{12,28},{14,30},{16,0},... | collective-permute-start | bytes 184328 | tf_op jit(solution)/shard_map/ppermute | solution.py:363
  338.6 10.1 %collective-permute-start.14 = (bf16[1,40,768]{2,1,0:T(8,128)(2,1)S(1)}, bf16[1,40,768]{2,1,0:T(8,128)(2,1)S(1)}, u32[]{:S(2)}, u32[]{:S(2)}) collective-permute-start(bf16[1,40,768]{2,1,0:T(8,128)(2,1)S(1)} %add_convert_fusion.14), channel_id=1, source_target_pairs={{0,16},{2,18},{4,20},{6,22},{8,24},{10,26},{12,28},{14,30},{16,0},... | collective-permute-start | bytes 184328 | tf_op jit(solution)/shard_map/ppermute | solution.py:363
  366.2 34.2 %collective-permute-start.3 = (bf16[512,768]{0,1:T(8,128)(2,1)S(1)}, bf16[512,768]{0,1:T(8,128)(2,1)S(1)}, u32[]{:S(2)}, u32[]{:S(2)}) collective-permute-start(bf16[512,768]{0,1:T(8,128)(2,1)S(1)} %broadcast_select_fusion.4), channel_id=1, source_target_pairs={{0,1},{1,0},{2,3},{3,2},{4,5},{5,4},{6,7},{7,6},{8,9},{9,8},{10,11... | collective-permute-start | bytes 2359304 | tf_op jit(solution)/shard_map/ppermute | solution.py:344
  371.0 9.1 %collective-permute-start.16 = (bf16[2,40,768]{2,1,0:T(8,128)(2,1)S(1)}, bf16[2,40,768]{2,1,0:T(8,128)(2,1)S(1)}, u32[]{:S(2)}, u32[]{:S(2)}) collective-permute-start(bf16[2,40,768]{2,1,0:T(8,128)(2,1)S(1)} %copy-done.26), channel_id=1, source_target_pairs={{0,8},{2,10},{4,12},{6,14},{8,0},{10,2},{12,4},{14,6},{16,24},{18,... | collective-permute-start | bytes 368648 | tf_op jit(solution)/shard_map/ppermute | solution.py:363
  373.6 11.8 %collective-permute-start.19 = (bf16[2,40,768]{2,1,0:T(8,128)(2,1)S(1)}, bf16[2,40,768]{2,1,0:T(8,128)(2,1)S(1)}, u32[]{:S(2)}, u32[]{:S(2)}) collective-permute-start(bf16[2,40,768]{2,1,0:T(8,128)(2,1)S(1)} %get-tuple-element.78), channel_id=1, source_target_pairs={{0,8},{2,10},{4,12},{6,14},{8,0},{10,2},{12,4},{14,6},{16,24},{18,... | collective-permute-start | bytes 368648 | tf_op jit(solution)/shard_map/ppermute | solution.py:363
  373.6 28.0 %collective-permute-start.26 = (f32[88,128]{1,0:T(8,128)S(1)}, f32[88,128]{1,0:T(8,128)S(1)}, u32[]{:S(2)}, u32[]{:S(2)}) collective-permute-start(f32[88,128]{1,0:T(8,128)S(1)} %fusion.155), channel_id=1, source_target_pairs={{0,8},{2,10},{4,12},{6,14},{8,0},{10,2},{12,4},{14,6},{16,24},{18,... | collective-permute-start | bytes 135176 | tf_op jit(solution)/shard_map/ppermute | solution.py:363
  380.2 17.3 %collective-permute-start.17 = (bf16[4,40,768]{2,1,0:T(8,128)(2,1)S(1)}, bf16[4,40,768]{2,1,0:T(8,128)(2,1)S(1)}, u32[]{:S(2)}, u32[]{:S(2)}) collective-permute-start(bf16[4,40,768]{2,1,0:T(8,128)(2,1)S(1)} %pad_maximum_fusion.13), channel_id=1, source_target_pairs={{0,1},{1,0},{2,3},{3,2},{4,5},{5,4},{6,7},{7,6},{8,9},{9,8},{10,11... | collective-permute-start | bytes 737288 | tf_op jit(solution)/shard_map/ppermute | solution.py:363
  385.4 12.7 %collective-permute-start.20 = (bf16[4,40,768]{2,1,0:T(8,128)(2,1)S(1)}, bf16[4,40,768]{2,1,0:T(8,128)(2,1)S(1)}, u32[]{:S(2)}, u32[]{:S(2)}) collective-permute-start(bf16[4,40,768]{2,1,0:T(8,128)(2,1)S(1)} %pad_maximum_fusion.14), channel_id=1, source_target_pairs={{0,4},{2,6},{4,0},{6,2},{8,12},{10,14},{12,8},{14,10},{16,20},{18,... | collective-permute-start | bytes 737288 | tf_op jit(solution)/shard_map/ppermute | solution.py:363
  397.6 16.0 %collective-permute-start.18 = (bf16[8,40,768]{2,1,0:T(8,128)(2,1)S(1)}, bf16[8,40,768]{2,1,0:T(8,128)(2,1)S(1)}, u32[]{:S(2)}, u32[]{:S(2)}) collective-permute-start(bf16[8,40,768]{2,1,0:T(8,128)(2,1)S(1)} %pad_maximum_fusion.10), channel_id=1, source_target_pairs={{0,4},{2,6},{4,0},{6,2},{8,12},{10,14},{12,8},{14,10},{16,20},{18,... | collective-permute-start | bytes 1474568 | tf_op jit(solution)/shard_map/ppermute | solution.py:363
  398.2 16.5 %collective-permute-start.21 = (bf16[8,40,768]{2,1,0:T(8,128)(2,1)S(1)}, bf16[8,40,768]{2,1,0:T(8,128)(2,1)S(1)}, u32[]{:S(2)}, u32[]{:S(2)}) collective-permute-start(bf16[8,40,768]{2,1,0:T(8,128)(2,1)S(1)} %pad_maximum_fusion.11), channel_id=1, source_target_pairs={{0,1},{1,0},{2,3},{3,2},{4,5},{5,4},{6,7},{7,6},{8,9},{9,8},{10,11... | collective-permute-start | bytes 1474568 | tf_op jit(solution)/shard_map/ppermute | solution.py:363
  401.7 18.5 %collective-permute-start.27 = (f32[88,128]{1,0:T(8,128)S(1)}, f32[88,128]{1,0:T(8,128)S(1)}, u32[]{:S(2)}, u32[]{:S(2)}) collective-permute-start(f32[88,128]{1,0:T(8,128)S(1)} %add.563), channel_id=1, source_target_pairs={{0,16},{2,18},{4,20},{6,22},{8,24},{10,26},{12,28},{14,30},{16,0},... | collective-permute-start | bytes 135176 | tf_op jit(solution)/shard_map/ppermute | solution.py:363
  420.0 25.1 %collective-permute-start.22 = (bf16[16,40,768]{2,1,0:T(8,128)(2,1)}, bf16[16,40,768]{2,1,0:T(8,128)(2,1)}, u32[]{:S(2)}, u32[]{:S(2)}) collective-permute-start(bf16[16,40,768]{2,1,0:T(8,128)(2,1)} %pad_maximum_fusion.8), channel_id=1, source_target_pairs={{0,2},{2,0},{4,6},{6,4},{8,10},{10,8},{12,14},{14,12},{16,18},{18,... | collective-permute-start | bytes 2949128 | tf_op jit(solution)/shard_map/ppermute | solution.py:363
  421.1 25.3 %collective-permute-start.23 = (bf16[16,40,768]{2,1,0:T(8,128)(2,1)}, bf16[16,40,768]{2,1,0:T(8,128)(2,1)}, u32[]{:S(2)}, u32[]{:S(2)}) collective-permute-start(bf16[16,40,768]{2,1,0:T(8,128)(2,1)} %pad_maximum_fusion.9), channel_id=1, source_target_pairs={{0,2},{2,0},{4,6},{6,4},{8,10},{10,8},{12,14},{14,12},{16,18},{18,... | collective-permute-start | bytes 2949128 | tf_op jit(solution)/shard_map/ppermute | solution.py:363
  (57 other events, 548.5 us)
Sparse Core Ops, SparseCore 0:
  180.3 239.6 all-reduce.4

commit v5 on v4

--- a/solution.py
+++ b/solution.py
@@ -484,7 +484,7 @@
     grad_start = (grad_r1 + sum(nt(grad3[c], qkv_weight[:, c * width:(c + 1) * width]) for c in range(3))).astype(BF)
     input_grad = unswap(grad_start, me)
     lay_part = route.product(feats, grad_start)
-    plan = [1, 2, 1, 1, 1, 1, 1]
+    plan = [1, 1, 1, 1, 1, 1, 2]
     bucket_parts = []
 
     def between(i, lanes):

time: 466 us -> 463 us (level)
  starting transfers between devices: 35.7 us -> 31 us
  transfers between devices with their start and end apart: 30 -> 30, of which waited for: 11 -> 12; matrix products, arithmetic and copies ran while one was open for 25% -> 25% of each run, Pallas kernels for 35% -> 35%
where the time goes in v5:
time: 463 us; the launch traced here: 458 us
  Pallas kernels  162 us (35%)
  matrix products  97 us (21%)
  waiting for transfers between devices  68.3 us (15%)
  other arithmetic  49.4 us (11%)
  local copies, waits for them, and re-layouts  34.6 us (7%)
  starting transfers between devices  31 us (7%)
  between operations  15.7 us (3%)
    pallas_call x1, Pallas kernels, fwd_attention(): pl.pallas_call(fwd_kernel, grid=(pairs * nb + 1,), in_specs=[pl.BlockSpec...  57.7 us
    pallas_call x8, Pallas kernels, hist(): pl.pallas_call(functools.partial(hist_kernel, heads=heads, dt=dt), grid=(...  56.9 us
    ppermute x25, waiting for transfers between devices, move(): lax.ppermute(x, axis, [(i, i ^ bit) for i in range(lax.axis_size(axis))])  55.5 us
    pallas_call x1, Pallas kernels, bwd_attention(): pl.pallas_call(bwd_kernel, grid=(pairs, nb), in_specs=[pl.BlockSpec((IB,...  47.6 us
    dot_general x6, matrix products, nn(): lax.dot_general(a, b, (((1,), (0,)), ((), ())), preferred_element_type=F32)  35.7 us
    dot_general x6, matrix products, nt(): lax.dot_general(a, b, (((1,), (1,)), ((), ())), preferred_element_type=F32)  31.2 us
    ppermute x25, starting transfers between devices, move(): lax.ppermute(x, axis, [(i, i ^ bit) for i in range(lax.axis_size(axis))])  23.5 us
    unnamed x121, local copies, waits for them, and re-layouts  18.9 us
  transfers between devices with their start and end apart: 30, of which 12 were waited for; matrix products, arithmetic and copies ran while one was open for 25% of the time, Pallas kernels for 35%

profile of v5, /device:TPU:0, one launch (start us, length us, event | category | flops | bytes accessed | tf_op | source)
XLA Modules:
  0.0 458.4 jit_solution(9321898752962983014)
XLA Ops:
  23.6 8.4 %collective-permute-done = bf16[512,768]{0,1:T(8,128)(2,1)} collective-permute-done((bf16[512,768]{0,1:T(8,128)(2,1)}, bf16[512,768]{0,1:T(8,128)(2,1)}, u32[]{:S(2)}, u32[]{:S(2)}) %collective-permute-start) | collective-permute-done | bytes 786464 | tf_op jit(solution)/shard_map/ppermute | solution.py:336
  42.3 57.7 %attend.1 = (bf16[1024,768]{1,0:T(8,128)(2,1)S(1)}, bf16[12,4,1024,256]{3,2,1,0:T(8,128)(2,1)}, f32[6,8,1024]{2,1,0:T(8,128)S(1)}) custom-call(s32[1]{0:T(128)} %dynamic_slice.68.len_ref, bf16[1024,2304]{1,0:T(8,128)(2,1)} %add_convert_fusion.1.q_ref.k_ref.v_ref, bf16[1024,2304]{1,0:T(8,128)(2,1)} %add_convert_fusion.1.q_ref.k_ref.v_ref, ...), custom_call_target="tpu_custom_call" | custom-call | flops 1000 | bytes 1000 | tf_op jit(solution)/shard_map/attend/pallas_call | solution.py:115
  103.0 19.0 %add_convert_fusion = (bf16[1024,3072]{1,0:T(8,128)(2,1)}, bf16[1024,3072]{1,0:T(8,128)(2,1)}) fusion(f32[3072]{0:T(1024)S(1)} %convert_element_type.361, bf16[768,3072]{1,0:T(8,128)(2,1)S(1)} %bitcast.548, f32[1024,768]{0,1:T(8,128)S(1)} %get-tuple-element.369, f32[768]{0:T(1024)S(1)} %convert_element_type.359, f32[768]{0:T(1024)S(1)} %convert_element_type.358, ...), kind=kOutput, calls=%fused_computation.2 | convolution fusion | flops 4920705024 | bytes 20473856 | tf_op jit(solution)/shard_map/dot_general | solution.py:20
  122.0 7.7 %fusion.126 = (f32[1024]{0:T(1024)S(1)}, f32[1024,768]{0,1:T(8,128)S(1)}) fusion(f32[768]{0:T(1024)S(1)} %convert_element_type.364, bf16[1024,3072]{1,0:T(8,128)(2,1)} %get-tuple-element.61, bf16[3072,768]{1,0:T(8,128)(2,1)S(1)} %bitcast.546, f32[768]{0:T(1024)S(1)} %convert_element_type.359, f32[768]{0:T(1024)S(1)} %convert_element_type.358, ...), kind=kOutput, calls=%fused_computation.406 | convolution fusion | flops 4837342208 | bytes 17323008 | tf_op jit(solution)/shard_map/dot_general | solution.py:20
  137.0 6.9 %convolution_convert_fusion.1 = bf16[3072,768]{1,0:T(8,128)(2,1)} fusion(bf16[1024,3072]{1,0:T(8,128)(2,1)S(1)} %bitcast.550, bf16[1024,768]{0,1:T(8,128)(2,1)S(1)} %get-tuple-element.254), kind=kOutput, calls=%fused_computation.9 | convolution fusion | flops 4834197504 | bytes 12582912 | tf_op jit(solution)/shard_map/dot_general | solution.py:315
  143.9 8.7 %multiply_convert_fusion = bf16[1024,3072]{1,0:T(8,128)(2,1)S(1)} fusion(bf16[1024,3072]{1,0:T(8,128)(2,1)} %get-tuple-element.62, bf16[1024,768]{0,1:T(8,128)(2,1)S(1)} %get-tuple-element.254, bf16[3072,768]{1,0:T(8,128)(2,1)} %param.33), kind=kOutput, calls=%fused_computation.1 | convolution fusion | flops 4841275392 | bytes 18874368 | tf_op jit(solution)/shard_map/dot_general | solution.py:18
  152.6 9.0 %multiply_reduce_fusion = (f32[768]{0:T(1024)S(1)}, f32[1024]{0:T(1024)S(1)}, f32[768]{0:T(1024)S(1)}, f32[1024,768]{0,1:T(8,128)S(1)}) fusion(f32[1024,768]{0,1:T(8,128)S(1)} %get-tuple-element.369, f32[1024]{0:T(1024)S(1)} %fusion.83, f32[1024]{0:T(1024)S(1)} %broadcast_multiply_fusion.1, f32[768]{0:T(1024)S(1)} %convert_element_type.358, ...), kind=kOutput, calls=%fused_computation.22 | convolution fusion | flops 4847563776 | bytes 22061056 | tf_op jit(solution)/shard_map/dot_general | solution.py:18
  162.5 7.2 %convolution_convert_fusion = bf16[768,3072]{1,0:T(8,128)(2,1)} fusion(bf16[1024,3072]{1,0:T(8,128)(2,1)S(1)} %multiply_convert_fusion, f32[1024,768]{0,1:T(8,128)S(1)} %get-tuple-element.369, f32[768]{0:T(1024)S(1)} %convert_element_type.359, f32[768]{0:T(1024)S(1)} %convert_element_type.358, f32[1024]{0:T(1024)S(1)} %fusion.83, ...), kind=kOutput, calls=%fused_computation.8 | convolution fusion | flops 4838129664 | bytes 14170112 | tf_op jit(solution)/shard_map/dot_general | solution.py:315
  183.0 47.6 %attend_back.1 = (bf16[3,1024,768]{2,1,0:T(8,128)(2,1)}, bf16[12,4,1024,256]{3,2,1,0:T(8,128)(2,1)}, f32[6,8,2048]{2,1,0:T(8,128)S(1)}) custom-call(bf16[1024,2304]{1,0:T(8,128)(2,1)} %add_convert_fusion.1.q_ref.k_ref.v_ref, bf16[1024,2304]{1,0:T(8,128)(2,1)} %add_convert_fusion.1.q_ref.k_ref.v_ref, ...), custom_call_target="tpu_custom_call", output_to_operand_aliasing={{1}: (5, {})} | custom-call | flops 1000 | bytes 1000 | tf_op jit(solution)/shard_map/attend_back/pallas_call | solution.py:197
  243.9 6.0 %convert_bitcast_fusion = bf16[3,384,768]{2,1,0:T(8,128)(2,1)} fusion(bf16[3,1024,768]{2,1,0:T(8,128)(2,1)} %get-tuple-element.66, bf16[1024,768]{0,1:T(8,128)(2,1)} %copy-done.23, s32[]{:T(128)S(6)} %select_n.354), kind=kOutput, calls=%fused_computation.46 | convolution fusion | flops 1812824064 | bytes 7274500 | tf_op jit(solution)/shard_map/td,...tf->...df/dot_general | solution.py:368
  255.6 7.0 %bucket_sums.8 = f32[64,192]{1,0:T(8,128)S(1)} custom-call(bf16[12,4,1024,256]{3,2,1,0:T(8,128)(2,1)} %get-tuple-element.82.ds_ref, s32[2,1024]{1,0:T(2,128)S(1)} %pad_add_fusion.cq_ref.crow_ref, s32[2,1024,128]{2,1,0:T(8,128)S(1)} %broadcast_in_dim.16.ck_ref.ccol_ref), custom_call_target="tpu_custom_call" | custom-call | flops 15000000512 | bytes 1000 | tf_op jit(solution)/shard_map/bucket_sums/pallas_call | solution.py:247
  271.0 7.0 %bucket_sums.9 = f32[64,192]{1,0:T(8,128)S(1)} custom-call(bf16[12,4,1024,256]{3,2,1,0:T(8,128)(2,1)} %get-tuple-element.82.ds_ref, s32[2,1024]{1,0:T(2,128)S(1)} %pad_add_fusion.cq_ref.crow_ref, s32[2,1024,128]{2,1,0:T(8,128)S(1)} %broadcast_in_dim.16.ck_ref.ccol_ref), custom_call_target="tpu_custom_call" | custom-call | flops 15000000512 | bytes 1000 | tf_op jit(solution)/shard_map/bucket_sums/pallas_call | solution.py:247
  287.1 7.4 %bucket_sums.10 = f32[64,192]{1,0:T(8,128)S(1)} custom-call(bf16[12,4,1024,256]{3,2,1,0:T(8,128)(2,1)} %get-tuple-element.82.ds_ref, s32[2,1024]{1,0:T(2,128)S(1)} %pad_add_fusion.cq_ref.crow_ref, s32[2,1024,128]{2,1,0:T(8,128)S(1)} %broadcast_in_dim.16.ck_ref.ccol_ref), custom_call_target="tpu_custom_call" | custom-call | flops 15000000512 | bytes 1000 | tf_op jit(solution)/shard_map/bucket_sums/pallas_call | solution.py:247
  296.8 7.0 %bucket_sums.11 = f32[64,192]{1,0:T(8,128)S(1)} custom-call(bf16[12,4,1024,256]{3,2,1,0:T(8,128)(2,1)} %get-tuple-element.82.ds_ref, s32[2,1024]{1,0:T(2,128)S(1)} %pad_add_fusion.cq_ref.crow_ref, s32[2,1024,128]{2,1,0:T(8,128)S(1)} %broadcast_in_dim.16.ck_ref.ccol_ref), custom_call_target="tpu_custom_call" | custom-call | flops 15000000512 | bytes 1000 | tf_op jit(solution)/shard_map/bucket_sums/pallas_call | solution.py:247
  304.0 6.4 %collective-permute-done.10 = bf16[2,40,768]{2,1,0:T(8,128)(2,1)S(1)} collective-permute-done((bf16[2,40,768]{2,1,0:T(8,128)(2,1)S(1)}, bf16[2,40,768]{2,1,0:T(8,128)(2,1)S(1)}, u32[]{:S(2)}, u32[]{:S(2)}) %collective-permute-start.10) | collective-permute-done | bytes 122912 | tf_op jit(solution)/shard_map/ppermute | solution.py:363
  310.4 7.0 %bucket_sums.12 = f32[64,192]{1,0:T(8,128)S(1)} custom-call(bf16[12,4,1024,256]{3,2,1,0:T(8,128)(2,1)} %get-tuple-element.82.ds_ref, s32[2,1024]{1,0:T(2,128)S(1)} %pad_add_fusion.cq_ref.crow_ref, s32[2,1024,128]{2,1,0:T(8,128)S(1)} %broadcast_in_dim.16.ck_ref.ccol_ref), custom_call_target="tpu_custom_call" | custom-call | flops 15000000512 | bytes 1000 | tf_op jit(solution)/shard_map/bucket_sums/pallas_call | solution.py:247
  325.7 7.0 %bucket_sums.13 = f32[64,192]{1,0:T(8,128)S(1)} custom-call(bf16[12,4,1024,256]{3,2,1,0:T(8,128)(2,1)} %get-tuple-element.82.ds_ref, s32[2,1024]{1,0:T(2,128)S(1)} %pad_add_fusion.cq_ref.crow_ref, s32[2,1024,128]{2,1,0:T(8,128)S(1)} %broadcast_in_dim.16.ck_ref.ccol_ref), custom_call_target="tpu_custom_call" | custom-call | flops 15000000512 | bytes 1000 | tf_op jit(solution)/shard_map/bucket_sums/pallas_call | solution.py:247
  335.5 5.8 %collective-permute-done.15 = bf16[1,40,768]{2,1,0:T(8,128)(2,1)S(1)} collective-permute-done((bf16[1,40,768]{2,1,0:T(8,128)(2,1)S(1)}, bf16[1,40,768]{2,1,0:T(8,128)(2,1)S(1)}, u32[]{:S(2)}, u32[]{:S(2)}) %collective-permute-start.15) | collective-permute-done | bytes 61472 | tf_op jit(solution)/shard_map/ppermute | solution.py:363
  342.0 7.0 %bucket_sums.15 = f32[64,192]{1,0:T(8,128)S(1)} custom-call(bf16[12,4,1024,256]{3,2,1,0:T(8,128)(2,1)} %get-tuple-element.82.ds_ref, s32[2,1024]{1,0:T(2,128)S(1)} %pad_add_fusion.cq_ref.crow_ref, s32[2,1024,128]{2,1,0:T(8,128)S(1)} %broadcast_in_dim.16.ck_ref.ccol_ref), custom_call_target="tpu_custom_call" | custom-call | flops 15000000512 | bytes 1000 | tf_op jit(solution)/shard_map/bucket_sums/pallas_call | solution.py:247
  349.0 7.3 %bucket_sums.14 = f32[64,192]{1,0:T(8,128)S(1)} custom-call(bf16[12,4,1024,256]{3,2,1,0:T(8,128)(2,1)} %get-tuple-element.82.ds_ref, s32[2,1024]{1,0:T(2,128)S(1)} %pad_add_fusion.cq_ref.crow_ref, s32[2,1024,128]{2,1,0:T(8,128)S(1)} %broadcast_in_dim.16.ck_ref.ccol_ref), custom_call_target="tpu_custom_call" | custom-call | flops 15000000512 | bytes 1000 | tf_op jit(solution)/shard_map/bucket_sums/pallas_call | solution.py:247
  370.3 6.4 %collective-permute-done.16 = bf16[2,40,768]{2,1,0:T(8,128)(2,1)S(1)} collective-permute-done((bf16[2,40,768]{2,1,0:T(8,128)(2,1)S(1)}, bf16[2,40,768]{2,1,0:T(8,128)(2,1)S(1)}, u32[]{:S(2)}, u32[]{:S(2)}) %collective-permute-start.16) | collective-permute-done | bytes 122912 | tf_op jit(solution)/shard_map/ppermute | solution.py:363
  383.6 12.4 %collective-permute-done.17 = bf16[4,40,768]{2,1,0:T(8,128)(2,1)S(1)} collective-permute-done((bf16[4,40,768]{2,1,0:T(8,128)(2,1)S(1)}, bf16[4,40,768]{2,1,0:T(8,128)(2,1)S(1)}, u32[]{:S(2)}, u32[]{:S(2)}) %collective-permute-start.17) | collective-permute-done | bytes 245792 | tf_op jit(solution)/shard_map/ppermute | solution.py:363
  399.3 10.8 %collective-permute-done.18 = bf16[8,40,768]{2,1,0:T(8,128)(2,1)S(1)} collective-permute-done((bf16[8,40,768]{2,1,0:T(8,128)(2,1)S(1)}, bf16[8,40,768]{2,1,0:T(8,128)(2,1)S(1)}, u32[]{:S(2)}, u32[]{:S(2)}) %collective-permute-start.18) | collective-permute-done | bytes 491552 | tf_op jit(solution)/shard_map/ppermute | solution.py:363
  427.0 7.9 %convert_element_type.433 = f32[768,3072]{1,0:T(8,128)} convert(bf16[768,3072]{1,0:T(8,128)(2,1)} %get-tuple-element.90) | non-fusion elementwise | flops 2359296 | bytes 14155776 | tf_op jit(solution)/shard_map/convert_element_type | solution.py:519
  (326 shorter events, 157.8 us)
Async XLA Ops:
  7.2 409.4 %all-reduce.5.cloned.1.call-start = ((), (), s32[]{:S(2)}) async-start(), calls=%async_computation | async-start | bytes 21233664 | tf_op jit(solution)/shard_map/psum | solution.py:479
  10.4 21.6 %collective-permute-start = (bf16[512,768]{0,1:T(8,128)(2,1)}, bf16[512,768]{0,1:T(8,128)(2,1)}, u32[]{:S(2)}, u32[]{:S(2)}) collective-permute-start(bf16[512,768]{0,1:T(8,128)(2,1)} %select_bitcast_fusion.5), channel_id=1, source_target_pairs={{0,1},{1,0},{2,3},{3,2},{4,5},{5,4},{6,7},{7,6},{8,9},{9,8},{10,11... | collective-permute-start | bytes 2359304 | tf_op jit(solution)/shard_map/ppermute | solution.py:336
  18.7 111.0 %collective-permute-start.2 = (bf16[512,768]{0,1:T(8,128)(2,1)}, bf16[512,768]{0,1:T(8,128)(2,1)}, u32[]{:S(2)}, u32[]{:S(2)}) collective-permute-start(bf16[512,768]{0,1:T(8,128)(2,1)} %select_bitcast_fusion.2), channel_id=1, source_target_pairs={{0,1},{1,0},{2,3},{3,2},{4,5},{5,4},{6,7},{7,6},{8,9},{9,8},{10,11... | collective-permute-start | bytes 2359304 | tf_op jit(solution)/shard_map/ppermute | solution.py:336
  241.7 124.0 %collective-permute-start.1 = (bf16[512,768]{0,1:T(8,128)(2,1)}, bf16[512,768]{0,1:T(8,128)(2,1)}, u32[]{:S(2)}, u32[]{:S(2)}) collective-permute-start(bf16[512,768]{0,1:T(8,128)(2,1)} %broadcast_select_fusion.6), channel_id=1, source_target_pairs={{0,1},{1,0},{2,3},{3,2},{4,5},{5,4},{6,7},{7,6},{8,9},{9,8},{10,11... | collective-permute-start | bytes 2359304 | tf_op jit(solution)/shard_map/ppermute | solution.py:344
  249.9 13.4 %collective-permute-start.4 = (bf16[3,384,768]{2,1,0:T(8,128)(2,1)}, bf16[3,384,768]{2,1,0:T(8,128)(2,1)}, u32[]{:S(2)}, u32[]{:S(2)}) collective-permute-start(bf16[3,384,768]{2,1,0:T(8,128)(2,1)} %convert_bitcast_fusion), channel_id=1, source_target_pairs={{0,2},{2,0},{4,6},{6,4},{8,10},{10,8},{12,14},{14,12},{16,18},{18,... | collective-permute-start | bytes 5308424 | tf_op jit(solution)/shard_map/ppermute | solution.py:363
  254.0 8.7 %collective-permute-start.5 = (bf16[64,768]{1,0:T(8,128)(2,1)S(1)}, bf16[64,768]{1,0:T(8,128)(2,1)S(1)}, u32[]{:S(2)}, u32[]{:S(2)}) collective-permute-start(bf16[64,768]{1,0:T(8,128)(2,1)S(1)} %convolution_convert_fusion.4), channel_id=1, source_target_pairs={{0,2},{2,0},{4,6},{6,4},{8,10},{10,8},{12,14},{14,12},{16,18},{18,... | collective-permute-start | bytes 294920 | tf_op jit(solution)/shard_map/ppermute | solution.py:363
  268.8 13.2 %collective-permute-start.7 = (bf16[8,40,768]{2,1,0:T(8,128)(2,1)S(1)}, bf16[8,40,768]{2,1,0:T(8,128)(2,1)S(1)}, u32[]{:S(2)}, u32[]{:S(2)}) collective-permute-start(bf16[8,40,768]{2,1,0:T(8,128)(2,1)S(1)} %constant_dynamic-slice_fusion.10), channel_id=1, source_target_pairs={{0,1},{1,0},{2,3},{3,2},{4,5},{5,4},{6,7},{7,6},{8,9},{9,8},{10,11... | collective-permute-start | bytes 1474568 | tf_op jit(solution)/shard_map/ppermute | solution.py:363
  269.0 14.2 %collective-permute-start.6 = (bf16[8,40,768]{2,1,0:T(8,128)(2,1)S(1)}, bf16[8,40,768]{2,1,0:T(8,128)(2,1)S(1)}, u32[]{:S(2)}, u32[]{:S(2)}) collective-permute-start(bf16[8,40,768]{2,1,0:T(8,128)(2,1)S(1)} %constant_dynamic-slice_fusion.11), channel_id=1, source_target_pairs={{0,4},{2,6},{4,0},{6,2},{8,12},{10,14},{12,8},{14,10},{16,20},{18,... | collective-permute-start | bytes 1474568 | tf_op jit(solution)/shard_map/ppermute | solution.py:363
  283.3 11.2 %collective-permute-start.9 = (bf16[4,40,768]{2,1,0:T(8,128)(2,1)S(1)}, bf16[4,40,768]{2,1,0:T(8,128)(2,1)S(1)}, u32[]{:S(2)}, u32[]{:S(2)}) collective-permute-start(bf16[4,40,768]{2,1,0:T(8,128)(2,1)S(1)} %constant_dynamic-slice_fusion.8), channel_id=1, source_target_pairs={{0,4},{2,6},{4,0},{6,2},{8,12},{10,14},{12,8},{14,10},{16,20},{18,... | collective-permute-start | bytes 737288 | tf_op jit(solution)/shard_map/ppermute | solution.py:363
  285.9 8.7 %collective-permute-start.8 = (bf16[4,40,768]{2,1,0:T(8,128)(2,1)S(1)}, bf16[4,40,768]{2,1,0:T(8,128)(2,1)S(1)}, u32[]{:S(2)}, u32[]{:S(2)}) collective-permute-start(bf16[4,40,768]{2,1,0:T(8,128)(2,1)S(1)} %constant_dynamic-slice_fusion.9), channel_id=1, source_target_pairs={{0,1},{1,0},{2,3},{3,2},{4,5},{5,4},{6,7},{7,6},{8,9},{9,8},{10,11... | collective-permute-start | bytes 737288 | tf_op jit(solution)/shard_map/ppermute | solution.py:363
  294.7 9.2 %collective-permute-start.11 = (bf16[2,40,768]{2,1,0:T(8,128)(2,1)S(1)}, bf16[2,40,768]{2,1,0:T(8,128)(2,1)S(1)}, u32[]{:S(2)}, u32[]{:S(2)}) collective-permute-start(bf16[2,40,768]{2,1,0:T(8,128)(2,1)S(1)} %constant_dynamic-slice_fusion.6), channel_id=1, source_target_pairs={{0,8},{2,10},{4,12},{6,14},{8,0},{10,2},{12,4},{14,6},{16,24},{18,... | collective-permute-start | bytes 368648 | tf_op jit(solution)/shard_map/ppermute | solution.py:363
  325.4 10.1 %collective-permute-start.14 = (bf16[1,40,768]{2,1,0:T(8,128)(2,1)S(1)}, bf16[1,40,768]{2,1,0:T(8,128)(2,1)S(1)}, u32[]{:S(2)}, u32[]{:S(2)}) collective-permute-start(bf16[1,40,768]{2,1,0:T(8,128)(2,1)S(1)} %add_convert_fusion.14), channel_id=1, source_target_pairs={{0,16},{2,18},{4,20},{6,22},{8,24},{10,26},{12,28},{14,30},{16,0},... | collective-permute-start | bytes 184328 | tf_op jit(solution)/shard_map/ppermute | solution.py:363
  332.7 8.6 %collective-permute-start.15 = (bf16[1,40,768]{2,1,0:T(8,128)(2,1)S(1)}, bf16[1,40,768]{2,1,0:T(8,128)(2,1)S(1)}, u32[]{:S(2)}, u32[]{:S(2)}) collective-permute-start(bf16[1,40,768]{2,1,0:T(8,128)(2,1)S(1)} %add_convert_fusion.13), channel_id=1, source_target_pairs={{0,16},{2,18},{4,20},{6,22},{8,24},{10,26},{12,28},{14,30},{16,0},... | collective-permute-start | bytes 184328 | tf_op jit(solution)/shard_map/ppermute | solution.py:363
  363.5 34.4 %collective-permute-start.3 = (bf16[512,768]{0,1:T(8,128)(2,1)S(1)}, bf16[512,768]{0,1:T(8,128)(2,1)S(1)}, u32[]{:S(2)}, u32[]{:S(2)}) collective-permute-start(bf16[512,768]{0,1:T(8,128)(2,1)S(1)} %broadcast_select_fusion.4), channel_id=1, source_target_pairs={{0,1},{1,0},{2,3},{3,2},{4,5},{5,4},{6,7},{7,6},{8,9},{9,8},{10,11... | collective-permute-start | bytes 2359304 | tf_op jit(solution)/shard_map/ppermute | solution.py:344
  368.1 8.6 %collective-permute-start.16 = (bf16[2,40,768]{2,1,0:T(8,128)(2,1)S(1)}, bf16[2,40,768]{2,1,0:T(8,128)(2,1)S(1)}, u32[]{:S(2)}, u32[]{:S(2)}) collective-permute-start(bf16[2,40,768]{2,1,0:T(8,128)(2,1)S(1)} %copy-done.26), channel_id=1, source_target_pairs={{0,8},{2,10},{4,12},{6,14},{8,0},{10,2},{12,4},{14,6},{16,24},{18,... | collective-permute-start | bytes 368648 | tf_op jit(solution)/shard_map/ppermute | solution.py:363
  368.1 13.8 %collective-permute-start.19 = (bf16[2,40,768]{2,1,0:T(8,128)(2,1)S(1)}, bf16[2,40,768]{2,1,0:T(8,128)(2,1)S(1)}, u32[]{:S(2)}, u32[]{:S(2)}) collective-permute-start(bf16[2,40,768]{2,1,0:T(8,128)(2,1)S(1)} %get-tuple-element.78), channel_id=1, source_target_pairs={{0,8},{2,10},{4,12},{6,14},{8,0},{10,2},{12,4},{14,6},{16,24},{18,... | collective-permute-start | bytes 368648 | tf_op jit(solution)/shard_map/ppermute | solution.py:363
  370.2 29.1 %collective-permute-start.26 = (f32[88,128]{1,0:T(8,128)S(1)}, f32[88,128]{1,0:T(8,128)S(1)}, u32[]{:S(2)}, u32[]{:S(2)}) collective-permute-start(f32[88,128]{1,0:T(8,128)S(1)} %fusion.155), channel_id=1, source_target_pairs={{0,8},{2,10},{4,12},{6,14},{8,0},{10,2},{12,4},{14,6},{16,24},{18,... | collective-permute-start | bytes 135176 | tf_op jit(solution)/shard_map/ppermute | solution.py:363
  376.8 19.2 %collective-permute-start.17 = (bf16[4,40,768]{2,1,0:T(8,128)(2,1)S(1)}, bf16[4,40,768]{2,1,0:T(8,128)(2,1)S(1)}, u32[]{:S(2)}, u32[]{:S(2)}) collective-permute-start(bf16[4,40,768]{2,1,0:T(8,128)(2,1)S(1)} %pad_maximum_fusion.13), channel_id=1, source_target_pairs={{0,1},{1,0},{2,3},{3,2},{4,5},{5,4},{6,7},{7,6},{8,9},{9,8},{10,11... | collective-permute-start | bytes 737288 | tf_op jit(solution)/shard_map/ppermute | solution.py:363
  382.0 14.1 %collective-permute-start.20 = (bf16[4,40,768]{2,1,0:T(8,128)(2,1)S(1)}, bf16[4,40,768]{2,1,0:T(8,128)(2,1)S(1)}, u32[]{:S(2)}, u32[]{:S(2)}) collective-permute-start(bf16[4,40,768]{2,1,0:T(8,128)(2,1)S(1)} %pad_maximum_fusion.14), channel_id=1, source_target_pairs={{0,4},{2,6},{4,0},{6,2},{8,12},{10,14},{12,8},{14,10},{16,20},{18,... | collective-permute-start | bytes 737288 | tf_op jit(solution)/shard_map/ppermute | solution.py:363
  396.0 14.1 %collective-permute-start.18 = (bf16[8,40,768]{2,1,0:T(8,128)(2,1)S(1)}, bf16[8,40,768]{2,1,0:T(8,128)(2,1)S(1)}, u32[]{:S(2)}, u32[]{:S(2)}) collective-permute-start(bf16[8,40,768]{2,1,0:T(8,128)(2,1)S(1)} %pad_maximum_fusion.10), channel_id=1, source_target_pairs={{0,4},{2,6},{4,0},{6,2},{8,12},{10,14},{12,8},{14,10},{16,20},{18,... | collective-permute-start | bytes 1474568 | tf_op jit(solution)/shard_map/ppermute | solution.py:363
  396.2 15.0 %collective-permute-start.21 = (bf16[8,40,768]{2,1,0:T(8,128)(2,1)S(1)}, bf16[8,40,768]{2,1,0:T(8,128)(2,1)S(1)}, u32[]{:S(2)}, u32[]{:S(2)}) collective-permute-start(bf16[8,40,768]{2,1,0:T(8,128)(2,1)S(1)} %pad_maximum_fusion.11), channel_id=1, source_target_pairs={{0,1},{1,0},{2,3},{3,2},{4,5},{5,4},{6,7},{7,6},{8,9},{9,8},{10,11... | collective-permute-start | bytes 1474568 | tf_op jit(solution)/shard_map/ppermute | solution.py:363
  399.3 17.5 %collective-permute-start.27 = (f32[88,128]{1,0:T(8,128)S(1)}, f32[88,128]{1,0:T(8,128)S(1)}, u32[]{:S(2)}, u32[]{:S(2)}) collective-permute-start(f32[88,128]{1,0:T(8,128)S(1)} %add.563), channel_id=1, source_target_pairs={{0,16},{2,18},{4,20},{6,22},{8,24},{10,26},{12,28},{14,30},{16,0},... | collective-permute-start | bytes 135176 | tf_op jit(solution)/shard_map/ppermute | solution.py:363
  416.6 25.4 %collective-permute-start.22 = (bf16[16,40,768]{2,1,0:T(8,128)(2,1)}, bf16[16,40,768]{2,1,0:T(8,128)(2,1)}, u32[]{:S(2)}, u32[]{:S(2)}) collective-permute-start(bf16[16,40,768]{2,1,0:T(8,128)(2,1)} %pad_maximum_fusion.8), channel_id=1, source_target_pairs={{0,2},{2,0},{4,6},{6,4},{8,10},{10,8},{12,14},{14,12},{16,18},{18,... | collective-permute-start | bytes 2949128 | tf_op jit(solution)/shard_map/ppermute | solution.py:363
  417.9 25.3 %collective-permute-start.23 = (bf16[16,40,768]{2,1,0:T(8,128)(2,1)}, bf16[16,40,768]{2,1,0:T(8,128)(2,1)}, u32[]{:S(2)}, u32[]{:S(2)}) collective-permute-start(bf16[16,40,768]{2,1,0:T(8,128)(2,1)} %pad_maximum_fusion.9), channel_id=1, source_target_pairs={{0,2},{2,0},{4,6},{6,4},{8,10},{10,8},{12,14},{14,12},{16,18},{18,... | collective-permute-start | bytes 2949128 | tf_op jit(solution)/shard_map/ppermute | solution.py:363
  (57 other events, 546.5 us)
Sparse Core Ops, SparseCore 0:
  180.3 236.2 all-reduce.4
